TPU v7x, 512 devices: a whole 4x4x16 slice. The times are simulated.
512 devices in a mesh: expert: 16 (over y, x), seq: 32 (over z, core).
Axes of the slice: x: 4, y: 4, z: 16, core: 2. Of those that a mesh axis runs over, the one named last changes fastest.
Arguments:
- tokens: bfloat16 [4096, 4096], P('seq', 'expert'), may hold values from -6 to 6
- cotangent: bfloat16 [4096, 4096], P('seq', 'expert'), may hold values from -4 to 4
- route: int32 [4096, 2], P('seq'), may hold values from 0 to 15, all different within a row; in each aligned block of 128 rows (0 to 127, 128 to 255, ...) at most 24 rows name the same one
- route_weight: float32 [4096, 2], P('seq'), may hold values from 0.25 to 1
- mean_gate: bfloat16 [16, 4096, 768], P('expert', 'seq'), may hold values from -0.09375 to 0.09375
- spread_gate: bfloat16 [16, 4096, 768], P('expert', 'seq'), may hold values from 0.0046691895 to 0.015625
- noise_gate: bfloat16 [16, 4096, 768], P('expert', 'seq'), may hold values from -4 to 4
- mean_up: bfloat16 [16, 4096, 768], P('expert', 'seq'), may hold values from -0.09375 to 0.09375
- spread_up: bfloat16 [16, 4096, 768], P('expert', 'seq'), may hold values from 0.0046691895 to 0.015625
- noise_up: bfloat16 [16, 4096, 768], P('expert', 'seq'), may hold values from -4 to 4
- mean_down: bfloat16 [16, 768, 4096], P('expert', None, 'seq'), may hold values from -0.21875 to 0.21875
- spread_down: bfloat16 [16, 768, 4096], P('expert', None, 'seq'), may hold values from 0.010803223 to 0.035888672
- noise_down: bfloat16 [16, 768, 4096], P('expert', None, 'seq'), may hold values from -4 to 4
Outputs:
- mixed_out: bfloat16 [4096, 4096], P('seq', 'expert')
- token_grad: bfloat16 [4096, 4096], P('seq', 'expert')
- grad_mean_gate: float32 [16, 4096, 768], P('expert', 'seq')
- grad_spread_gate: float32 [16, 4096, 768], P('expert', 'seq')
- grad_mean_up: float32 [16, 4096, 768], P('expert', 'seq')
- grad_spread_up: float32 [16, 4096, 768], P('expert', 'seq')
- grad_mean_down: float32 [16, 768, 4096], P('expert', None, 'seq')
- grad_spread_down: float32 [16, 768, 4096], P('expert', None, 'seq')
Inputs may be any that keep to these rules, and one draw needn't show every extreme that they name: `route`: the 2 routes of a token name different experts. Within each aligned block of 128 rows (one index of seq), no expert is named by more than 24 routes, a bound that some block reaches.
All inputs are finite; a program needn't handle non-finite values.
Results may differ from a plain program's by a relative error of at most 0.0083.
Values may be sent and summed in bfloat16 or wider, within the bound.
No kernel may reach another device: no remote copies, remote signals or barrier semaphores. Data moves between devices by JAX's collectives and lax.ppermute only.
A program may use at most 64 MiB of HBM per device.

v0:
```python
import jax
import jax.numpy as jnp
from jax import lax
from jax.sharding import PartitionSpec as P


def sampled(mean_part, spread, noise_part):
    return (
        mean_part.astype(jnp.float32) + spread.astype(jnp.float32) * noise_part.astype(jnp.float32)
    ).astype(jnp.bfloat16)


def contract_rows(left_side, right_side):
    return lax.dot_general(
        left_side, right_side, (((0,), (0,)), ((), ())), preferred_element_type=jnp.float32
    )


def contract_cols(left_side, right_side):
    return lax.dot_general(
        left_side, right_side, (((1,), (1,)), ((), ())), preferred_element_type=jnp.float32
    )


def local_rows(summed, back_hidden, hidden_width):
    gate_val = summed[:, :hidden_width]
    up_val = summed[:, hidden_width:]
    sigmoid_gate = jax.nn.sigmoid(gate_val)
    active = gate_val * sigmoid_gate
    hidden = (active * up_val).astype(jnp.bfloat16)
    grad_gate = (
        back_hidden * up_val * sigmoid_gate * (1.0 + gate_val * (1.0 - sigmoid_gate))
    ).astype(jnp.bfloat16)
    grad_upper = (back_hidden * active).astype(jnp.bfloat16)
    return (hidden, jnp.concatenate([grad_gate, grad_upper], axis=1))


def body(
    tokens,
    cotangent,
    route,
    route_weight,
    mean_gate,
    spread_gate,
    noise_gate,
    mean_up,
    spread_up,
    noise_up,
    mean_down,
    spread_down,
    noise_down,
):
    experts = lax.axis_size("expert")
    group_rows, routes = route.shape
    feature_cols = tokens.shape[1]
    hidden_width = mean_gate.shape[2]
    capacity = group_rows * routes // experts * 3 // 2
    flat_route = route.reshape(-1)
    flat_weight = route_weight.reshape(-1)
    choose = (flat_route[:, None] == jnp.arange(experts, dtype=jnp.int32)[None, :]).astype(
        jnp.int32
    )
    earlier = jnp.cumsum(choose, axis=0) - choose
    position = jnp.sum(earlier * choose, axis=1)
    target = flat_route * capacity + position
    select = (jnp.arange(experts * capacity, dtype=jnp.int32)[:, None] == target[None, :]).astype(
        jnp.float32
    )
    picker = jnp.sum(select.reshape(experts * capacity, group_rows, routes), axis=2).astype(
        jnp.bfloat16
    )
    slot_weight = jnp.sum(select * flat_weight[None, :], axis=1)
    send_x = jnp.dot(picker, tokens, preferred_element_type=jnp.float32).astype(jnp.bfloat16)
    picked_cot = jnp.dot(picker, cotangent, preferred_element_type=jnp.float32)
    send_d = (slot_weight[:, None] * picked_cot).astype(jnp.bfloat16)
    slot_shape = (experts, capacity, feature_cols)
    slot_x, slot_d = (
        lax.all_to_all(
            lax.all_to_all(
                send_x.reshape(slot_shape), "expert", split_axis=0, concat_axis=2, tiled=True
            ),
            "seq",
            split_axis=2,
            concat_axis=1,
            tiled=True,
        ),
        lax.all_to_all(
            lax.all_to_all(
                send_d.reshape(slot_shape), "expert", split_axis=0, concat_axis=2, tiled=True
            ),
            "seq",
            split_axis=2,
            concat_axis=1,
            tiled=True,
        ),
    )
    slot_x = slot_x[0]
    slot_d = slot_d[0]
    w_gate = sampled(mean_gate[0], spread_gate[0], noise_gate[0])
    w_up = sampled(mean_up[0], spread_up[0], noise_up[0])
    w_down = sampled(mean_down[0], spread_down[0], noise_down[0])
    w_both = jnp.concatenate([w_gate, w_up], axis=1)
    summed = lax.psum_scatter(
        jnp.dot(slot_x, w_both, preferred_element_type=jnp.float32),
        "seq",
        scatter_dimension=0,
        tiled=True,
    )
    back_hidden = lax.psum_scatter(
        contract_cols(slot_d, w_down), "seq", scatter_dimension=0, tiled=True
    )
    hidden, both_grad = local_rows(summed, back_hidden, hidden_width)
    shard_rows = lax.all_gather(hidden, "seq", axis=0, tiled=True)
    outputs = jnp.dot(shard_rows, w_down, preferred_element_type=jnp.float32)
    down_total = contract_rows(shard_rows, slot_d)
    shard_rows = lax.all_gather(both_grad, "seq", axis=0, tiled=True)
    pair_total = contract_rows(slot_x, shard_rows)
    back_rows = contract_cols(shard_rows, w_both)
    out_send = outputs.astype(jnp.bfloat16)[None]
    back_send = back_rows.astype(jnp.bfloat16)[None]
    out_middle, back_middle = (
        lax.all_to_all(out_send, "seq", split_axis=1, concat_axis=2, tiled=True),
        lax.all_to_all(back_send, "seq", split_axis=1, concat_axis=2, tiled=True),
    )
    out_home, back_home = (
        lax.all_to_all(out_middle, "expert", split_axis=2, concat_axis=0, tiled=True),
        lax.all_to_all(back_middle, "expert", split_axis=2, concat_axis=0, tiled=True),
    )
    out_flat = out_home.reshape(experts * capacity, feature_cols)
    back_flat = back_home.reshape(experts * capacity, feature_cols)
    out_routes = out_flat[target].astype(jnp.float32) * flat_weight[:, None]
    mixed_out = jnp.sum(out_routes.reshape(group_rows, routes, feature_cols), axis=1).astype(
        jnp.bfloat16
    )
    back_routes = back_flat[target].astype(jnp.float32)
    token_grad = jnp.sum(back_routes.reshape(group_rows, routes, feature_cols), axis=1).astype(
        jnp.bfloat16
    )
    gate_grad = pair_total[:, :hidden_width]
    up_grad = pair_total[:, hidden_width:]
    return (
        mixed_out,
        token_grad,
        gate_grad[None],
        (gate_grad * noise_gate[0].astype(jnp.float32))[None],
        up_grad[None],
        (up_grad * noise_up[0].astype(jnp.float32))[None],
        down_total[None],
        (down_total * noise_down[0].astype(jnp.float32))[None],
    )


def solution(mesh):
    placed = (
        P("seq", "expert"),
        P("seq", "expert"),
        P("seq", None),
        P("seq", None),
        P("expert", "seq", None),
        P("expert", "seq", None),
        P("expert", "seq", None),
        P("expert", "seq", None),
        P("expert", "seq", None),
        P("expert", "seq", None),
        P("expert", None, "seq"),
        P("expert", None, "seq"),
        P("expert", None, "seq"),
    )
    return jax.shard_map(
        body,
        mesh=mesh,
        in_specs=placed,
        out_specs=(
            P("seq", "expert"),
            P("seq", "expert"),
            P("expert", "seq", None),
            P("expert", "seq", None),
            P("expert", "seq", None),
            P("expert", "seq", None),
            P("expert", None, "seq"),
            P("expert", None, "seq"),
        ),
        check_vma=False,
    )
```

profile of v0, /device:TPU:1, one launch (start us, length us, event | category | flops | bytes accessed | tf_op | source)
XLA Modules:
  0.0 550.0 jit_solution(8517370732769382123)
XLA Ops:
  11.4 14.6 %all_to_all.132 = bf16[16,24,256]{2,1,0:T(8,128)(2,1)S(1)} all-to-all(bf16[16,24,256]{2,1,0:T(8,128)(2,1)S(1)} %bitcast.201), channel_id=1, replica_groups=mesh['expert'=16,'seq'=32] {'expert'}, dimensions={0} | all-to-all | bytes 393216 | tf_op jit(solution)/shard_map/all_to_all | solution.py:88
  26.0 2.8 copy.98
  29.3 22.4 %reduce.3 = bf16[4096,24]{1,0:T(8,128)(2,1)S(1)} reduce(bf16[4096,1,24]{2,1,0:T(2,128)(2,1)S(1)} %bitcast.174, bf16[]{:T(256)} %broadcast.88), dimensions={1}, to_apply=%bitcast.145.reduce_sub_computation | reduce | bytes 393218
  53.1 35.8 %all_to_all.133 = bf16[32,2,1536]{2,1,0:T(2,128)(2,1)S(1)} all-to-all(bf16[32,2,1536]{2,1,0:T(2,128)(2,1)S(1)} %reshape.167), channel_id=1, replica_groups=mesh['expert'=16,'seq'=32] {'seq'}, dimensions={0} | all-to-all | bytes 393216 | tf_op jit(solution)/shard_map/all_to_all | solution.py:87
  88.9 3.0 reshape.168
  91.9 2.1 copy.99
  96.4 10.1 %all_to_all.134 = bf16[16,24,256]{2,1,0:T(8,128)(2,1)S(1)} all-to-all(bf16[16,24,256]{2,1,0:T(8,128)(2,1)S(1)} %bitcast.208), channel_id=1, replica_groups=mesh['expert'=16,'seq'=32] {'expert'}, dimensions={0} | all-to-all | bytes 393216 | tf_op jit(solution)/shard_map/all_to_all | solution.py:79
  106.4 2.8 copy.87
  109.2 22.4 %reduce.4 = bf16[4096,24]{1,0:T(8,128)(2,1)S(1)} reduce(bf16[4096,1,24]{2,1,0:T(2,128)(2,1)S(1)} %bitcast.177, bf16[]{:T(256)} %broadcast.88), dimensions={1}, to_apply=%bitcast.139.reduce_sub_computation | reduce | bytes 393218
  133.7 6.6 %all-to-all-start.1 = ((bf16[32,2,1536]{2,1,0:T(2,128)(2,1)}), bf16[32,2,1536]{2,1,0:T(2,128)(2,1)S(1)}, u32[]{:S(2)}, u32[]{:S(2)}) async-start(bf16[32,2,1536]{2,1,0:T(2,128)(2,1)} %reshape.161), calls=%async_computation.1 | async-start | bytes 393216 | tf_op jit(solution)/shard_map/all_to_all | solution.py:78
  141.9 16.0 %all-to-all-done.1 = bf16[32,2,1536]{2,1,0:T(2,128)(2,1)S(1)} async-done(((bf16[32,2,1536]{2,1,0:T(2,128)(2,1)}), bf16[32,2,1536]{2,1,0:T(2,128)(2,1)S(1)}, u32[]{:S(2)}, u32[]{:S(2)}) %all-to-all-start.1) | async-done | bytes 196640 | tf_op jit(solution)/shard_map/all_to_all | solution.py:78
  157.9 3.0 reshape.162
  163.1 2.9 fusion.15
  166.1 30.4 %reduce-scatter.5.cloned.1.call-done = f32[24,768]{1,0:T(8,128)} async-done(((f32[768,768]{1,0:T(8,128)}), f32[24,768]{1,0:T(8,128)}) %reduce-scatter.5.cloned.1.call-update) | async-done | bytes 73744 | tf_op jit(solution)/shard_map/reduce_scatter | solution.py:109
  196.4 116.9 %reduce-scatter.3.cloned.1.call-done = f32[24,1536]{1,0:T(8,128)} async-done(((f32[768,1536]{1,0:T(8,128)}), f32[24,1536]{1,0:T(8,128)}) %reduce-scatter.3.cloned.1.call-update) | async-done | bytes 147472 | tf_op jit(solution)/shard_map/reduce_scatter | solution.py:103
  315.7 72.6 %all-gather.3.cloned.1.call-done = bf16[768,768]{1,0:T(8,128)(2,1)} async-done(((bf16[24,768]{1,0:T(8,128)(2,1)}), bf16[768,768]{1,0:T(8,128)(2,1)}) %all-gather.3.cloned.1.call-update) | async-done | bytes 1179664 | tf_op jit(solution)/shard_map/all_gather | solution.py:113
  393.0 8.7 %all-to-all-start.2 = ((bf16[32,2,1536]{2,1,0:T(2,128)(2,1)}), bf16[32,2,1536]{2,1,0:T(2,128)(2,1)S(1)}, u32[]{:S(2)}, u32[]{:S(2)}) async-start(bf16[32,2,1536]{2,1,0:T(2,128)(2,1)} %reshape.163), calls=%async_computation.3 | async-start | bytes 393216 | tf_op jit(solution)/shard_map/all_to_all | solution.py:122
  403.1 18.4 %all-to-all-done.2 = bf16[32,2,1536]{2,1,0:T(2,128)(2,1)S(1)} async-done(((bf16[32,2,1536]{2,1,0:T(2,128)(2,1)}), bf16[32,2,1536]{2,1,0:T(2,128)(2,1)S(1)}, u32[]{:S(2)}, u32[]{:S(2)}) %all-to-all-start.2) | async-done | bytes 196640 | tf_op jit(solution)/shard_map/all_to_all | solution.py:122
  421.8 2.8 copy.92
  424.6 22.4 %reduce.6 = bf16[4096,24]{1,0:T(8,128)(2,1)S(1)} reduce(bf16[4096,1,24]{2,1,0:T(2,128)(2,1)S(1)} %bitcast.179, bf16[]{:T(256)} %broadcast.88), dimensions={1}, to_apply=%bitcast.143.reduce_sub_computation | reduce | bytes 393218
  449.0 6.6 %all-to-all-start.3 = ((bf16[16,2,3072]{2,1,0:T(2,128)(2,1)}), bf16[16,2,3072]{2,1,0:T(2,128)(2,1)S(1)}, u32[]{:S(2)}, u32[]{:S(2)}) async-start(bf16[16,2,3072]{2,1,0:T(2,128)(2,1)} %reshape.165), calls=%async_computation.4 | async-start | bytes 393216 | tf_op jit(solution)/shard_map/all_to_all | solution.py:126
  455.6 7.0 %all-gather.5.cloned.1.call-done = bf16[768,1536]{1,0:T(8,128)(2,1)} async-done(((bf16[24,1536]{1,0:T(8,128)(2,1)}), bf16[768,1536]{1,0:T(8,128)(2,1)}) %all-gather.5.cloned.1.call-update) | async-done | bytes 2359312 | tf_op jit(solution)/shard_map/all_gather | solution.py:116
  462.6 2.5 fusion.1
  468.0 8.0 %all-to-all-start.6 = ((bf16[32,2,1536]{2,1,0:T(2,128)(2,1)}), bf16[32,2,1536]{2,1,0:T(2,128)(2,1)S(1)}, u32[]{:S(2)}, u32[]{:S(2)}) async-start(bf16[32,2,1536]{2,1,0:T(2,128)(2,1)} %reshape.169), calls=%async_computation.8 | async-start | bytes 393216 | tf_op jit(solution)/shard_map/all_to_all | solution.py:123
  476.7 3.0 reshape.166
  485.7 8.7 %all-to-all-done.6 = bf16[32,2,1536]{2,1,0:T(2,128)(2,1)S(1)} async-done(((bf16[32,2,1536]{2,1,0:T(2,128)(2,1)}), bf16[32,2,1536]{2,1,0:T(2,128)(2,1)S(1)}, u32[]{:S(2)}, u32[]{:S(2)}) %all-to-all-start.6) | async-done | bytes 196640 | tf_op jit(solution)/shard_map/all_to_all | solution.py:123
  494.7 2.8 copy.103
  497.4 22.5 %reduce.8 = bf16[4096,24]{1,0:T(8,128)(2,1)S(1)} reduce(bf16[4096,1,24]{2,1,0:T(2,128)(2,1)S(1)} %bitcast.175, bf16[]{:T(256)} %broadcast.88), dimensions={1}, to_apply=%bitcast.149.reduce_sub_computation | reduce | bytes 393218
  521.9 6.5 %all-to-all-start.7 = ((bf16[16,2,3072]{2,1,0:T(2,128)(2,1)}), bf16[16,2,3072]{2,1,0:T(2,128)(2,1)S(1)}, u32[]{:S(2)}, u32[]{:S(2)}) async-start(bf16[16,2,3072]{2,1,0:T(2,128)(2,1)} %reshape.171), calls=%async_computation.9 | async-start | bytes 393216 | tf_op jit(solution)/shard_map/all_to_all | solution.py:127
  528.5 2.1 fusion.14
  530.6 5.1 all-to-all-done.7
  535.6 3.0 reshape.172
  (117 shorter events, 41.2 us)
Async XLA Ops:
  7.2 4.1 copy-start
  7.2 189.2 %reduce-scatter.5.cloned.1.call-start = ((), (), s32[]{:S(2)}) async-start(), calls=%async_computation.12 | async-start | bytes 2433024 | tf_op jit(solution)/shard_map/reduce_scatter | solution.py:109
  10.2 15.9 %copy-start.15 = (f32[128,2]{1,0:T(8,128)}, f32[128,2]{1,0:T(8,128)S(1)}, u32[]{:S(2)}) copy-start(f32[128,2]{1,0:T(8,128)S(1)} %copy.95) | copy-start | bytes 3076
  91.9 2.3 copy-start.4
  91.9 2.3 copy-start.8
  91.9 2.3 copy-start.10
  94.2 2.0 copy-start.18
  133.7 24.2 %all-to-all-start.1 = ((bf16[32,2,1536]{2,1,0:T(2,128)(2,1)}), bf16[32,2,1536]{2,1,0:T(2,128)(2,1)S(1)}, u32[]{:S(2)}, u32[]{:S(2)}) async-start(bf16[32,2,1536]{2,1,0:T(2,128)(2,1)} %reshape.161), calls=%async_computation.1 | async-start | bytes 393216 | tf_op jit(solution)/shard_map/all_to_all | solution.py:78
  140.3 173.0 %reduce-scatter.3.cloned.1.call-start = ((), (), s32[]{:S(2)}) async-start(), calls=%async_computation.10 | async-start | bytes 4866048 | tf_op jit(solution)/shard_map/reduce_scatter | solution.py:103
  141.8 21.3 %copy-start.13 = (bf16[128,768]{1,0:T(8,128)(2,1)}, bf16[128,768]{1,0:T(8,128)(2,1)S(1)}, u32[]{:S(2)}) copy-start(bf16[128,768]{1,0:T(8,128)(2,1)S(1)} %get-tuple-element.17) | copy-start | bytes 589828
  141.8 21.3 %copy-start.14 = (bf16[128,768]{1,0:T(8,128)(2,1)}, bf16[128,768]{1,0:T(8,128)(2,1)S(1)}, u32[]{:S(2)}) copy-start(bf16[128,768]{1,0:T(8,128)(2,1)S(1)} %get-tuple-element.18) | copy-start | bytes 589828
  166.0 222.3 %copy-start.5 = (bf16[1,768,128]{2,1,0:T(8,128)(2,1)S(1)}, bf16[1,768,128]{2,1,0:T(8,128)(2,1)}, u32[]{:S(2)}) copy-start(bf16[1,768,128]{2,1,0:T(8,128)(2,1)} %param.25) | copy-start | bytes 589828
  166.0 222.3 %copy-start.9 = (bf16[1,768,128]{2,1,0:T(8,128)(2,1)S(1)}, bf16[1,768,128]{2,1,0:T(8,128)(2,1)}, u32[]{:S(2)}) copy-start(bf16[1,768,128]{2,1,0:T(8,128)(2,1)} %param.24) | copy-start | bytes 589828
  166.0 222.3 %copy-start.11 = (bf16[1,768,128]{2,1,0:T(8,128)(2,1)S(1)}, bf16[1,768,128]{2,1,0:T(8,128)(2,1)}, u32[]{:S(2)}) copy-start(bf16[1,768,128]{2,1,0:T(8,128)(2,1)} %param.23) | copy-start | bytes 589828
  166.0 222.3 %all-gather.3.cloned.1.call-start = ((), (), s32[]{:S(2)}) async-start(), calls=%async_computation.11 | async-start | bytes 1216512 | tf_op jit(solution)/shard_map/all_gather | solution.py:113
  314.9 86.8 %copy-start.17 = (s32[128,2]{1,0:T(8,128)S(1)}, s32[128,2]{1,0:T(8,128)}, u32[]{:S(2)}) copy-start(s32[128,2]{1,0:T(8,128)} %get-tuple-element.15) | copy-start | bytes 3076
  315.0 147.6 %all-gather.5.cloned.1.call-start = ((), (), s32[]{:S(2)}) async-start(), calls=%async_computation.13 | async-start | bytes 2433024 | tf_op jit(solution)/shard_map/all_gather | solution.py:116
  388.3 13.6 %copy-start.1 = (bf16[768,768]{1,0:T(8,128)(2,1)S(1)}, bf16[768,768]{1,0:T(8,128)(2,1)}, u32[]{:S(2)}) copy-start(bf16[768,768]{1,0:T(8,128)(2,1)} %all-gather.3.cloned.1.call-done) | copy-start | bytes 3538948
  393.0 28.5 %all-to-all-start.2 = ((bf16[32,2,1536]{2,1,0:T(2,128)(2,1)}), bf16[32,2,1536]{2,1,0:T(2,128)(2,1)S(1)}, u32[]{:S(2)}, u32[]{:S(2)}) async-start(bf16[32,2,1536]{2,1,0:T(2,128)(2,1)} %reshape.163), calls=%async_computation.3 | async-start | bytes 393216 | tf_op jit(solution)/shard_map/all_to_all | solution.py:122
  449.0 18.9 %all-to-all-start.3 = ((bf16[16,2,3072]{2,1,0:T(2,128)(2,1)}), bf16[16,2,3072]{2,1,0:T(2,128)(2,1)S(1)}, u32[]{:S(2)}, u32[]{:S(2)}) async-start(bf16[16,2,3072]{2,1,0:T(2,128)(2,1)} %reshape.165), calls=%async_computation.4 | async-start | bytes 393216 | tf_op jit(solution)/shard_map/all_to_all | solution.py:126
  465.1 10.9 %copy-start.6 = (bf16[1,768,128]{2,1,0:T(8,128)(2,1)S(1)}, bf16[1,768,128]{2,1,0:T(8,128)(2,1)}, u32[]{:S(2)}) copy-start(bf16[1,768,128]{2,1,0:T(8,128)(2,1)} %param.25) | copy-start | bytes 589828
  465.1 10.9 %copy-start.7 = (f32[768,128]{1,0:T(8,128)S(1)}, f32[768,128]{1,0:T(8,128)}, u32[]{:S(2)}) copy-start(f32[768,128]{1,0:T(8,128)} %fusion.31) | copy-start | bytes 1179652
  468.0 26.5 %all-to-all-start.6 = ((bf16[32,2,1536]{2,1,0:T(2,128)(2,1)}), bf16[32,2,1536]{2,1,0:T(2,128)(2,1)S(1)}, u32[]{:S(2)}, u32[]{:S(2)}) async-start(bf16[32,2,1536]{2,1,0:T(2,128)(2,1)} %reshape.169), calls=%async_computation.8 | async-start | bytes 393216 | tf_op jit(solution)/shard_map/all_to_all | solution.py:123
  479.7 3.6 copy-start.16
  481.8 2.5 copy-start.3
  497.4 31.0 %copy-start.12 = (bf16[1,128,768]{2,1,0:T(8,128)(2,1)S(1)}, bf16[1,128,768]{2,1,0:T(8,128)(2,1)}, u32[]{:S(2)}) copy-start(bf16[1,128,768]{2,1,0:T(8,128)(2,1)} %param.19) | copy-start | bytes 589828
  519.9 8.6 %copy-start.2 = (f32[128,1536]{1,0:T(8,128)S(1)}, f32[128,1536]{1,0:T(8,128)}, u32[]{:S(2)}) copy-start(f32[128,1536]{1,0:T(8,128)} %fusion.30) | copy-start | bytes 2359300
  521.9 13.7 %all-to-all-start.7 = ((bf16[16,2,3072]{2,1,0:T(2,128)(2,1)}), bf16[16,2,3072]{2,1,0:T(2,128)(2,1)S(1)}, u32[]{:S(2)}, u32[]{:S(2)}) async-start(bf16[16,2,3072]{2,1,0:T(2,128)(2,1)} %reshape.171), calls=%async_computation.9 | async-start | bytes 393216 | tf_op jit(solution)/shard_map/all_to_all | solution.py:127
Sparse Core Ops, SparseCore 0:
  96.3 100.1 reduce-scatter.4
  199.3 114.0 reduce-scatter.2
  316.0 72.2 all-gather.2
  390.9 71.6 all-gather.4
where the time goes:
time: 558 us; the launch traced here: 550 us
  waiting for transfers between devices  275 us (49%)
  other arithmetic  104 us (19%)
  blocking collectives  60.4 us (11%)
  local copies, waits for them, and re-layouts  47.4 us (8%)
  starting transfers between devices  36.5 us (7%)
  between operations  14.9 us (3%)
  matrix products  12.1 us (2%)
    reduce_scatter x1, waiting for transfers between devices, body(): lax.psum_scatter(jnp.dot(slot_x, w_both, preferred_element_type=jnp.float...  117 us
    unnamed x6, other arithmetic  93.3 us
    all_gather x1, waiting for transfers between devices, body(): shard_rows = lax.all_gather(hidden, 'seq', axis=0, tiled=True)  72.6 us
    all_to_all x1, blocking collectives, body(): lax.all_to_all(lax.all_to_all(send_d.reshape(slot_shape), 'expert', split...  35.8 us
    reduce_scatter x1, waiting for transfers between devices, body(): lax.psum_scatter(contract_cols(slot_d, w_down), 'seq', scatter_dimension=...  30.4 us
    unnamed x59, local copies, waits for them, and re-layouts  23.5 us
    all_to_all x1, waiting for transfers between devices, body(): lax.all_to_all(out_send, 'seq', split_axis=1, concat_axis=2, tiled=True)  18.4 us
    all_to_all x1, waiting for transfers between devices, body(): lax.all_to_all(lax.all_to_all(send_x.reshape(slot_shape), 'expert', split...  16 us
  transfers between devices with their start and end apart: 9, of which 8 were waited for; matrix products, arithmetic and copies ran while one was open for 16% of the time, Pallas kernels for 0%

commit v1 on v0

v1 whole, which is shorter than its diff:
```python
import jax
import jax.numpy as jnp
from jax import lax
from jax.sharding import Mesh, PartitionSpec as P

BF = jnp.bfloat16
F32 = jnp.float32
PLANE = ("y", "x")
RING = ("za", "zb", "core")
QUAD = 4


def sampled(mean_part, spread, noise_part):
    return (mean_part.astype(F32) + spread.astype(F32) * noise_part.astype(F32)).astype(BF)


def contract(left_side, right_side, left_dim, right_dim):
    return lax.dot_general(
        left_side,
        right_side,
        (((left_dim,), (right_dim,)), ((), ())),
        preferred_element_type=F32,
    )


def shift(value, step):
    return lax.ppermute(value, "za", [(i, (i + step) % QUAD) for i in range(QUAD)])


def place_routes(route, experts, capacity):
    rows = route.shape[0]
    names = lax.broadcasted_iota(jnp.int32, (rows, experts), 1)
    first = (route[:, 0:1] == names).astype(BF)
    second = (route[:, 1:2] == names).astype(BF)
    below = (
        lax.broadcasted_iota(jnp.int32, (rows, rows), 0)
        > lax.broadcasted_iota(jnp.int32, (rows, rows), 1)
    ).astype(BF)
    earlier = contract(below, first + second, 1, 0)
    place_first = jnp.sum(earlier * first.astype(F32), axis=1, keepdims=True)
    place_second = jnp.sum(
        (earlier + first.astype(F32)) * second.astype(F32), axis=1, keepdims=True
    )
    slots = lax.broadcasted_iota(jnp.int32, (rows, experts * capacity), 1)
    one = (route[:, 0:1] * capacity + place_first.astype(jnp.int32) == slots).astype(BF)
    two = (route[:, 1:2] * capacity + place_second.astype(jnp.int32) == slots).astype(BF)
    return one, two


def activate(total, width):
    gate_val = total[:, :width]
    up_val = total[:, width : 2 * width]
    back_hidden = total[:, 2 * width :]
    sigmoid_gate = jax.nn.sigmoid(gate_val)
    active = gate_val * sigmoid_gate
    hidden = (active * up_val).astype(BF)
    grad_gate = (
        back_hidden * up_val * sigmoid_gate * (1.0 + gate_val * (1.0 - sigmoid_gate))
    ).astype(BF)
    grad_upper = (back_hidden * active).astype(BF)
    return jnp.concatenate([grad_gate, grad_upper, hidden], axis=1)


def body(
    tokens,
    cotangent,
    route,
    route_weight,
    mean_gate,
    spread_gate,
    noise_gate,
    mean_up,
    spread_up,
    noise_up,
    mean_down,
    spread_down,
    noise_down,
):
    experts = lax.axis_size(PLANE)
    quads = lax.axis_size("zb")
    group_rows, routes = route.shape
    feats = tokens.shape[1]
    half = feats // 2
    width = mean_gate.shape[2]
    cap = group_rows * routes // experts * 3 // 2
    me = lax.axis_index("za")
    core = lax.axis_index("core")

    w_local = jnp.concatenate(
        [
            sampled(mean_gate[0], spread_gate[0], noise_gate[0]),
            sampled(mean_up[0], spread_up[0], noise_up[0]),
            sampled(mean_down[0], spread_down[0], noise_down[0]).T,
        ],
        axis=1,
    )
    weights = lax.all_gather(w_local, "zb", axis=0, tiled=True)
    w_both = weights[:, : 2 * width]
    w_down = weights[:, 2 * width :]

    one, two = place_routes(route, experts, cap)
    cot = cotangent.astype(F32)
    scaled = jnp.concatenate(
        [
            (route_weight[:, 0:1] * cot).astype(BF),
            (route_weight[:, 1:2] * cot).astype(BF),
        ],
        axis=0,
    )
    send_x = contract(one + two, tokens, 0, 0).astype(BF)
    send_d = contract(jnp.concatenate([one, two], axis=0), scaled, 0, 0).astype(BF)
    send = jnp.concatenate([send_x, send_d], axis=1).reshape(experts, cap, 2 * feats)
    got = lax.all_to_all(send, PLANE, split_axis=0, concat_axis=0, tiled=True)
    got = got.reshape(QUAD, quads, cap, 2, 2, half).transpose(4, 0, 2, 3, 1, 5)
    got = got.reshape(2 * QUAD, cap, 2 * quads * half)
    got = lax.all_to_all(got, ("core", "za"), split_axis=0, concat_axis=0, tiled=True)
    slots = got.reshape(2 * QUAD * cap, 2 * quads * half)
    slot_x = slots[:, : quads * half]
    slot_d = slots[:, quads * half :]

    part = jnp.concatenate(
        [contract(slot_x, w_both, 1, 0), contract(slot_d, w_down, 1, 0)], axis=1
    ).reshape(2, QUAD, cap, 3 * width)
    mine = lax.dynamic_index_in_dim(part, core, 0, keepdims=False)
    other = lax.dynamic_index_in_dim(part, 1 - core, 0, keepdims=False).astype(BF)
    part = mine + lax.ppermute(other, "core", [(0, 1), (1, 0)]).astype(F32)

    def piece(step):
        return lax.dynamic_index_in_dim(part, (me + step) % QUAD, 0, keepdims=False)

    cut = 3 * width // 2
    far = piece(2).astype(BF)
    from_left = shift(far[:, :cut], 1).astype(F32)
    from_right = shift(far[:, cut:], -1).astype(F32)
    ahead = piece(1)
    ahead = jnp.concatenate([ahead[:, :cut] + from_left, ahead[:, cut:]], axis=1).astype(BF)
    behind = piece(3)
    behind = jnp.concatenate([behind[:, :cut], behind[:, cut:] + from_right], axis=1).astype(BF)
    total = piece(0) + shift(ahead, 1).astype(F32) + shift(behind, -1).astype(F32)

    rows = lax.all_gather(activate(total, width), "za", axis=0, tiled=True)
    rows = lax.all_gather(rows, "core", axis=0, tiled=True)
    grads = rows[:, : 2 * width]
    hidden = rows[:, 2 * width :]

    w_grads = jnp.concatenate(
        [contract(slot_x, grads, 0, 0).astype(BF), contract(slot_d, hidden, 0, 0).astype(BF)],
        axis=1,
    )
    w_grads = lax.psum_scatter(w_grads, "zb", scatter_dimension=0, tiled=True)

    outs = jnp.concatenate(
        [contract(hidden, w_down, 1, 1).astype(BF), contract(grads, w_both, 1, 1).astype(BF)],
        axis=1,
    ).reshape(2 * QUAD, cap, 2 * quads * half)
    home = lax.all_to_all(outs, ("core", "za"), split_axis=0, concat_axis=0, tiled=True)
    home = home.reshape(2, QUAD, cap, 2, quads, half).transpose(1, 4, 2, 3, 0, 5)
    home = home.reshape(experts, cap, 2 * feats)
    home = lax.all_to_all(home, PLANE, split_axis=0, concat_axis=0, tiled=True)
    home = home.reshape(experts * cap, 2 * feats)
    out_one = contract(one, home[:, :feats], 1, 0)
    out_two = contract(two, home[:, :feats], 1, 0)
    mixed_out = (route_weight[:, 0:1] * out_one + route_weight[:, 1:2] * out_two).astype(BF)
    token_grad = contract(one + two, home[:, feats:], 1, 0).astype(BF)

    w_grads = w_grads.astype(F32)
    gate_grad = w_grads[:, :width]
    up_grad = w_grads[:, width : 2 * width]
    down_grad = w_grads[:, 2 * width :].T
    return (
        mixed_out,
        token_grad,
        gate_grad[None],
        (gate_grad * noise_gate[0].astype(F32))[None],
        up_grad[None],
        (up_grad * noise_up[0].astype(F32))[None],
        down_grad[None],
        (down_grad * noise_down[0].astype(F32))[None],
    )


def solution(mesh):
    fine = Mesh(mesh.devices.reshape(4, 4, QUAD, 4, 2), PLANE + RING)
    by_token = P(RING, PLANE)
    by_group = P(RING, None)
    by_row = P(PLANE, RING, None)
    by_column = P(PLANE, None, RING)
    return jax.shard_map(
        body,
        mesh=fine,
        in_specs=(by_token,) * 2 + (by_group,) * 2 + (by_row,) * 6 + (by_column,) * 3,
        out_specs=(by_token,) * 2 + (by_row,) * 4 + (by_column,) * 2,
        check_vma=False,
    )
```

time: 558 us -> 246 us (0.44); the launches traced: 550 us -> 246 us
  waiting for transfers between devices: 275 us -> 76.5 us
  other arithmetic: 104 us -> 6.7 us
  local copies, waits for them, and re-layouts: 47.4 us -> 7.73 us
  blocking collectives: 60.4 us -> 90.4 us
    reduce_scatter x2 -> x1, waiting for transfers between devices: 147 us -> 12.4 us  [body(): w_grads = lax.psum_scatter(w_grads, 'zb', scatter_dimension=0, tiled=True)]
    unnamed x6 -> x0, other arithmetic: 93.3 us -> none
    all_gather x2 -> x1, waiting for transfers between devices: 79.6 us -> 22.9 us  [body(): weights = lax.all_gather(w_local, 'zb', axis=0, tiled=True)]
    all_to_all x5 -> x1, waiting for transfers between devices: 48.2 us -> 22.4 us  [body(): lax.all_to_all(got, ('core', 'za'), split_axis=0, concat_axis=0, tiled=True)]
    all_gather x0 -> x2, blocking collectives: none -> 24.9 us  [the longest x1 21.6 us: body(): rows = lax.all_gather(activate(total, width), 'za', axis=0, tiled=True)]
    ppermute x0 -> x5, starting transfers between devices: none -> 21.4 us  [the longest x4 18.6 us: shift(): lax.ppermute(value, 'za', [(i, (i + step) % QUAD) for i in range(QUAD)])]
    all_to_all x20 -> x0, local copies, waits for them, and re-layouts: 19.9 us -> none  [the longest x2 2.79 us: body(): lax.all_to_all(out_send, 'seq', split_axis=1, concat_axis=2, tiled=True)]
    ppermute x0 -> x5, waiting for transfers between devices: none -> 18.8 us  [the longest x4 17.3 us: shift(): lax.ppermute(value, 'za', [(i, (i + step) % QUAD) for i in range(QUAD)])]
  transfers between devices with their start and end apart: 9 -> 8, of which waited for: 8 -> 7; matrix products, arithmetic and copies ran while one was open for 16% -> 4% of each run, Pallas kernels for 0% -> 0%
where the time goes in v1:
time: 246 us
  blocking collectives  90.4 us (37%)
  waiting for transfers between devices  76.5 us (31%)
  starting transfers between devices  39 us (16%)
  between operations  14.6 us (6%)
  matrix products  10.6 us (4%)
  local copies, waits for them, and re-layouts  7.73 us (3%)
  other arithmetic  6.7 us (3%)
    all_to_all x1, blocking collectives, body(): lax.all_to_all(outs, ('core', 'za'), split_axis=0, concat_axis=0, tiled=T...  35.1 us
    all_gather x1, waiting for transfers between devices, body(): weights = lax.all_gather(w_local, 'zb', axis=0, tiled=True)  22.9 us
    all_to_all x1, waiting for transfers between devices, body(): lax.all_to_all(got, ('core', 'za'), split_axis=0, concat_axis=0, tiled=True)  22.4 us
    all_gather x1, blocking collectives, body(): rows = lax.all_gather(activate(total, width), 'za', axis=0, tiled=True)  21.6 us
    ppermute x4, starting transfers between devices, shift(): lax.ppermute(value, 'za', [(i, (i + step) % QUAD) for i in range(QUAD)])  18.6 us
    all_to_all x1, starting transfers between devices, body(): lax.all_to_all(got, ('core', 'za'), split_axis=0, concat_axis=0, tiled=True)  17.6 us
    ppermute x4, waiting for transfers between devices, shift(): lax.ppermute(value, 'za', [(i, (i + step) % QUAD) for i in range(QUAD)])  17.3 us
    all_to_all x1, blocking collectives, body(): got = lax.all_to_all(send, PLANE, split_axis=0, concat_axis=0, tiled=True)  15.9 us
  transfers between devices with their start and end apart: 8, of which 7 were waited for; matrix products, arithmetic and copies ran while one was open for 4% of the time, Pallas kernels for 0%

profile of v1, /device:TPU:1, one launch (start us, length us, event | category | flops | bytes accessed | tf_op | source)
XLA Modules:
  0.0 245.6 jit_solution(10932125833612311079)
XLA Ops:
  7.3 1.2 copy.36
  8.5 1.1 copy.35
  9.6 1.1 copy.37
  13.2 15.9 %all_to_all.20 = bf16[16,24,512]{2,1,0:T(8,128)(2,1)S(1)} all-to-all(bf16[16,24,512]{2,1,0:T(8,128)(2,1)S(1)} %bitcast.98), channel_id=1, replica_groups=mesh['y'=4,'x'=4,'za'=4,'zb'=4,'core'=2] {'y','x'}, dimensions={0} | all-to-all | bytes 786432 | tf_op jit(solution)/shard_map/all_to_all | solution.py:113
  29.4 1.0 reshape.83
  30.4 17.6 %all-to-all-start.1 = ((bf16[8,24,1024]{2,1,0:T(8,128)(2,1)}), bf16[8,24,1024]{2,1,0:T(8,128)(2,1)S(1)}, u32[]{:S(2)}, u32[]{:S(2)}) async-start(bf16[8,24,1024]{2,1,0:T(8,128)(2,1)} %reshape.83), calls=%async_computation.1 | async-start | bytes 786432 | tf_op jit(solution)/shard_map/all_to_all | solution.py:116
  48.0 22.4 %all-to-all-done.1 = bf16[8,24,1024]{2,1,0:T(8,128)(2,1)S(1)} async-done(((bf16[8,24,1024]{2,1,0:T(8,128)(2,1)}), bf16[8,24,1024]{2,1,0:T(8,128)(2,1)S(1)}, u32[]{:S(2)}, u32[]{:S(2)}) %all-to-all-start.1) | async-done | bytes 393248 | tf_op jit(solution)/shard_map/all_to_all | solution.py:116
  70.5 22.9 %all-gather.2.cloned.1.call-done = bf16[512,2304]{1,0:T(8,128)(2,1)} async-done(((bf16[128,2304]{1,0:T(8,128)(2,1)}), bf16[512,2304]{1,0:T(8,128)(2,1)}) %all-gather.2.cloned.1.call-update) | async-done | bytes 2359312 | tf_op jit(solution)/shard_map/all_gather | solution.py:97
  93.3 1.5 fusion.10
  94.8 1.9 fusion.2
  96.9 2.8 %collective-permute-start = (bf16[4,24,2304]{2,1,0:T(8,128)(2,1)S(1)}, bf16[4,24,2304]{2,1,0:T(8,128)(2,1)}, u32[]{:S(2)}, u32[]{:S(2)}) collective-permute-start(bf16[4,24,2304]{2,1,0:T(8,128)(2,1)S(1)} %fusion.14), channel_id=1, source_target_pairs={{0,1},{1,0},{2,3},{3,2},{4,5},{5,4},{6,7},{7,6},{8,9},{9,8},{10,11... | collective-permute-start | bytes 1327112 | tf_op jit(solution)/shard_map/ppermute | solution.py:126
  99.7 1.5 collective-permute-done
  101.2 1.1 bitcast_add_fusion
  102.4 6.5 %collective-permute-start.3 = (bf16[24,1152]{1,0:T(8,128)(2,1)S(1)}, bf16[24,1152]{1,0:T(8,128)(2,1)S(1)}, u32[]{:S(2)}, u32[]{:S(2)}) collective-permute-start(bf16[24,1152]{1,0:T(8,128)(2,1)S(1)} %get-tuple-element.45), channel_id=1, source_target_pairs={{0,24},{8,0},{16,8},{24,16},{1,25},{9,1},{17,9},{25,17},{2,26},{10... | collective-permute-start | bytes 165896 | tf_op jit(solution)/shard_map/ppermute | solution.py:27
  108.9 2.9 %collective-permute-start.1 = (bf16[24,1152]{1,0:T(8,128)(2,1)S(1)}, bf16[24,1152]{1,0:T(8,128)(2,1)S(1)}, u32[]{:S(2)}, u32[]{:S(2)}) collective-permute-start(bf16[24,1152]{1,0:T(8,128)(2,1)S(1)} %get-tuple-element.44), channel_id=1, source_target_pairs={{0,8},{8,16},{16,24},{24,0},{1,9},{9,17},{17,25},{25,1},{2,10},{10... | collective-permute-start | bytes 165896 | tf_op jit(solution)/shard_map/ppermute | solution.py:27
  111.8 3.6 %collective-permute-done.3 = bf16[24,1152]{1,0:T(8,128)(2,1)S(1)} collective-permute-done((bf16[24,1152]{1,0:T(8,128)(2,1)S(1)}, bf16[24,1152]{1,0:T(8,128)(2,1)S(1)}, u32[]{:S(2)}, u32[]{:S(2)}) %collective-permute-start.3) | collective-permute-done | bytes 55328 | tf_op jit(solution)/shard_map/ppermute | solution.py:27
  115.4 5.8 %collective-permute-start.4 = (bf16[24,2304]{1,0:T(8,128)(2,1)S(1)}, bf16[24,2304]{1,0:T(8,128)(2,1)S(1)}, u32[]{:S(2)}, u32[]{:S(2)}) collective-permute-start(bf16[24,2304]{1,0:T(8,128)(2,1)S(1)} %pad_maximum_fusion.6), channel_id=1, source_target_pairs={{0,24},{8,0},{16,8},{24,16},{1,25},{9,1},{17,9},{25,17},{2,26},{10... | collective-permute-start | bytes 331784 | tf_op jit(solution)/shard_map/ppermute | solution.py:27
  121.2 3.4 %collective-permute-start.2 = (bf16[24,2304]{1,0:T(8,128)(2,1)S(1)}, bf16[24,2304]{1,0:T(8,128)(2,1)S(1)}, u32[]{:S(2)}, u32[]{:S(2)}) collective-permute-start(bf16[24,2304]{1,0:T(8,128)(2,1)S(1)} %pad_maximum_fusion.5), channel_id=1, source_target_pairs={{0,8},{8,16},{16,24},{24,0},{1,9},{9,17},{17,25},{25,1},{2,10},{10... | collective-permute-start | bytes 331784 | tf_op jit(solution)/shard_map/ppermute | solution.py:27
  124.7 6.5 %collective-permute-done.4 = bf16[24,2304]{1,0:T(8,128)(2,1)S(1)} collective-permute-done((bf16[24,2304]{1,0:T(8,128)(2,1)S(1)}, bf16[24,2304]{1,0:T(8,128)(2,1)S(1)}, u32[]{:S(2)}, u32[]{:S(2)}) %collective-permute-start.4) | collective-permute-done | bytes 110624 | tf_op jit(solution)/shard_map/ppermute | solution.py:27
  131.2 7.3 %collective-permute-done.2 = bf16[24,2304]{1,0:T(8,128)(2,1)S(1)} collective-permute-done((bf16[24,2304]{1,0:T(8,128)(2,1)S(1)}, bf16[24,2304]{1,0:T(8,128)(2,1)S(1)}, u32[]{:S(2)}, u32[]{:S(2)}) %collective-permute-start.2) | collective-permute-done | bytes 110624 | tf_op jit(solution)/shard_map/ppermute | solution.py:27
  138.6 21.6 %all_gather.10 = bf16[96,2304]{1,0:T(8,128)(2,1)S(1)} all-gather(bf16[24,2304]{1,0:T(8,128)(2,1)S(1)} %pad_maximum_fusion.7), channel_id=1, replica_groups=mesh['y'=4,'x'=4,'za'=4,'zb'=4,'core'=2] {'za'}, dimensions={0}, use_global_device_ids=true | all-gather | bytes 552960 | tf_op jit(solution)/shard_map/all_gather | solution.py:141
  160.2 3.3 %all_gather.11 = bf16[192,2304]{1,0:T(8,128)(2,1)S(1)} all-gather(bf16[96,2304]{1,0:T(8,128)(2,1)S(1)} %all_gather.10), channel_id=1, replica_groups=mesh['y'=4,'x'=4,'za'=4,'zb'=4,'core'=2] {'core'}, dimensions={0}, use_global_device_ids=true | all-gather | bytes 1327104 | tf_op jit(solution)/shard_map/all_gather | solution.py:142
  164.5 1.6 pad_maximum_fusion
  166.1 1.5 convolution_convert_fusion.4
  167.7 2.1 fusion.4
  169.8 35.1 %all_to_all.21 = bf16[8,24,1024]{2,1,0:T(8,128)(2,1)S(1)} all-to-all(bf16[8,24,1024]{2,1,0:T(8,128)(2,1)S(1)} %bitcast.97), channel_id=1, replica_groups=mesh['y'=4,'x'=4,'za'=4,'zb'=4,'core'=2] {'core','za'}, dimensions={0} | all-to-all | bytes 786432 | tf_op jit(solution)/shard_map/all_to_all | solution.py:156
  205.8 14.5 %all_to_all.22 = bf16[16,24,512]{2,1,0:T(8,128)(2,1)S(1)} all-to-all(bf16[16,24,512]{2,1,0:T(8,128)(2,1)S(1)} %reshape.88), channel_id=1, replica_groups=mesh['y'=4,'x'=4,'za'=4,'zb'=4,'core'=2] {'y','x'}, dimensions={0} | all-to-all | bytes 786432 | tf_op jit(solution)/shard_map/all_to_all | solution.py:159
  222.2 12.4 %reduce-scatter.2.cloned.1.call-done = bf16[128,2304]{1,0:T(8,128)(2,1)} async-done(((bf16[512,2304]{1,0:T(8,128)(2,1)}), bf16[128,2304]{1,0:T(8,128)(2,1)}) %reduce-scatter.2.cloned.1.call-update) | async-done | bytes 589840 | tf_op jit(solution)/shard_map/reduce_scatter | solution.py:150
  234.6 1.1 convert_element_type.242
  235.7 1.2 slice_bitcast_fusion
  237.0 0.9 copy.39
  237.9 0.9 copy.40
  (66 shorter events, 7.0 us)
Async XLA Ops:
  7.2 5.4 %copy-start = (bf16[128,256]{1,0:T(8,128)(2,1)S(1)}, bf16[128,256]{1,0:T(8,128)(2,1)}, u32[]{:S(2)}) copy-start(bf16[128,256]{1,0:T(8,128)(2,1)} %param.13) | copy-start | bytes 196612
  7.2 3.6 %copy-start.4 = (bf16[1,128,768]{2,1,0:T(8,128)(2,1)S(1)}, bf16[1,128,768]{2,1,0:T(8,128)(2,1)}, u32[]{:S(2)}) copy-start(bf16[1,128,768]{2,1,0:T(8,128)(2,1)} %param.18) | copy-start | bytes 589828
  7.2 3.6 %copy-start.5 = (bf16[1,128,768]{2,1,0:T(8,128)(2,1)S(1)}, bf16[1,128,768]{2,1,0:T(8,128)(2,1)}, u32[]{:S(2)}) copy-start(bf16[1,128,768]{2,1,0:T(8,128)(2,1)} %param.17) | copy-start | bytes 589828
  7.2 3.6 %copy-start.1 = (bf16[1,128,768]{2,1,0:T(8,128)(2,1)S(1)}, bf16[1,128,768]{2,1,0:T(8,128)(2,1)}, u32[]{:S(2)}) copy-start(bf16[1,128,768]{2,1,0:T(8,128)(2,1)} %param.19) | copy-start | bytes 589828
  7.2 3.6 %copy-start.2 = (bf16[1,128,768]{2,1,0:T(8,128)(2,1)S(1)}, bf16[1,128,768]{2,1,0:T(8,128)(2,1)}, u32[]{:S(2)}) copy-start(bf16[1,128,768]{2,1,0:T(8,128)(2,1)} %param.22) | copy-start | bytes 589828
  7.2 3.6 %copy-start.6 = (bf16[1,128,768]{2,1,0:T(8,128)(2,1)S(1)}, bf16[1,128,768]{2,1,0:T(8,128)(2,1)}, u32[]{:S(2)}) copy-start(bf16[1,128,768]{2,1,0:T(8,128)(2,1)} %param.21) | copy-start | bytes 589828
  7.2 3.6 %copy-start.7 = (bf16[1,128,768]{2,1,0:T(8,128)(2,1)S(1)}, bf16[1,128,768]{2,1,0:T(8,128)(2,1)}, u32[]{:S(2)}) copy-start(bf16[1,128,768]{2,1,0:T(8,128)(2,1)} %param.20) | copy-start | bytes 589828
  7.2 86.1 %all-gather.2.cloned.1.call-start = ((), (), s32[]{:S(2)}) async-start(), calls=%async_computation.5 | async-start | bytes 2949120 | tf_op jit(solution)/shard_map/all_gather | solution.py:97
  10.8 1.1 copy-start.9
  10.8 1.2 copy-start.10
  10.8 1.4 copy-start.8
  30.4 40.1 %all-to-all-start.1 = ((bf16[8,24,1024]{2,1,0:T(8,128)(2,1)}), bf16[8,24,1024]{2,1,0:T(8,128)(2,1)S(1)}, u32[]{:S(2)}, u32[]{:S(2)}) async-start(bf16[8,24,1024]{2,1,0:T(8,128)(2,1)} %reshape.83), calls=%async_computation.1 | async-start | bytes 786432 | tf_op jit(solution)/shard_map/all_to_all | solution.py:116
  48.0 186.5 %reduce-scatter.2.cloned.1.call-start = ((), (), s32[]{:S(2)}) async-start(), calls=%async_computation.6 | async-start | bytes 2949120 | tf_op jit(solution)/shard_map/reduce_scatter | solution.py:150
  96.9 4.3 %collective-permute-start = (bf16[4,24,2304]{2,1,0:T(8,128)(2,1)S(1)}, bf16[4,24,2304]{2,1,0:T(8,128)(2,1)}, u32[]{:S(2)}, u32[]{:S(2)}) collective-permute-start(bf16[4,24,2304]{2,1,0:T(8,128)(2,1)S(1)} %fusion.14), channel_id=1, source_target_pairs={{0,1},{1,0},{2,3},{3,2},{4,5},{5,4},{6,7},{7,6},{8,9},{9,8},{10,11... | collective-permute-start | bytes 1327112 | tf_op jit(solution)/shard_map/ppermute | solution.py:126
  102.4 13.0 %collective-permute-start.3 = (bf16[24,1152]{1,0:T(8,128)(2,1)S(1)}, bf16[24,1152]{1,0:T(8,128)(2,1)S(1)}, u32[]{:S(2)}, u32[]{:S(2)}) collective-permute-start(bf16[24,1152]{1,0:T(8,128)(2,1)S(1)} %get-tuple-element.45), channel_id=1, source_target_pairs={{0,24},{8,0},{16,8},{24,16},{1,25},{9,1},{17,9},{25,17},{2,26},{10... | collective-permute-start | bytes 165896 | tf_op jit(solution)/shard_map/ppermute | solution.py:27
  108.9 12.3 %collective-permute-start.1 = (bf16[24,1152]{1,0:T(8,128)(2,1)S(1)}, bf16[24,1152]{1,0:T(8,128)(2,1)S(1)}, u32[]{:S(2)}, u32[]{:S(2)}) collective-permute-start(bf16[24,1152]{1,0:T(8,128)(2,1)S(1)} %get-tuple-element.44), channel_id=1, source_target_pairs={{0,8},{8,16},{16,24},{24,0},{1,9},{9,17},{17,25},{25,1},{2,10},{10... | collective-permute-start | bytes 165896 | tf_op jit(solution)/shard_map/ppermute | solution.py:27
  115.4 15.8 %collective-permute-start.4 = (bf16[24,2304]{1,0:T(8,128)(2,1)S(1)}, bf16[24,2304]{1,0:T(8,128)(2,1)S(1)}, u32[]{:S(2)}, u32[]{:S(2)}) collective-permute-start(bf16[24,2304]{1,0:T(8,128)(2,1)S(1)} %pad_maximum_fusion.6), channel_id=1, source_target_pairs={{0,24},{8,0},{16,8},{24,16},{1,25},{9,1},{17,9},{25,17},{2,26},{10... | collective-permute-start | bytes 331784 | tf_op jit(solution)/shard_map/ppermute | solution.py:27
  121.2 17.2 %collective-permute-start.2 = (bf16[24,2304]{1,0:T(8,128)(2,1)S(1)}, bf16[24,2304]{1,0:T(8,128)(2,1)S(1)}, u32[]{:S(2)}, u32[]{:S(2)}) collective-permute-start(bf16[24,2304]{1,0:T(8,128)(2,1)S(1)} %pad_maximum_fusion.5), channel_id=1, source_target_pairs={{0,8},{8,16},{16,24},{24,0},{1,9},{9,17},{17,25},{25,1},{2,10},{10... | collective-permute-start | bytes 331784 | tf_op jit(solution)/shard_map/ppermute | solution.py:27
  205.8 29.9 %copy-start.3 = (bf16[1,128,768]{2,1,0:T(8,128)(2,1)S(1)}, bf16[1,128,768]{2,1,0:T(8,128)(2,1)}, u32[]{:S(2)}) copy-start(bf16[1,128,768]{2,1,0:T(8,128)(2,1)} %param.22) | copy-start | bytes 589828
Sparse Core Ops, SparseCore 0:
  12.0 81.2 all-gather.1
  166.2 68.2 reduce-scatter.1

commit v2 on v1

v2 whole, which is shorter than its diff:
```python
import jax
import jax.numpy as jnp
from jax import lax
from jax.experimental import pallas as pl
from jax.experimental.pallas import tpu as pltpu
from jax.sharding import Mesh, PartitionSpec as P

BF = jnp.bfloat16
F32 = jnp.float32
PLANE = ("y", "x")
RING = ("za", "zb", "core")
QUAD = 4
WINDOW = ((0, 1, -1, 2), (0, 1, -1, -2))


def sampled(mean_part, spread, noise_part):
    return (mean_part.astype(F32) + spread.astype(F32) * noise_part.astype(F32)).astype(BF)


def contract(left_side, right_side, left_dim, right_dim):
    return lax.dot_general(
        left_side,
        right_side,
        (((left_dim,), (right_dim,)), ((), ())),
        preferred_element_type=F32,
    )


def shift(value, step):
    return lax.ppermute(value, "za", [(i, (i + step) % QUAD) for i in range(QUAD)])


def along_ring(value, steps):
    chips = lax.axis_size("za") * lax.axis_size("zb")
    pairs = [
        (2 * z + core, 2 * ((z + steps[core]) % chips) + core)
        for z in range(chips)
        for core in range(2)
    ]
    return lax.ppermute(value, RING, pairs)


def kernel_call(kernel, outs, *operands, free=0, scalars=0):
    whole = pl.BlockSpec(memory_space=pltpu.VMEM)
    count = len(operands) - free - scalars
    moved = sum(a.size * a.dtype.itemsize for a in operands) + sum(
        o.size * o.dtype.itemsize for o in outs
    )
    return pl.pallas_call(
        kernel,
        out_shape=tuple(outs),
        in_specs=[pl.BlockSpec(memory_space=pltpu.SMEM)] * scalars
        + [whole] * count
        + [pl.BlockSpec(memory_space=pl.ANY)] * free,
        out_specs=(whole,) * len(outs),
        compiler_params=pltpu.CompilerParams(vmem_limit_bytes=8 * 1024 * 1024),
        cost_estimate=pl.CostEstimate(flops=0, bytes_accessed=moved, transcendentals=0),
    )(*operands)


def sample_kernel(mg, sg, ng, mu, su, nu, md, sd, nd, out):
    width = mg.shape[2]
    out[:, :width] = sampled(mg[0], sg[0], ng[0])
    out[:, width : 2 * width] = sampled(mu[0], su[0], nu[0])
    down = md[0].astype(F32) + sd[0].astype(F32) * nd[0].astype(F32)
    out[:, 2 * width :] = down.T.astype(BF)


def spread_kernel(where, got, *rest):
    out = rest[-1]
    chips, half = got.shape[0], got.shape[2] // 4
    for core in range(2):
        for za in range(QUAD):
            for at, step in enumerate(WINDOW[core]):
                chip = lax.rem(where[0] + (4 * za + step + chips), chips)
                for kind in range(2):
                    lane = (4 * kind + at) * half
                    here = (2 * kind + core) * half
                    out[core * QUAD + za, :, lane : lane + half] = got[
                        chip, :, here : here + half
                    ]


def collect_kernel(where, got, out):
    chips, half = out.shape[0], out.shape[2] // 4
    for core in range(2):
        for za in range(QUAD):
            for at, step in enumerate(WINDOW[core]):
                chip = lax.rem(where[0] + (4 * za + step + chips), chips)
                for kind in range(2):
                    lane = (4 * kind + at) * half
                    here = (2 * kind + core) * half
                    out[chip, :, here : here + half] = got[
                        core * QUAD + za, :, lane : lane + half
                    ]


def forward_kernel(where, slots, w0, w1, w2, w3, mine, other):
    quads, cap, width = mine.shape[0], mine.shape[1], w0.shape[1] // 3
    rows, half = quads * cap, w0.shape[0]
    core = where[0]
    for side, out in ((core, mine), (1 - core, other)):
        start = pl.multiple_of(side * rows, rows)
        for part in range(3):
            kind = part // 2
            total = None
            for at, w in enumerate((w0, w1, w2, w3)):
                lane = (4 * kind + at) * half
                term = contract(
                    slots[pl.ds(start, rows), lane : lane + half],
                    w[:, part * width : (part + 1) * width],
                    1,
                    0,
                )
                total = term if total is None else total + term
            for quad in range(quads):
                out[quad, :, part * width : (part + 1) * width] = total[
                    quad * cap : (quad + 1) * cap
                ].astype(out.dtype)


def split_kernel(where, mine, other, far_right, far_left, own, ahead, behind):
    me, cut = where[0], far_right.shape[1]

    def piece(step, lanes):
        at = jnp.bitwise_and(me + step, QUAD - 1)
        return mine[at, :, lanes] + other[at, :, lanes].astype(F32)

    whole = slice(0, 2 * cut)
    far_right[...] = piece(2, slice(0, cut)).astype(BF)
    far_left[...] = piece(2, slice(cut, 2 * cut)).astype(BF)
    own[...] = piece(0, whole)
    ahead[...] = piece(1, whole)
    behind[...] = piece(3, whole)


def relay_kernel(ahead, behind, from_left, from_right, to_right, to_left):
    cut = from_left.shape[1]
    to_right[:, :cut] = (ahead[:, :cut] + from_left[...].astype(F32)).astype(BF)
    to_right[:, cut:] = ahead[:, cut:].astype(BF)
    to_left[:, :cut] = behind[:, :cut].astype(BF)
    to_left[:, cut:] = (behind[:, cut:] + from_right[...].astype(F32)).astype(BF)


def activate_kernel(own, from_left, from_right, out):
    width = own.shape[1] // 3

    def total(start):
        lanes = slice(start, start + width)
        return own[:, lanes] + from_left[:, lanes].astype(F32) + from_right[:, lanes].astype(F32)

    gate_val, up_val, back_hidden = total(0), total(width), total(2 * width)
    sigmoid_gate = jax.nn.sigmoid(gate_val)
    active = gate_val * sigmoid_gate
    out[:, :width] = (
        back_hidden * up_val * sigmoid_gate * (1.0 + gate_val * (1.0 - sigmoid_gate))
    ).astype(BF)
    out[:, width : 2 * width] = (back_hidden * active).astype(BF)
    out[:, 2 * width :] = (active * up_val).astype(BF)


def outs_kernel(rows, w0, w1, w2, w3, out):
    width, half = w0.shape[1] // 3, w0.shape[0]
    for at, w in enumerate((w0, w1, w2, w3)):
        value = contract(rows[:, 2 * width :], w[:, 2 * width :], 1, 1)
        out[:, at * half : (at + 1) * half] = value.astype(BF)
        value = contract(rows[:, : 2 * width], w[:, : 2 * width], 1, 1)
        out[:, (4 + at) * half : (5 + at) * half] = value.astype(BF)


def grads_kernel(slots, rows, after, g0, g1, g2, g3):
    del after
    width, half = g0.shape[1] // 3, g0.shape[0]
    for at, g in enumerate((g0, g1, g2, g3)):
        left = slots[:, at * half : (at + 1) * half]
        value = contract(left, rows[:, : 2 * width], 0, 0)
        g[:, : 2 * width] = value.astype(g.dtype)
        left = slots[:, (4 + at) * half : (5 + at) * half]
        value = contract(left, rows[:, 2 * width :], 0, 0)
        g[:, 2 * width :] = value.astype(g.dtype)


def finish_kernel(g0, g1, g2, g3, ng, nu, nd, mg, sg, mu, su, md, sd):
    width = ng.shape[2]

    def total(start):
        lanes = slice(start, start + width)
        return (g0[:, lanes] + g1[:, lanes].astype(F32)) + (
            g2[:, lanes].astype(F32) + g3[:, lanes].astype(F32)
        )

    gate = total(0)
    mg[0] = gate
    sg[0] = gate * ng[0].astype(F32)
    up = total(width)
    mu[0] = up
    su[0] = up * nu[0].astype(F32)
    down = total(2 * width).T
    md[0] = down
    sd[0] = down * nd[0].astype(F32)


def place_routes(route, experts, capacity):
    rows = route.shape[0]
    names = lax.broadcasted_iota(jnp.int32, (rows, experts), 1)
    first = (route[:, 0:1] == names).astype(BF)
    second = (route[:, 1:2] == names).astype(BF)
    below = (
        lax.broadcasted_iota(jnp.int32, (rows, rows), 0)
        > lax.broadcasted_iota(jnp.int32, (rows, rows), 1)
    ).astype(BF)
    earlier = contract(below, first + second, 1, 0)
    place_first = jnp.sum(earlier * first.astype(F32), axis=1, keepdims=True)
    place_second = jnp.sum(
        (earlier + first.astype(F32)) * second.astype(F32), axis=1, keepdims=True
    )
    slots = lax.broadcasted_iota(jnp.int32, (rows, experts * capacity), 1)
    one = (route[:, 0:1] * capacity + place_first.astype(jnp.int32) == slots).astype(BF)
    two = (route[:, 1:2] * capacity + place_second.astype(jnp.int32) == slots).astype(BF)
    return one, two


def body(
    tokens,
    cotangent,
    route,
    route_weight,
    mean_gate,
    spread_gate,
    noise_gate,
    mean_up,
    spread_up,
    noise_up,
    mean_down,
    spread_down,
    noise_down,
):
    experts = lax.axis_size(PLANE)
    group_rows, routes = route.shape
    feats = tokens.shape[1]
    half = feats // 2
    width = mean_gate.shape[2]
    cap = group_rows * routes // experts * 3 // 2
    rows_all = 2 * QUAD * cap
    me = lax.axis_index("za").astype(jnp.int32).reshape(1)
    zb = lax.axis_index("zb").astype(jnp.int32).reshape(1)
    core = lax.axis_index("core").astype(jnp.int32).reshape(1)

    (w_own,) = kernel_call(
        sample_kernel,
        [jax.ShapeDtypeStruct((half, 3 * width), BF)],
        mean_gate,
        spread_gate,
        noise_gate,
        mean_up,
        spread_up,
        noise_up,
        mean_down,
        spread_down,
        noise_down,
    )
    weights = (
        w_own,
        along_ring(w_own, (-1, -1)),
        along_ring(w_own, (1, 1)),
        along_ring(w_own, (-2, 2)),
    )

    one, two = place_routes(route, experts, cap)
    cot = cotangent.astype(F32)
    scaled = jnp.concatenate(
        [
            (route_weight[:, 0:1] * cot).astype(BF),
            (route_weight[:, 1:2] * cot).astype(BF),
        ],
        axis=0,
    )
    send_x = contract(one + two, tokens, 0, 0).astype(BF)
    send_d = contract(jnp.concatenate([one, two], axis=0), scaled, 0, 0).astype(BF)
    send = jnp.concatenate([send_x, send_d], axis=1).reshape(experts, cap, 2 * feats)
    got = lax.all_to_all(send, PLANE, split_axis=0, concat_axis=0, tiled=True)
    (got,) = kernel_call(
        spread_kernel,
        [jax.ShapeDtypeStruct((2 * QUAD, cap, 8 * half), BF)],
        zb,
        got,
        *weights[1:],
        scalars=1,
        free=3,
    )
    got = lax.all_to_all(got, ("core", "za"), split_axis=0, concat_axis=0, tiled=True)
    slots = got.reshape(rows_all, 8 * half)

    mine, other = kernel_call(
        forward_kernel,
        [
            jax.ShapeDtypeStruct((QUAD, cap, 3 * width), F32),
            jax.ShapeDtypeStruct((QUAD, cap, 3 * width), BF),
        ],
        core,
        slots,
        *weights,
        scalars=1,
    )
    other = lax.ppermute(other, "core", [(0, 1), (1, 0)])
    cut = 3 * width // 2
    total = jax.ShapeDtypeStruct((cap, 3 * width), F32)
    wire = jax.ShapeDtypeStruct((cap, 3 * width), BF)
    half_wire = jax.ShapeDtypeStruct((cap, cut), BF)
    far_right, far_left, own, ahead, behind = kernel_call(
        split_kernel, [half_wire] * 2 + [total] * 3, me, mine, other, scalars=1
    )
    to_right, to_left = kernel_call(
        relay_kernel, [wire] * 2, ahead, behind, shift(far_right, 1), shift(far_left, -1)
    )
    (rows,) = kernel_call(
        activate_kernel, [wire], own, shift(to_right, 1), shift(to_left, -1)
    )

    rows = lax.all_gather(rows, "za", axis=0, tiled=True)
    rows = lax.all_gather(rows, "core", axis=0, tiled=True)
    (outs,) = kernel_call(
        outs_kernel, [jax.ShapeDtypeStruct((rows_all, 8 * half), BF)], rows, *weights
    )
    outs = outs.reshape(2 * QUAD, cap, 8 * half)
    home = lax.all_to_all(outs, ("core", "za"), split_axis=0, concat_axis=0, tiled=True)

    w_grads = kernel_call(
        grads_kernel,
        [jax.ShapeDtypeStruct((half, 3 * width), F32)]
        + [jax.ShapeDtypeStruct((half, 3 * width), BF)] * 3,
        slots,
        rows,
        home,
        free=1,
    )
    w_grads = (
        w_grads[0],
        along_ring(w_grads[1], (1, 1)),
        along_ring(w_grads[2], (-1, -1)),
        along_ring(w_grads[3], (2, -2)),
    )

    (home,) = kernel_call(
        collect_kernel,
        [jax.ShapeDtypeStruct((experts, cap, 2 * feats), BF)],
        zb,
        home,
        scalars=1,
    )
    home = lax.all_to_all(home, PLANE, split_axis=0, concat_axis=0, tiled=True)
    home = home.reshape(experts * cap, 2 * feats)
    out_one = contract(one, home[:, :feats], 1, 0)
    out_two = contract(two, home[:, :feats], 1, 0)
    mixed_out = (route_weight[:, 0:1] * out_one + route_weight[:, 1:2] * out_two).astype(BF)
    token_grad = contract(one + two, home[:, feats:], 1, 0).astype(BF)

    by_row = jax.ShapeDtypeStruct((1, half, width), F32)
    by_column = jax.ShapeDtypeStruct((1, width, half), F32)
    ends = kernel_call(
        finish_kernel,
        [by_row] * 4 + [by_column] * 2,
        *w_grads,
        noise_gate,
        noise_up,
        noise_down,
    )
    return (mixed_out, token_grad) + tuple(ends)


def solution(mesh):
    fine = Mesh(mesh.devices.reshape(4, 4, QUAD, 4, 2), PLANE + RING)
    by_token = P(RING, PLANE)
    by_group = P(RING, None)
    by_row = P(PLANE, RING, None)
    by_column = P(PLANE, None, RING)
    return jax.shard_map(
        body,
        mesh=fine,
        in_specs=(by_token,) * 2 + (by_group,) * 2 + (by_row,) * 6 + (by_column,) * 3,
        out_specs=(by_token,) * 2 + (by_row,) * 4 + (by_column,) * 2,
        check_vma=False,
    )
```

time: 246 us -> 229 us (0.931)
  starting transfers between devices: 39 us -> 73.9 us
  blocking collectives: 90.4 us -> 66.3 us
  waiting for transfers between devices: 76.5 us -> 61 us
  between operations: 14.6 us -> 1 us
  Pallas kernels: 0 us -> 8.87 us
  other arithmetic: 6.7 us -> 0.26 us
  matrix products: 10.6 us -> 5.46 us
  local copies, waits for them, and re-layouts: 7.73 us -> 11.4 us
    all_to_all x2 -> x0, blocking collectives: 30.4 us -> none  [the longest x1 15.9 us: body(): got = lax.all_to_all(send, PLANE, split_axis=0, concat_axis=0, tiled=True)]
    ppermute x1 -> x7, starting transfers between devices: 2.81 us -> 27.7 us  [the longest x6 25.8 us: along_ring(): return lax.ppermute(value, RING, pairs)]
    ppermute x1 -> x7, waiting for transfers between devices: 1.48 us -> 25.8 us  [the longest x6 24 us: along_ring(): return lax.ppermute(value, RING, pairs)]
    all_gather x1 -> x0, waiting for transfers between devices: 22.9 us -> none  [body(): weights = lax.all_gather(w_local, 'zb', axis=0, tiled=True)]
    all_to_all x0 -> x2, starting transfers between devices: none -> 13.1 us  [the longest x1 6.76 us: body(): got = lax.all_to_all(send, PLANE, split_axis=0, concat_axis=0, tiled=True)]
    reduce_scatter x1 -> x0, waiting for transfers between devices: 12.4 us -> none  [body(): w_grads = lax.psum_scatter(w_grads, 'zb', scatter_dimension=0, tiled=True)]
    all_gather x1, blocking collectives: 3.28 us -> 13.8 us  [body(): rows = lax.all_gather(rows, 'core', axis=0, tiled=True)]
    pallas_call x0 -> x10, Pallas kernels: none -> 8.87 us  [kernel_call(): pl.pallas_call(kernel, out_shape=tuple(outs), in_specs=[pl.BlockSpec(memo...]
  transfers between devices with their start and end apart: 8 -> 14, of which waited for: 7 -> 10; matrix products, arithmetic and copies ran while one was open for 4% -> 3% of each run, Pallas kernels for 0% -> 1%
where the time goes in v2:
time: 229 us; the launch traced here: 228 us
  starting transfers between devices  73.9 us (32%)
  blocking collectives  66.3 us (29%)
  waiting for transfers between devices  61 us (27%)
  local copies, waits for them, and re-layouts  11.4 us (5%)
  Pallas kernels  8.87 us (4%)
  matrix products  5.46 us (2%)
    all_to_all x1, blocking collectives, body(): lax.all_to_all(outs, ('core', 'za'), split_axis=0, concat_axis=0, tiled=T...  31.3 us
    ppermute x6, starting transfers between devices, along_ring(): return lax.ppermute(value, RING, pairs)  25.8 us
    ppermute x4, starting transfers between devices, shift(): lax.ppermute(value, 'za', [(i, (i + step) % QUAD) for i in range(QUAD)])  24.3 us
    ppermute x6, waiting for transfers between devices, along_ring(): return lax.ppermute(value, RING, pairs)  24 us
    all_gather x1, blocking collectives, body(): rows = lax.all_gather(rows, 'za', axis=0, tiled=True)  21.2 us
    all_to_all x1, waiting for transfers between devices, body(): lax.all_to_all(got, ('core', 'za'), split_axis=0, concat_axis=0, tiled=True)  17.1 us
    all_gather x1, blocking collectives, body(): rows = lax.all_gather(rows, 'core', axis=0, tiled=True)  13.8 us
    unnamed x40, local copies, waits for them, and re-layouts  10.5 us
  transfers between devices with their start and end apart: 14, of which 10 were waited for; matrix products, arithmetic and copies ran while one was open for 3% of the time, Pallas kernels for 1%

profile of v2, /device:TPU:1, one launch (start us, length us, event | category | flops | bytes accessed | tf_op | source)
XLA Modules:
  0.0 228.3 jit_solution(3479116401572925032)
XLA Ops:
  9.4 5.7 %collective-permute-start.2 = (bf16[128,2304]{1,0:T(8,128)(2,1)S(1)}, bf16[128,2304]{1,0:T(8,128)(2,1)S(1)}, u32[]{:S(2)}, u32[]{:S(2)}) collective-permute-start(bf16[128,2304]{1,0:T(8,128)(2,1)S(1)} %shard_map.188.w0), channel_id=1, source_target_pairs={{0,28},{1,5},{2,30},{3,7},{4,0},{5,9},{6,2},{7,11},{8,4},{9,13},{1... | collective-permute-start | bytes 1769480 | tf_op jit(solution)/shard_map/ppermute | solution.py:40
  15.1 3.5 %collective-permute-start.1 = (bf16[128,2304]{1,0:T(8,128)(2,1)S(1)}, bf16[128,2304]{1,0:T(8,128)(2,1)S(1)}, u32[]{:S(2)}, u32[]{:S(2)}) collective-permute-start(bf16[128,2304]{1,0:T(8,128)(2,1)S(1)} %shard_map.188.w0), channel_id=1, source_target_pairs={{0,2},{1,3},{2,4},{3,5},{4,6},{5,7},{6,8},{7,9},{8,10},{9,11},{10,... | collective-permute-start | bytes 1769480 | tf_op jit(solution)/shard_map/ppermute | solution.py:40
  18.7 6.5 %collective-permute-start = (bf16[128,2304]{1,0:T(8,128)(2,1)S(1)}, bf16[128,2304]{1,0:T(8,128)(2,1)S(1)}, u32[]{:S(2)}, u32[]{:S(2)}) collective-permute-start(bf16[128,2304]{1,0:T(8,128)(2,1)S(1)} %shard_map.188.w0), channel_id=1, source_target_pairs={{0,30},{1,31},{2,0},{3,1},{4,2},{5,3},{6,4},{7,5},{8,6},{9,7},{10,... | collective-permute-start | bytes 1769480 | tf_op jit(solution)/shard_map/ppermute | solution.py:40
  27.3 6.8 %all-to-all-start = ((bf16[16,24,512]{2,1,0:T(8,128)(2,1)}), bf16[16,24,512]{2,1,0:T(8,128)(2,1)S(1)}, u32[]{:S(2)}, u32[]{:S(2)}) async-start(bf16[16,24,512]{2,1,0:T(8,128)(2,1)} %bitcast.11), calls=%async_computation | async-start | bytes 786432 | tf_op jit(solution)/shard_map/all_to_all | solution.py:281
  34.0 8.2 %all-to-all-done.got = bf16[16,24,512]{2,1,0:T(8,128)(2,1)S(1)} async-done(((bf16[16,24,512]{2,1,0:T(8,128)(2,1)}), bf16[16,24,512]{2,1,0:T(8,128)(2,1)S(1)}, u32[]{:S(2)}, u32[]{:S(2)}) %all-to-all-start) | async-done | bytes 393248 | tf_op jit(solution)/shard_map/all_to_all | solution.py:281
  42.3 5.6 %collective-permute-done.1.rest_1_.w2 = bf16[128,2304]{1,0:T(8,128)(2,1)S(1)} collective-permute-done((bf16[128,2304]{1,0:T(8,128)(2,1)S(1)}, bf16[128,2304]{1,0:T(8,128)(2,1)S(1)}, u32[]{:S(2)}, u32[]{:S(2)}) %collective-permute-start.1) | collective-permute-done | bytes 589856 | tf_op jit(solution)/shard_map/ppermute | solution.py:40
  48.7 8.8 %all-to-all-start.1 = ((bf16[8,24,1024]{2,1,0:T(8,128)(2,1)}), bf16[8,24,1024]{2,1,0:T(8,128)(2,1)S(1)}, u32[]{:S(2)}, u32[]{:S(2)}) async-start(bf16[8,24,1024]{2,1,0:T(8,128)(2,1)} %shard_map.189), calls=%async_computation.1 | async-start | bytes 786432 | tf_op jit(solution)/shard_map/all_to_all | solution.py:291
  57.5 17.1 %all-to-all-done.1 = bf16[8,24,1024]{2,1,0:T(8,128)(2,1)S(1)} async-done(((bf16[8,24,1024]{2,1,0:T(8,128)(2,1)}), bf16[8,24,1024]{2,1,0:T(8,128)(2,1)S(1)}, u32[]{:S(2)}, u32[]{:S(2)}) %all-to-all-start.1) | async-done | bytes 393248 | tf_op jit(solution)/shard_map/all_to_all | solution.py:291
  76.6 1.9 collective-permute-start.3
  78.5 1.8 collective-permute-done.3.other
  80.3 1.2 copy-done.4
  81.5 13.2 %collective-permute-start.4 = (bf16[24,1152]{1,0:T(8,128)(2,1)S(1)}, bf16[24,1152]{1,0:T(8,128)(2,1)S(1)}, u32[]{:S(2)}, u32[]{:S(2)}) collective-permute-start(bf16[24,1152]{1,0:T(8,128)(2,1)S(1)} %get-tuple-element.32), channel_id=1, source_target_pairs={{0,8},{8,16},{16,24},{24,0},{1,9},{9,17},{17,25},{25,1},{2,10},{10... | collective-permute-start | bytes 165896 | tf_op jit(solution)/shard_map/ppermute | solution.py:30
  94.8 1.9 collective-permute-start.5
  96.7 7.0 %collective-permute-done.5.from_right = bf16[24,1152]{1,0:T(8,128)(2,1)S(1)} collective-permute-done((bf16[24,1152]{1,0:T(8,128)(2,1)S(1)}, bf16[24,1152]{1,0:T(8,128)(2,1)S(1)}, u32[]{:S(2)}, u32[]{:S(2)}) %collective-permute-start.5) | collective-permute-done | bytes 55328 | tf_op jit(solution)/shard_map/ppermute | solution.py:30
  103.7 2.4 %collective-permute-start.6 = (bf16[24,2304]{1,0:T(8,128)(2,1)S(1)}, bf16[24,2304]{1,0:T(8,128)(2,1)S(1)}, u32[]{:S(2)}, u32[]{:S(2)}) collective-permute-start(bf16[24,2304]{1,0:T(8,128)(2,1)S(1)} %get-tuple-element.34), channel_id=1, source_target_pairs={{0,8},{8,16},{16,24},{24,0},{1,9},{9,17},{17,25},{25,1},{2,10},{10... | collective-permute-start | bytes 331784 | tf_op jit(solution)/shard_map/ppermute | solution.py:30
  106.2 6.8 %collective-permute-start.7 = (bf16[24,2304]{1,0:T(8,128)(2,1)S(1)}, bf16[24,2304]{1,0:T(8,128)(2,1)S(1)}, u32[]{:S(2)}, u32[]{:S(2)}) collective-permute-start(bf16[24,2304]{1,0:T(8,128)(2,1)S(1)} %get-tuple-element.35), channel_id=1, source_target_pairs={{0,24},{8,0},{16,8},{24,16},{1,25},{9,1},{17,9},{25,17},{2,26},{10... | collective-permute-start | bytes 331784 | tf_op jit(solution)/shard_map/ppermute | solution.py:30
  114.0 1.8 collective-permute-done.7.from_right
  115.9 21.2 %all_gather.6 = bf16[96,2304]{1,0:T(8,128)(2,1)S(1)} all-gather(bf16[24,2304]{1,0:T(8,128)(2,1)S(1)} %shard_map.193), channel_id=1, replica_groups=mesh['y'=4,'x'=4,'za'=4,'zb'=4,'core'=2] {'za'}, dimensions={0}, use_global_device_ids=true | all-gather | bytes 552960 | tf_op jit(solution)/shard_map/all_gather | solution.py:320
  137.1 13.8 %all_gather.7.rows = bf16[192,2304]{1,0:T(8,128)(2,1)S(1)} all-gather(bf16[96,2304]{1,0:T(8,128)(2,1)S(1)} %all_gather.6), channel_id=1, replica_groups=mesh['y'=4,'x'=4,'za'=4,'zb'=4,'core'=2] {'core'}, dimensions={0}, use_global_device_ids=true | all-gather | bytes 1327104 | tf_op jit(solution)/shard_map/all_gather | solution.py:321
  152.0 31.3 %all_to_all.20.got.after = bf16[8,24,1024]{2,1,0:T(8,128)(2,1)S(1)} all-to-all(bf16[8,24,1024]{2,1,0:T(8,128)(2,1)S(1)} %bitcast.30), channel_id=1, replica_groups=mesh['y'=4,'x'=4,'za'=4,'zb'=4,'core'=2] {'core','za'}, dimensions={0} | all-to-all | bytes 786432 | tf_op jit(solution)/shard_map/all_to_all | solution.py:326
  184.1 6.4 %all-to-all-start.3 = ((bf16[16,24,512]{2,1,0:T(8,128)(2,1)}), bf16[16,24,512]{2,1,0:T(8,128)(2,1)}, u32[]{:S(2)}, u32[]{:S(2)}) async-start(bf16[16,24,512]{2,1,0:T(8,128)(2,1)} %shard_map.195), calls=%async_computation.3 | async-start | bytes 786432 | tf_op jit(solution)/shard_map/all_to_all | solution.py:351
  190.6 1.7 shard_map.196
  192.3 1.9 collective-permute-start.8
  194.2 5.0 %collective-permute-start.9 = (bf16[128,2304]{1,0:T(8,128)(2,1)}, bf16[128,2304]{1,0:T(8,128)(2,1)S(1)}, u32[]{:S(2)}, u32[]{:S(2)}) collective-permute-start(bf16[128,2304]{1,0:T(8,128)(2,1)} %get-tuple-element.38), channel_id=1, source_target_pairs={{0,30},{1,31},{2,0},{3,1},{4,2},{5,3},{6,4},{7,5},{8,6},{9,7},{10,... | collective-permute-start | bytes 1769480 | tf_op jit(solution)/shard_map/ppermute | solution.py:40
  199.2 3.1 %collective-permute-start.10 = (bf16[128,2304]{1,0:T(8,128)(2,1)}, bf16[128,2304]{1,0:T(8,128)(2,1)}, u32[]{:S(2)}, u32[]{:S(2)}) collective-permute-start(bf16[128,2304]{1,0:T(8,128)(2,1)} %get-tuple-element.39), channel_id=1, source_target_pairs={{0,4},{1,29},{2,6},{3,31},{4,8},{5,1},{6,10},{7,3},{8,12},{9,5},{1... | collective-permute-start | bytes 1769480 | tf_op jit(solution)/shard_map/ppermute | solution.py:40
  202.3 1.8 convolution_convert_fusion.2
  204.1 1.2 convolution_multiply_fusion.1
  205.3 1.8 fusion.1
  207.1 3.4 %collective-permute-done.8.g1 = bf16[128,2304]{1,0:T(8,128)(2,1)S(1)} collective-permute-done((bf16[128,2304]{1,0:T(8,128)(2,1)}, bf16[128,2304]{1,0:T(8,128)(2,1)S(1)}, u32[]{:S(2)}, u32[]{:S(2)}) %collective-permute-start.8) | collective-permute-done | bytes 589856 | tf_op jit(solution)/shard_map/ppermute | solution.py:40
  210.5 3.3 %collective-permute-done.9.g2 = bf16[128,2304]{1,0:T(8,128)(2,1)S(1)} collective-permute-done((bf16[128,2304]{1,0:T(8,128)(2,1)}, bf16[128,2304]{1,0:T(8,128)(2,1)S(1)}, u32[]{:S(2)}, u32[]{:S(2)}) %collective-permute-start.9) | collective-permute-done | bytes 589856 | tf_op jit(solution)/shard_map/ppermute | solution.py:40
  213.7 11.7 %collective-permute-done.10.g3 = bf16[128,2304]{1,0:T(8,128)(2,1)} collective-permute-done((bf16[128,2304]{1,0:T(8,128)(2,1)}, bf16[128,2304]{1,0:T(8,128)(2,1)}, u32[]{:S(2)}, u32[]{:S(2)}) %collective-permute-start.10) | collective-permute-done | bytes 589856 | tf_op jit(solution)/shard_map/ppermute | solution.py:40
  225.5 2.8 %shard_map.197 = (f32[1,128,768]{2,1,0:T(8,128)}, f32[1,128,768]{2,1,0:T(8,128)}, f32[1,128,768]{2,1,0:T(8,128)}, f32[1,128,768]{2,1,0:T(8,128)}, f32[1,768,128]{2,1,0:T(8,128)}, /*index=5*/f32[1,768,128]{2,1,0:T(8,128)}) custom-call(f32[128,2304]{1,0:T(8,128)S(1)} %get-tuple-element.36.g0, bf16[128,2304]{1,0:T(8,128)(2,1)S(1)} %collective-permute-done.8.g1, ...), custom_call_target="tpu_custom_call" | custom-call | bytes 5898240 | tf_op jit(solution)/shard_map/pallas_call | solution.py:49
  (62 shorter events, 16.7 us)
Async XLA Ops:
  0.6 24.9 %copy-start = (bf16[128,256]{1,0:T(8,128)(2,1)S(1)}, bf16[128,256]{1,0:T(8,128)(2,1)}, u32[]{:S(2)}) copy-start(bf16[128,256]{1,0:T(8,128)(2,1)} %param.13) | copy-start | bytes 196612
  0.7 1.0 copy-start.5
  1.6 0.9 copy-start.7
  2.5 0.9 copy-start.9
  3.5 0.9 copy-start.11
  4.4 0.9 copy-start.12
  5.3 0.9 copy-start.13
  6.2 0.9 copy-start.14
  9.0 16.2 %copy-start.19 = (f32[128,2]{0,1:T(2,128)S(1)}, f32[128,2]{0,1:T(2,128)}, u32[]{:S(2)}) copy-start(f32[128,2]{0,1:T(2,128)} %param.16) | copy-start | bytes 3076
  9.0 16.2 %copy-start.18 = (s32[128,2]{0,1:T(2,128)S(1)}, s32[128,2]{0,1:T(2,128)}, u32[]{:S(2)}) copy-start(s32[128,2]{0,1:T(2,128)} %param.15) | copy-start | bytes 3076
  9.0 16.8 %copy-start.17 = (bf16[128,256]{1,0:T(8,128)(2,1)S(1)}, bf16[128,256]{1,0:T(8,128)(2,1)}, u32[]{:S(2)}) copy-start(bf16[128,256]{1,0:T(8,128)(2,1)} %param.14) | copy-start | bytes 196612
  9.4 32.9 %collective-permute-start.2 = (bf16[128,2304]{1,0:T(8,128)(2,1)S(1)}, bf16[128,2304]{1,0:T(8,128)(2,1)S(1)}, u32[]{:S(2)}, u32[]{:S(2)}) collective-permute-start(bf16[128,2304]{1,0:T(8,128)(2,1)S(1)} %shard_map.188.w0), channel_id=1, source_target_pairs={{0,28},{1,5},{2,30},{3,7},{4,0},{5,9},{6,2},{7,11},{8,4},{9,13},{1... | collective-permute-start | bytes 1769480 | tf_op jit(solution)/shard_map/ppermute | solution.py:40
  15.1 32.7 %collective-permute-start.1 = (bf16[128,2304]{1,0:T(8,128)(2,1)S(1)}, bf16[128,2304]{1,0:T(8,128)(2,1)S(1)}, u32[]{:S(2)}, u32[]{:S(2)}) collective-permute-start(bf16[128,2304]{1,0:T(8,128)(2,1)S(1)} %shard_map.188.w0), channel_id=1, source_target_pairs={{0,2},{1,3},{2,4},{3,5},{4,6},{5,7},{6,8},{7,9},{8,10},{9,11},{10,... | collective-permute-start | bytes 1769480 | tf_op jit(solution)/shard_map/ppermute | solution.py:40
  18.7 29.2 %collective-permute-start = (bf16[128,2304]{1,0:T(8,128)(2,1)S(1)}, bf16[128,2304]{1,0:T(8,128)(2,1)S(1)}, u32[]{:S(2)}, u32[]{:S(2)}) collective-permute-start(bf16[128,2304]{1,0:T(8,128)(2,1)S(1)} %shard_map.188.w0), channel_id=1, source_target_pairs={{0,30},{1,31},{2,0},{3,1},{4,2},{5,3},{6,4},{7,5},{8,6},{9,7},{10,... | collective-permute-start | bytes 1769480 | tf_op jit(solution)/shard_map/ppermute | solution.py:40
  27.3 15.0 %all-to-all-start = ((bf16[16,24,512]{2,1,0:T(8,128)(2,1)}), bf16[16,24,512]{2,1,0:T(8,128)(2,1)S(1)}, u32[]{:S(2)}, u32[]{:S(2)}) async-start(bf16[16,24,512]{2,1,0:T(8,128)(2,1)} %bitcast.11), calls=%async_computation | async-start | bytes 786432 | tf_op jit(solution)/shard_map/all_to_all | solution.py:281
  48.7 25.9 %all-to-all-start.1 = ((bf16[8,24,1024]{2,1,0:T(8,128)(2,1)}), bf16[8,24,1024]{2,1,0:T(8,128)(2,1)S(1)}, u32[]{:S(2)}, u32[]{:S(2)}) async-start(bf16[8,24,1024]{2,1,0:T(8,128)(2,1)} %shard_map.189), calls=%async_computation.1 | async-start | bytes 786432 | tf_op jit(solution)/shard_map/all_to_all | solution.py:291
  74.6 1.1 copy-start.1
  75.7 0.9 copy-start.3
  76.6 3.7 %collective-permute-start.3 = (bf16[4,24,2304]{2,1,0:T(8,128)(2,1)S(1)}, bf16[4,24,2304]{2,1,0:T(8,128)(2,1)S(1)}, u32[]{:S(2)}, u32[]{:S(2)}) collective-permute-start(bf16[4,24,2304]{2,1,0:T(8,128)(2,1)S(1)} %get-tuple-element.28), channel_id=1, source_target_pairs={{0,1},{1,0},{2,3},{3,2},{4,5},{5,4},{6,7},{7,6},{8,9},{9,8},{10,11... | collective-permute-start | bytes 1327112 | tf_op jit(solution)/shard_map/ppermute | solution.py:305
  80.3 1.2 copy-start.4
  81.5 15.2 %collective-permute-start.4 = (bf16[24,1152]{1,0:T(8,128)(2,1)S(1)}, bf16[24,1152]{1,0:T(8,128)(2,1)S(1)}, u32[]{:S(2)}, u32[]{:S(2)}) collective-permute-start(bf16[24,1152]{1,0:T(8,128)(2,1)S(1)} %get-tuple-element.32), channel_id=1, source_target_pairs={{0,8},{8,16},{16,24},{24,0},{1,9},{9,17},{17,25},{25,1},{2,10},{10... | collective-permute-start | bytes 165896 | tf_op jit(solution)/shard_map/ppermute | solution.py:30
  94.8 8.9 %collective-permute-start.5 = (bf16[24,1152]{1,0:T(8,128)(2,1)S(1)}, bf16[24,1152]{1,0:T(8,128)(2,1)S(1)}, u32[]{:S(2)}, u32[]{:S(2)}) collective-permute-start(bf16[24,1152]{1,0:T(8,128)(2,1)S(1)} %get-tuple-element.33), channel_id=1, source_target_pairs={{0,24},{8,0},{16,8},{24,16},{1,25},{9,1},{17,9},{25,17},{2,26},{10... | collective-permute-start | bytes 165896 | tf_op jit(solution)/shard_map/ppermute | solution.py:30
  103.7 10.3 %collective-permute-start.6 = (bf16[24,2304]{1,0:T(8,128)(2,1)S(1)}, bf16[24,2304]{1,0:T(8,128)(2,1)S(1)}, u32[]{:S(2)}, u32[]{:S(2)}) collective-permute-start(bf16[24,2304]{1,0:T(8,128)(2,1)S(1)} %get-tuple-element.34), channel_id=1, source_target_pairs={{0,8},{8,16},{16,24},{24,0},{1,9},{9,17},{17,25},{25,1},{2,10},{10... | collective-permute-start | bytes 331784 | tf_op jit(solution)/shard_map/ppermute | solution.py:30
  106.2 9.7 %collective-permute-start.7 = (bf16[24,2304]{1,0:T(8,128)(2,1)S(1)}, bf16[24,2304]{1,0:T(8,128)(2,1)S(1)}, u32[]{:S(2)}, u32[]{:S(2)}) collective-permute-start(bf16[24,2304]{1,0:T(8,128)(2,1)S(1)} %get-tuple-element.35), channel_id=1, source_target_pairs={{0,24},{8,0},{16,8},{24,16},{1,25},{9,1},{17,9},{25,17},{2,26},{10... | collective-permute-start | bytes 331784 | tf_op jit(solution)/shard_map/ppermute | solution.py:30
  152.0 38.5 %copy-start.2 = (bf16[8,24,1024]{2,1,0:T(8,128)(2,1)S(1)}, bf16[8,24,1024]{2,1,0:T(8,128)(2,1)}, u32[]{:S(2)}) copy-start(bf16[8,24,1024]{2,1,0:T(8,128)(2,1)} %copy-done.1) | copy-start | bytes 1179652
  184.1 18.2 %all-to-all-start.3 = ((bf16[16,24,512]{2,1,0:T(8,128)(2,1)}), bf16[16,24,512]{2,1,0:T(8,128)(2,1)}, u32[]{:S(2)}, u32[]{:S(2)}) async-start(bf16[16,24,512]{2,1,0:T(8,128)(2,1)} %shard_map.195), calls=%async_computation.3 | async-start | bytes 786432 | tf_op jit(solution)/shard_map/all_to_all | solution.py:351
  190.5 34.9 %copy-start.6 = (bf16[1,128,768]{2,1,0:T(8,128)(2,1)S(1)}, bf16[1,128,768]{2,1,0:T(8,128)(2,1)}, u32[]{:S(2)}) copy-start(bf16[1,128,768]{2,1,0:T(8,128)(2,1)} %ng.3) | copy-start | bytes 589828
  190.5 34.9 %copy-start.8 = (bf16[1,128,768]{2,1,0:T(8,128)(2,1)S(1)}, bf16[1,128,768]{2,1,0:T(8,128)(2,1)}, u32[]{:S(2)}) copy-start(bf16[1,128,768]{2,1,0:T(8,128)(2,1)} %nu.3) | copy-start | bytes 589828
  190.5 34.9 %copy-start.10 = (bf16[1,768,128]{2,1,0:T(8,128)(2,1)S(1)}, bf16[1,768,128]{2,1,0:T(8,128)(2,1)}, u32[]{:S(2)}) copy-start(bf16[1,768,128]{2,1,0:T(8,128)(2,1)} %nd.3) | copy-start | bytes 589828
  192.3 18.2 %collective-permute-start.8 = (bf16[128,2304]{1,0:T(8,128)(2,1)}, bf16[128,2304]{1,0:T(8,128)(2,1)S(1)}, u32[]{:S(2)}, u32[]{:S(2)}) collective-permute-start(bf16[128,2304]{1,0:T(8,128)(2,1)} %get-tuple-element.37), channel_id=1, source_target_pairs={{0,2},{1,3},{2,4},{3,5},{4,6},{5,7},{6,8},{7,9},{8,10},{9,11},{10,... | collective-permute-start | bytes 1769480 | tf_op jit(solution)/shard_map/ppermute | solution.py:40
  194.2 19.5 %collective-permute-start.9 = (bf16[128,2304]{1,0:T(8,128)(2,1)}, bf16[128,2304]{1,0:T(8,128)(2,1)S(1)}, u32[]{:S(2)}, u32[]{:S(2)}) collective-permute-start(bf16[128,2304]{1,0:T(8,128)(2,1)} %get-tuple-element.38), channel_id=1, source_target_pairs={{0,30},{1,31},{2,0},{3,1},{4,2},{5,3},{6,4},{7,5},{8,6},{9,7},{10,... | collective-permute-start | bytes 1769480 | tf_op jit(solution)/shard_map/ppermute | solution.py:40
  199.2 26.3 %collective-permute-start.10 = (bf16[128,2304]{1,0:T(8,128)(2,1)}, bf16[128,2304]{1,0:T(8,128)(2,1)}, u32[]{:S(2)}, u32[]{:S(2)}) collective-permute-start(bf16[128,2304]{1,0:T(8,128)(2,1)} %get-tuple-element.39), channel_id=1, source_target_pairs={{0,4},{1,29},{2,6},{3,31},{4,8},{5,1},{6,10},{7,3},{8,12},{9,5},{1... | collective-permute-start | bytes 1769480 | tf_op jit(solution)/shard_map/ppermute | solution.py:40
  (2 other events, 1.9 us)

commit v3 on v2

--- a/solution.py
+++ b/solution.py
@@ -40,7 +40,7 @@
     return lax.ppermute(value, RING, pairs)
 
 
-def kernel_call(kernel, outs, *operands, free=0, scalars=0):
+def kernel_call(kernel, outs, *operands, free=0, scalars=0, scratch=()):
     whole = pl.BlockSpec(memory_space=pltpu.VMEM)
     count = len(operands) - free - scalars
     moved = sum(a.size * a.dtype.itemsize for a in operands) + sum(
@@ -53,17 +53,47 @@
         + [whole] * count
         + [pl.BlockSpec(memory_space=pl.ANY)] * free,
         out_specs=(whole,) * len(outs),
+        scratch_shapes=list(scratch),
         compiler_params=pltpu.CompilerParams(vmem_limit_bytes=8 * 1024 * 1024),
         cost_estimate=pl.CostEstimate(flops=0, bytes_accessed=moved, transcendentals=0),
     )(*operands)
 
 
-def sample_kernel(mg, sg, ng, mu, su, nu, md, sd, nd, out):
-    width = mg.shape[2]
-    out[:, :width] = sampled(mg[0], sg[0], ng[0])
-    out[:, width : 2 * width] = sampled(mu[0], su[0], nu[0])
-    down = md[0].astype(F32) + sd[0].astype(F32) * nd[0].astype(F32)
+def sample_kernel(*refs):
+    sources, out, rows, columns, done = refs[:9], refs[9], refs[10], refs[11], refs[12]
+    places = [rows.at[i] for i in range(6)] + [columns.at[i] for i in range(3)]
+    copies = [
+        pltpu.make_async_copy(source.at[0], place, done.at[i])
+        for i, (source, place) in enumerate(zip(sources, places))
+    ]
+    for copy in copies:
+        copy.start()
+    width = rows.shape[2]
+    for part in range(2):
+        for copy in copies[3 * part : 3 * part + 3]:
+            copy.wait()
+        out[:, part * width : (part + 1) * width] = sampled(
+            rows[3 * part], rows[3 * part + 1], rows[3 * part + 2]
+        )
+    for copy in copies[6:]:
+        copy.wait()
+    down = columns[0].astype(F32) + columns[1].astype(F32) * columns[2].astype(F32)
     out[:, 2 * width :] = down.T.astype(BF)
+
+
+def pick_kernel(route, weight, tokens, cotangent, out):
+    experts, cap, feats = out.shape[0], out.shape[1], tokens.shape[1]
+    one, two = place_routes(route[...], experts, cap)
+    cot = cotangent[...].astype(F32)
+    x = contract(one + two, tokens[...], 0, 0).astype(BF)
+    d = (
+        contract(one, (weight[:, 0:1] * cot).astype(BF), 0, 0)
+        + contract(two, (weight[:, 1:2] * cot).astype(BF), 0, 0)
+    ).astype(BF)
+    for expert in range(experts):
+        rows = slice(expert * cap, (expert + 1) * cap)
+        out[expert, :, :feats] = x[rows]
+        out[expert, :, feats:] = d[rows]
 
 
 def spread_kernel(where, got, *rest):
@@ -81,7 +111,8 @@
                     ]
 
 
-def collect_kernel(where, got, out):
+def collect_kernel(where, got, *rest):
+    out = rest[-1]
     chips, half = out.shape[0], out.shape[2] // 4
     for core in range(2):
         for za in range(QUAD):
@@ -95,36 +126,47 @@
                     ]
 
 
-def forward_kernel(where, slots, w0, w1, w2, w3, mine, other):
-    quads, cap, width = mine.shape[0], mine.shape[1], w0.shape[1] // 3
-    rows, half = quads * cap, w0.shape[0]
-    core = where[0]
-    for side, out in ((core, mine), (1 - core, other)):
-        start = pl.multiple_of(side * rows, rows)
-        for part in range(3):
-            kind = part // 2
-            total = None
-            for at, w in enumerate((w0, w1, w2, w3)):
-                lane = (4 * kind + at) * half
-                term = contract(
-                    slots[pl.ds(start, rows), lane : lane + half],
-                    w[:, part * width : (part + 1) * width],
-                    1,
-                    0,
-                )
-                total = term if total is None else total + term
-            for quad in range(quads):
-                out[quad, :, part * width : (part + 1) * width] = total[
-                    quad * cap : (quad + 1) * cap
-                ].astype(out.dtype)
-
-
-def split_kernel(where, mine, other, far_right, far_left, own, ahead, behind):
-    me, cut = where[0], far_right.shape[1]
+def partial_sum(slots, weights, side, rows, part):
+    width, half = weights[0].shape[1] // 3, weights[0].shape[0]
+    start = pl.multiple_of(side * rows, rows)
+    total = None
+    for at, w in enumerate(weights):
+        lane = (4 * (part // 2) + at) * half
+        term = contract(
+            slots[pl.ds(start, rows), lane : lane + half],
+            w[:, part * width : (part + 1) * width],
+            1,
+            0,
+        )
+        total = term if total is None else total + term
+    return total
+
+
+def sibling_kernel(where, slots, w0, w1, w2, w3, out):
+    quads, cap, width = out.shape[0], out.shape[1], w0.shape[1] // 3
+    for part in range(3):
+        total = partial_sum(slots, (w0, w1, w2, w3), 1 - where[0], quads * cap, part)
+        for quad in range(quads):
+            out[quad, :, part * width : (part + 1) * width] = total[
+                quad * cap : (quad + 1) * cap
+            ].astype(out.dtype)
+
+
+def split_kernel(
+    where, slots, w0, w1, w2, w3, other, far_right, far_left, own, ahead, behind, mine
+):
+    quads, cap, width = other.shape[0], other.shape[1], w0.shape[1] // 3
+    core, me, cut = where[0], where[1], far_right.shape[1]
+    for part in range(3):
+        lanes = slice(part * width, (part + 1) * width)
+        total = partial_sum(slots, (w0, w1, w2, w3), core, quads * cap, part)
+        for quad in range(quads):
+            mine[quad, :, lanes] = total[quad * cap : (quad + 1) * cap] + other[
+                quad, :, lanes
+            ].astype(F32)
 
     def piece(step, lanes):
-        at = jnp.bitwise_and(me + step, QUAD - 1)
-        return mine[at, :, lanes] + other[at, :, lanes].astype(F32)
+        return mine[jnp.bitwise_and(me + step, QUAD - 1), :, lanes]
 
     whole = slice(0, 2 * cut)
     far_right[...] = piece(2, slice(0, cut)).astype(BF)
@@ -180,6 +222,17 @@
         g[:, 2 * width :] = value.astype(g.dtype)
 
 
+def combine_kernel(route, weight, home, mixed, grad):
+    experts, cap, feats = home.shape[0], home.shape[1], mixed.shape[1]
+    one, two = place_routes(route[...], experts, cap)
+    slots = jnp.concatenate([home[e].astype(F32) for e in range(experts)], axis=0).astype(BF)
+    mixed[...] = (
+        weight[:, 0:1] * contract(one, slots[:, :feats], 1, 0)
+        + weight[:, 1:2] * contract(two, slots[:, :feats], 1, 0)
+    ).astype(BF)
+    grad[...] = contract(one + two, slots[:, feats:], 1, 0).astype(BF)
+
+
 def finish_kernel(g0, g1, g2, g3, ng, nu, nd, mg, sg, mu, su, md, sd):
     width = ng.shape[2]
 
@@ -200,23 +253,25 @@
     sd[0] = down * nd[0].astype(F32)
 
 
+def ones_where(condition):
+    return jnp.where(condition, 1.0, 0.0).astype(F32)
+
+
 def place_routes(route, experts, capacity):
     rows = route.shape[0]
     names = lax.broadcasted_iota(jnp.int32, (rows, experts), 1)
-    first = (route[:, 0:1] == names).astype(BF)
-    second = (route[:, 1:2] == names).astype(BF)
-    below = (
+    first = ones_where(route[:, 0:1] == names)
+    second = ones_where(route[:, 1:2] == names)
+    below = ones_where(
         lax.broadcasted_iota(jnp.int32, (rows, rows), 0)
         > lax.broadcasted_iota(jnp.int32, (rows, rows), 1)
     ).astype(BF)
-    earlier = contract(below, first + second, 1, 0)
-    place_first = jnp.sum(earlier * first.astype(F32), axis=1, keepdims=True)
-    place_second = jnp.sum(
-        (earlier + first.astype(F32)) * second.astype(F32), axis=1, keepdims=True
-    )
+    earlier = contract(below, (first + second).astype(BF), 1, 0)
+    place_first = jnp.sum(earlier * first, axis=1, keepdims=True).astype(jnp.int32)
+    place_second = jnp.sum((earlier + first) * second, axis=1, keepdims=True).astype(jnp.int32)
     slots = lax.broadcasted_iota(jnp.int32, (rows, experts * capacity), 1)
-    one = (route[:, 0:1] * capacity + place_first.astype(jnp.int32) == slots).astype(BF)
-    two = (route[:, 1:2] * capacity + place_second.astype(jnp.int32) == slots).astype(BF)
+    one = ones_where(route[:, 0:1] * capacity + place_first == slots).astype(BF)
+    two = ones_where(route[:, 1:2] * capacity + place_second == slots).astype(BF)
     return one, two
 
 
@@ -246,9 +301,18 @@
     zb = lax.axis_index("zb").astype(jnp.int32).reshape(1)
     core = lax.axis_index("core").astype(jnp.int32).reshape(1)
 
-    (w_own,) = kernel_call(
+    w_own = pl.pallas_call(
         sample_kernel,
-        [jax.ShapeDtypeStruct((half, 3 * width), BF)],
+        out_shape=jax.ShapeDtypeStruct((half, 3 * width), BF),
+        in_specs=[pl.BlockSpec(memory_space=pltpu.HBM)] * 9,
+        out_specs=pl.BlockSpec(memory_space=pltpu.VMEM),
+        scratch_shapes=[
+            pltpu.VMEM((6, half, width), BF),
+            pltpu.VMEM((3, width, half), BF),
+            pltpu.SemaphoreType.DMA((9,)),
+        ],
+        compiler_params=pltpu.CompilerParams(vmem_limit_bytes=60 * 1024 * 1024),
+    )(
         mean_gate,
         spread_gate,
         noise_gate,
@@ -266,18 +330,14 @@
         along_ring(w_own, (-2, 2)),
     )
 
-    one, two = place_routes(route, experts, cap)
-    cot = cotangent.astype(F32)
-    scaled = jnp.concatenate(
-        [
-            (route_weight[:, 0:1] * cot).astype(BF),
-            (route_weight[:, 1:2] * cot).astype(BF),
-        ],
-        axis=0,
-    )
-    send_x = contract(one + two, tokens, 0, 0).astype(BF)
-    send_d = contract(jnp.concatenate([one, two], axis=0), scaled, 0, 0).astype(BF)
-    send = jnp.concatenate([send_x, send_d], axis=1).reshape(experts, cap, 2 * feats)
+    (send,) = kernel_call(
+        pick_kernel,
+        [jax.ShapeDtypeStruct((experts, cap, 2 * feats), BF)],
+        route,
+        route_weight,
+        tokens,
+        cotangent,
+    )
     got = lax.all_to_all(send, PLANE, split_axis=0, concat_axis=0, tiled=True)
     (got,) = kernel_call(
         spread_kernel,
@@ -291,12 +351,9 @@
     got = lax.all_to_all(got, ("core", "za"), split_axis=0, concat_axis=0, tiled=True)
     slots = got.reshape(rows_all, 8 * half)
 
-    mine, other = kernel_call(
-        forward_kernel,
-        [
-            jax.ShapeDtypeStruct((QUAD, cap, 3 * width), F32),
-            jax.ShapeDtypeStruct((QUAD, cap, 3 * width), BF),
-        ],
+    (other,) = kernel_call(
+        sibling_kernel,
+        [jax.ShapeDtypeStruct((QUAD, cap, 3 * width), BF)],
         core,
         slots,
         *weights,
@@ -308,7 +365,14 @@
     wire = jax.ShapeDtypeStruct((cap, 3 * width), BF)
     half_wire = jax.ShapeDtypeStruct((cap, cut), BF)
     far_right, far_left, own, ahead, behind = kernel_call(
-        split_kernel, [half_wire] * 2 + [total] * 3, me, mine, other, scalars=1
+        split_kernel,
+        [half_wire] * 2 + [total] * 3,
+        jnp.concatenate([core, me]),
+        slots,
+        *weights,
+        other,
+        scalars=1,
+        scratch=[pltpu.VMEM((QUAD, cap, 3 * width), F32)],
     )
     to_right, to_left = kernel_call(
         relay_kernel, [wire] * 2, ahead, behind, shift(far_right, 1), shift(far_left, -1)
@@ -325,7 +389,7 @@
     outs = outs.reshape(2 * QUAD, cap, 8 * half)
     home = lax.all_to_all(outs, ("core", "za"), split_axis=0, concat_axis=0, tiled=True)
 
-    w_grads = kernel_call(
+    w_sent = kernel_call(
         grads_kernel,
         [jax.ShapeDtypeStruct((half, 3 * width), F32)]
         + [jax.ShapeDtypeStruct((half, 3 * width), BF)] * 3,
@@ -335,10 +399,10 @@
         free=1,
     )
     w_grads = (
-        w_grads[0],
-        along_ring(w_grads[1], (1, 1)),
-        along_ring(w_grads[2], (-1, -1)),
-        along_ring(w_grads[3], (2, -2)),
+        w_sent[0],
+        along_ring(w_sent[1], (1, 1)),
+        along_ring(w_sent[2], (-1, -1)),
+        along_ring(w_sent[3], (2, -2)),
     )
 
     (home,) = kernel_call(
@@ -346,15 +410,18 @@
         [jax.ShapeDtypeStruct((experts, cap, 2 * feats), BF)],
         zb,
         home,
+        w_sent[3],
         scalars=1,
+        free=1,
     )
     home = lax.all_to_all(home, PLANE, split_axis=0, concat_axis=0, tiled=True)
-    home = home.reshape(experts * cap, 2 * feats)
-    out_one = contract(one, home[:, :feats], 1, 0)
-    out_two = contract(two, home[:, :feats], 1, 0)
-    mixed_out = (route_weight[:, 0:1] * out_one + route_weight[:, 1:2] * out_two).astype(BF)
-    token_grad = contract(one + two, home[:, feats:], 1, 0).astype(BF)
-
+    mixed_out, token_grad = kernel_call(
+        combine_kernel,
+        [jax.ShapeDtypeStruct((group_rows, feats), BF)] * 2,
+        route,
+        route_weight,
+        home,
+    )
     by_row = jax.ShapeDtypeStruct((1, half, width), F32)
     by_column = jax.ShapeDtypeStruct((1, width, half), F32)
     ends = kernel_call(

time: 229 us -> 213 us (0.930)
  waiting for transfers between devices: 61 us -> 48.9 us
  local copies, waits for them, and re-layouts: 11.4 us -> 0.27 us
  blocking collectives: 66.3 us -> 76.7 us
  matrix products: 5.46 us -> 0 us
  Pallas kernels: 8.87 us -> 12.7 us
    all_to_all x0 -> x1, blocking collectives: none -> 16.8 us  [body(): home = lax.all_to_all(home, PLANE, split_axis=0, concat_axis=0, tiled=True)]
    ppermute x6, waiting for transfers between devices: 24 us -> 11.8 us  [along_ring(): return lax.ppermute(value, RING, pairs)]
    unnamed x40 -> x18, local copies, waits for them, and re-layouts: 10.5 us -> 0.27 us
    all_to_all x1 -> x0, starting transfers between devices: 6.37 us -> none  [body(): home = lax.all_to_all(home, PLANE, split_axis=0, concat_axis=0, tiled=True)]
    dot_general x6 -> x0, matrix products: 5.46 us -> none  [contract(): lax.dot_general(left_side, right_side, (((left_dim,), (right_dim,)), ((),...]
    ppermute x6, starting transfers between devices: 25.8 us -> 30.8 us  [along_ring(): return lax.ppermute(value, RING, pairs)]
    all_to_all x1, blocking collectives: 31.3 us -> 26.3 us  [body(): lax.all_to_all(outs, ('core', 'za'), split_axis=0, concat_axis=0, tiled=T...]
    pallas_call x0 -> x1, Pallas kernels: none -> 2.61 us  [body(): pl.pallas_call(sample_kernel, out_shape=jax.ShapeDtypeStruct((half, 3 * w...]
  transfers between devices with their start and end apart: 14 -> 13, of which waited for: 10 -> 8; matrix products, arithmetic and copies ran while one was open for 3% -> 0% of each run, Pallas kernels for 1% -> 1%
where the time goes in v3:
time: 213 us; the launch traced here: 212 us
  blocking collectives  76.7 us (36%)
  starting transfers between devices  72.9 us (34%)
  waiting for transfers between devices  48.9 us (23%)
  Pallas kernels  12.7 us (6%)
    ppermute x6, starting transfers between devices, along_ring(): return lax.ppermute(value, RING, pairs)  30.8 us
    all_to_all x1, blocking collectives, body(): lax.all_to_all(outs, ('core', 'za'), split_axis=0, concat_axis=0, tiled=T...  26.3 us
    ppermute x4, starting transfers between devices, shift(): lax.ppermute(value, 'za', [(i, (i + step) % QUAD) for i in range(QUAD)])  24.3 us
    all_gather x1, blocking collectives, body(): rows = lax.all_gather(rows, 'za', axis=0, tiled=True)  20.1 us
    all_to_all x1, waiting for transfers between devices, body(): lax.all_to_all(got, ('core', 'za'), split_axis=0, concat_axis=0, tiled=True)  17.1 us
    all_to_all x1, blocking collectives, body(): home = lax.all_to_all(home, PLANE, split_axis=0, concat_axis=0, tiled=True)  16.8 us
    all_gather x1, blocking collectives, body(): rows = lax.all_gather(rows, 'core', axis=0, tiled=True)  13.4 us
    ppermute x6, waiting for transfers between devices, along_ring(): return lax.ppermute(value, RING, pairs)  11.8 us
  transfers between devices with their start and end apart: 13, of which 8 were waited for; matrix products, arithmetic and copies ran while one was open for 0% of the time, Pallas kernels for 1%

profile of v3, /device:TPU:1, one launch (start us, length us, event | category | flops | bytes accessed | tf_op | source)
XLA Modules:
  0.0 212.4 jit_solution(13655762457408189510)
XLA Ops:
  0.7 2.6 %shard_map.189.w0 = bf16[128,2304]{1,0:T(8,128)(2,1)} custom-call(bf16[1,128,768]{2,1,0:T(8,128)(2,1)} %refs_0_.1, bf16[1,128,768]{2,1,0:T(8,128)(2,1)} %refs_1_.1, bf16[1,128,768]{2,1,0:T(8,128)(2,1)} %ng.1, bf16[1,128,768]{2,1,0:T(8,128)(2,1)} %refs_3_.1, bf16[1,128,768]{2,1,0:T(8,128)(2,1)} %refs_4_.1, bf16[1,128,768]{2,1,0:T(8,128)(2,1)} %nu.1, ...), custom_call_target="tpu_custom_call" | custom-call | tf_op jit(solution)/shard_map/pallas_call | solution.py:304
  3.3 5.7 %collective-permute-start.2 = (bf16[128,2304]{1,0:T(8,128)(2,1)}, bf16[128,2304]{1,0:T(8,128)(2,1)S(1)}, u32[]{:S(2)}, u32[]{:S(2)}) collective-permute-start(bf16[128,2304]{1,0:T(8,128)(2,1)} %shard_map.189.w0), channel_id=1, source_target_pairs={{0,28},{1,5},{2,30},{3,7},{4,0},{5,9},{6,2},{7,11},{8,4},{9,13},{1... | collective-permute-start | bytes 1769480 | tf_op jit(solution)/shard_map/ppermute | solution.py:40
  9.0 3.5 %collective-permute-start.1 = (bf16[128,2304]{1,0:T(8,128)(2,1)}, bf16[128,2304]{1,0:T(8,128)(2,1)S(1)}, u32[]{:S(2)}, u32[]{:S(2)}) collective-permute-start(bf16[128,2304]{1,0:T(8,128)(2,1)} %shard_map.189.w0), channel_id=1, source_target_pairs={{0,2},{1,3},{2,4},{3,5},{4,6},{5,7},{6,8},{7,9},{8,10},{9,11},{10,... | collective-permute-start | bytes 1769480 | tf_op jit(solution)/shard_map/ppermute | solution.py:40
  12.6 6.5 %collective-permute-start = (bf16[128,2304]{1,0:T(8,128)(2,1)}, bf16[128,2304]{1,0:T(8,128)(2,1)S(1)}, u32[]{:S(2)}, u32[]{:S(2)}) collective-permute-start(bf16[128,2304]{1,0:T(8,128)(2,1)} %shard_map.189.w0), channel_id=1, source_target_pairs={{0,30},{1,31},{2,0},{3,1},{4,2},{5,3},{6,4},{7,5},{8,6},{9,7},{10,... | collective-permute-start | bytes 1769480 | tf_op jit(solution)/shard_map/ppermute | solution.py:40
  19.4 1.5 shard_map.188
  20.9 6.8 %all-to-all-start = ((bf16[16,24,512]{2,1,0:T(8,128)(2,1)}), bf16[16,24,512]{2,1,0:T(8,128)(2,1)S(1)}, u32[]{:S(2)}, u32[]{:S(2)}) async-start(bf16[16,24,512]{2,1,0:T(8,128)(2,1)} %shard_map.188), calls=%async_computation | async-start | bytes 786432 | tf_op jit(solution)/shard_map/all_to_all | solution.py:341
  27.7 8.2 %all-to-all-done.got = bf16[16,24,512]{2,1,0:T(8,128)(2,1)S(1)} async-done(((bf16[16,24,512]{2,1,0:T(8,128)(2,1)}), bf16[16,24,512]{2,1,0:T(8,128)(2,1)S(1)}, u32[]{:S(2)}, u32[]{:S(2)}) %all-to-all-start) | async-done | bytes 393248 | tf_op jit(solution)/shard_map/all_to_all | solution.py:341
  35.9 5.8 %collective-permute-done.1.rest_1_.w2 = bf16[128,2304]{1,0:T(8,128)(2,1)S(1)} collective-permute-done((bf16[128,2304]{1,0:T(8,128)(2,1)}, bf16[128,2304]{1,0:T(8,128)(2,1)S(1)}, u32[]{:S(2)}, u32[]{:S(2)}) %collective-permute-start.1) | collective-permute-done | bytes 589856 | tf_op jit(solution)/shard_map/ppermute | solution.py:40
  42.5 9.1 %all-to-all-start.1 = ((bf16[8,24,1024]{2,1,0:T(8,128)(2,1)}), bf16[8,24,1024]{2,1,0:T(8,128)(2,1)S(1)}, u32[]{:S(2)}, u32[]{:S(2)}) async-start(bf16[8,24,1024]{2,1,0:T(8,128)(2,1)} %shard_map.190), calls=%async_computation.1 | async-start | bytes 786432 | tf_op jit(solution)/shard_map/all_to_all | solution.py:351
  51.6 17.1 %all-to-all-done.1 = bf16[8,24,1024]{2,1,0:T(8,128)(2,1)S(1)} async-done(((bf16[8,24,1024]{2,1,0:T(8,128)(2,1)}), bf16[8,24,1024]{2,1,0:T(8,128)(2,1)S(1)}, u32[]{:S(2)}, u32[]{:S(2)}) %all-to-all-start.1) | async-done | bytes 393248 | tf_op jit(solution)/shard_map/all_to_all | solution.py:351
  68.7 1.4 shard_map.191
  70.1 1.9 collective-permute-start.3
  72.1 1.9 collective-permute-done.3.other
  74.0 1.3 shard_map.192
  75.2 13.2 %collective-permute-start.4 = (bf16[24,1152]{1,0:T(8,128)(2,1)S(1)}, bf16[24,1152]{1,0:T(8,128)(2,1)S(1)}, u32[]{:S(2)}, u32[]{:S(2)}) collective-permute-start(bf16[24,1152]{1,0:T(8,128)(2,1)S(1)} %get-tuple-element.30), channel_id=1, source_target_pairs={{0,8},{8,16},{16,24},{24,0},{1,9},{9,17},{17,25},{25,1},{2,10},{10... | collective-permute-start | bytes 165896 | tf_op jit(solution)/shard_map/ppermute | solution.py:30
  88.5 1.9 collective-permute-start.5
  90.4 7.0 %collective-permute-done.5.from_right = bf16[24,1152]{1,0:T(8,128)(2,1)S(1)} collective-permute-done((bf16[24,1152]{1,0:T(8,128)(2,1)S(1)}, bf16[24,1152]{1,0:T(8,128)(2,1)S(1)}, u32[]{:S(2)}, u32[]{:S(2)}) %collective-permute-start.5) | collective-permute-done | bytes 55328 | tf_op jit(solution)/shard_map/ppermute | solution.py:30
  97.4 2.4 %collective-permute-start.6 = (bf16[24,2304]{1,0:T(8,128)(2,1)S(1)}, bf16[24,2304]{1,0:T(8,128)(2,1)S(1)}, u32[]{:S(2)}, u32[]{:S(2)}) collective-permute-start(bf16[24,2304]{1,0:T(8,128)(2,1)S(1)} %get-tuple-element.32), channel_id=1, source_target_pairs={{0,8},{8,16},{16,24},{24,0},{1,9},{9,17},{17,25},{25,1},{2,10},{10... | collective-permute-start | bytes 331784 | tf_op jit(solution)/shard_map/ppermute | solution.py:30
  99.9 6.8 %collective-permute-start.7 = (bf16[24,2304]{1,0:T(8,128)(2,1)S(1)}, bf16[24,2304]{1,0:T(8,128)(2,1)S(1)}, u32[]{:S(2)}, u32[]{:S(2)}) collective-permute-start(bf16[24,2304]{1,0:T(8,128)(2,1)S(1)} %get-tuple-element.33), channel_id=1, source_target_pairs={{0,24},{8,0},{16,8},{24,16},{1,25},{9,1},{17,9},{25,17},{2,26},{10... | collective-permute-start | bytes 331784 | tf_op jit(solution)/shard_map/ppermute | solution.py:30
  106.7 1.1 collective-permute-done.6.from_left
  107.8 1.8 collective-permute-done.7.from_right
  109.6 20.1 %all_gather.6 = bf16[96,2304]{1,0:T(8,128)(2,1)S(1)} all-gather(bf16[24,2304]{1,0:T(8,128)(2,1)S(1)} %shard_map.194), channel_id=1, replica_groups=mesh['y'=4,'x'=4,'za'=4,'zb'=4,'core'=2] {'za'}, dimensions={0}, use_global_device_ids=true | all-gather | bytes 552960 | tf_op jit(solution)/shard_map/all_gather | solution.py:384
  129.8 13.4 %all_gather.7.rows = bf16[192,2304]{1,0:T(8,128)(2,1)S(1)} all-gather(bf16[96,2304]{1,0:T(8,128)(2,1)S(1)} %all_gather.6), channel_id=1, replica_groups=mesh['y'=4,'x'=4,'za'=4,'zb'=4,'core'=2] {'core'}, dimensions={0}, use_global_device_ids=true | all-gather | bytes 1327104 | tf_op jit(solution)/shard_map/all_gather | solution.py:385
  143.2 1.1 shard_map.195
  144.2 26.3 %all_to_all.20.after.got = bf16[8,24,1024]{2,1,0:T(8,128)(2,1)S(1)} all-to-all(bf16[8,24,1024]{2,1,0:T(8,128)(2,1)S(1)} %bitcast.8), channel_id=1, replica_groups=mesh['y'=4,'x'=4,'za'=4,'zb'=4,'core'=2] {'core','za'}, dimensions={0} | all-to-all | bytes 786432 | tf_op jit(solution)/shard_map/all_to_all | solution.py:390
  171.4 4.3 %collective-permute-start.8 = (bf16[128,2304]{1,0:T(8,128)(2,1)S(1)}, bf16[128,2304]{1,0:T(8,128)(2,1)S(1)}, u32[]{:S(2)}, u32[]{:S(2)}) collective-permute-start(bf16[128,2304]{1,0:T(8,128)(2,1)S(1)} %get-tuple-element.38), channel_id=1, source_target_pairs={{0,2},{1,3},{2,4},{3,5},{4,6},{5,7},{6,8},{7,9},{8,10},{9,11},{10,... | collective-permute-start | bytes 1769480 | tf_op jit(solution)/shard_map/ppermute | solution.py:40
  175.7 7.5 %collective-permute-start.9 = (bf16[128,2304]{1,0:T(8,128)(2,1)S(1)}, bf16[128,2304]{1,0:T(8,128)(2,1)S(1)}, u32[]{:S(2)}, u32[]{:S(2)}) collective-permute-start(bf16[128,2304]{1,0:T(8,128)(2,1)S(1)} %get-tuple-element.39), channel_id=1, source_target_pairs={{0,30},{1,31},{2,0},{3,1},{4,2},{5,3},{6,4},{7,5},{8,6},{9,7},{10,... | collective-permute-start | bytes 1769480 | tf_op jit(solution)/shard_map/ppermute | solution.py:40
  183.2 3.2 %collective-permute-start.10 = (bf16[128,2304]{1,0:T(8,128)(2,1)S(1)}, bf16[128,2304]{1,0:T(8,128)(2,1)S(1)}, u32[]{:S(2)}, u32[]{:S(2)}) collective-permute-start(bf16[128,2304]{1,0:T(8,128)(2,1)S(1)} %get-tuple-element.34.rest_0_), channel_id=1, source_target_pairs={{0,4},{1,29},{2,6},{3,31},{4,8},{5,1},{6,10},{7,3},{8,12},{9,5},{1... | collective-permute-start | bytes 1769480 | tf_op jit(solution)/shard_map/ppermute | solution.py:40
  186.6 16.8 %all_to_all.21.home = bf16[16,24,512]{2,1,0:T(8,128)(2,1)S(1)} all-to-all(bf16[16,24,512]{2,1,0:T(8,128)(2,1)S(1)} %shard_map.197), channel_id=1, replica_groups=mesh['y'=4,'x'=4,'za'=4,'zb'=4,'core'=2] {'y','x'}, dimensions={0} | all-to-all | bytes 786432 | tf_op jit(solution)/shard_map/all_to_all | solution.py:417
  203.4 1.3 shard_map.198
  204.7 6.0 %collective-permute-done.10.g3 = bf16[128,2304]{1,0:T(8,128)(2,1)S(1)} collective-permute-done((bf16[128,2304]{1,0:T(8,128)(2,1)S(1)}, bf16[128,2304]{1,0:T(8,128)(2,1)S(1)}, u32[]{:S(2)}, u32[]{:S(2)}) %collective-permute-start.10) | collective-permute-done | bytes 589856 | tf_op jit(solution)/shard_map/ppermute | solution.py:40
  210.7 1.7 shard_map.199
  (29 shorter events, 2.2 us)
Async XLA Ops:
  0.6 18.5 %copy-start.6 = (s32[128,2]{0,1:T(2,128)S(1)}, s32[128,2]{0,1:T(2,128)}, u32[]{:S(2)}) copy-start(s32[128,2]{0,1:T(2,128)} %param.15) | copy-start | bytes 3076
  0.6 18.6 %copy-start.7 = (f32[128,2]{0,1:T(2,128)S(1)}, f32[128,2]{0,1:T(2,128)}, u32[]{:S(2)}) copy-start(f32[128,2]{0,1:T(2,128)} %param.16) | copy-start | bytes 3076
  0.7 18.7 %copy-start.5 = (bf16[128,256]{1,0:T(8,128)(2,1)S(1)}, bf16[128,256]{1,0:T(8,128)(2,1)}, u32[]{:S(2)}) copy-start(bf16[128,256]{1,0:T(8,128)(2,1)} %cotangent.1) | copy-start | bytes 196612
  0.7 18.7 %copy-start.4 = (bf16[128,256]{1,0:T(8,128)(2,1)S(1)}, bf16[128,256]{1,0:T(8,128)(2,1)}, u32[]{:S(2)}) copy-start(bf16[128,256]{1,0:T(8,128)(2,1)} %tokens.1) | copy-start | bytes 196612
  3.3 32.6 %collective-permute-start.2 = (bf16[128,2304]{1,0:T(8,128)(2,1)}, bf16[128,2304]{1,0:T(8,128)(2,1)S(1)}, u32[]{:S(2)}, u32[]{:S(2)}) collective-permute-start(bf16[128,2304]{1,0:T(8,128)(2,1)} %shard_map.189.w0), channel_id=1, source_target_pairs={{0,28},{1,5},{2,30},{3,7},{4,0},{5,9},{6,2},{7,11},{8,4},{9,13},{1... | collective-permute-start | bytes 1769480 | tf_op jit(solution)/shard_map/ppermute | solution.py:40
  9.0 32.7 %collective-permute-start.1 = (bf16[128,2304]{1,0:T(8,128)(2,1)}, bf16[128,2304]{1,0:T(8,128)(2,1)S(1)}, u32[]{:S(2)}, u32[]{:S(2)}) collective-permute-start(bf16[128,2304]{1,0:T(8,128)(2,1)} %shard_map.189.w0), channel_id=1, source_target_pairs={{0,2},{1,3},{2,4},{3,5},{4,6},{5,7},{6,8},{7,9},{8,10},{9,11},{10,... | collective-permute-start | bytes 1769480 | tf_op jit(solution)/shard_map/ppermute | solution.py:40
  12.6 29.1 %collective-permute-start = (bf16[128,2304]{1,0:T(8,128)(2,1)}, bf16[128,2304]{1,0:T(8,128)(2,1)S(1)}, u32[]{:S(2)}, u32[]{:S(2)}) collective-permute-start(bf16[128,2304]{1,0:T(8,128)(2,1)} %shard_map.189.w0), channel_id=1, source_target_pairs={{0,30},{1,31},{2,0},{3,1},{4,2},{5,3},{6,4},{7,5},{8,6},{9,7},{10,... | collective-permute-start | bytes 1769480 | tf_op jit(solution)/shard_map/ppermute | solution.py:40
  20.9 15.0 %all-to-all-start = ((bf16[16,24,512]{2,1,0:T(8,128)(2,1)}), bf16[16,24,512]{2,1,0:T(8,128)(2,1)S(1)}, u32[]{:S(2)}, u32[]{:S(2)}) async-start(bf16[16,24,512]{2,1,0:T(8,128)(2,1)} %shard_map.188), calls=%async_computation | async-start | bytes 786432 | tf_op jit(solution)/shard_map/all_to_all | solution.py:341
  41.7 27.0 %copy-start = (bf16[128,2304]{1,0:T(8,128)(2,1)S(1)}, bf16[128,2304]{1,0:T(8,128)(2,1)}, u32[]{:S(2)}) copy-start(bf16[128,2304]{1,0:T(8,128)(2,1)} %shard_map.189.w0) | copy-start | bytes 1769476
  42.5 26.2 %all-to-all-start.1 = ((bf16[8,24,1024]{2,1,0:T(8,128)(2,1)}), bf16[8,24,1024]{2,1,0:T(8,128)(2,1)S(1)}, u32[]{:S(2)}, u32[]{:S(2)}) async-start(bf16[8,24,1024]{2,1,0:T(8,128)(2,1)} %shard_map.190), calls=%async_computation.1 | async-start | bytes 786432 | tf_op jit(solution)/shard_map/all_to_all | solution.py:351
  70.1 3.9 %collective-permute-start.3 = (bf16[4,24,2304]{2,1,0:T(8,128)(2,1)}, bf16[4,24,2304]{2,1,0:T(8,128)(2,1)S(1)}, u32[]{:S(2)}, u32[]{:S(2)}) collective-permute-start(bf16[4,24,2304]{2,1,0:T(8,128)(2,1)} %shard_map.191), channel_id=1, source_target_pairs={{0,1},{1,0},{2,3},{3,2},{4,5},{5,4},{6,7},{7,6},{8,9},{9,8},{10,11... | collective-permute-start | bytes 1327112 | tf_op jit(solution)/shard_map/ppermute | solution.py:362
  75.2 15.2 %collective-permute-start.4 = (bf16[24,1152]{1,0:T(8,128)(2,1)S(1)}, bf16[24,1152]{1,0:T(8,128)(2,1)S(1)}, u32[]{:S(2)}, u32[]{:S(2)}) collective-permute-start(bf16[24,1152]{1,0:T(8,128)(2,1)S(1)} %get-tuple-element.30), channel_id=1, source_target_pairs={{0,8},{8,16},{16,24},{24,0},{1,9},{9,17},{17,25},{25,1},{2,10},{10... | collective-permute-start | bytes 165896 | tf_op jit(solution)/shard_map/ppermute | solution.py:30
  88.5 8.9 %collective-permute-start.5 = (bf16[24,1152]{1,0:T(8,128)(2,1)S(1)}, bf16[24,1152]{1,0:T(8,128)(2,1)S(1)}, u32[]{:S(2)}, u32[]{:S(2)}) collective-permute-start(bf16[24,1152]{1,0:T(8,128)(2,1)S(1)} %get-tuple-element.31), channel_id=1, source_target_pairs={{0,24},{8,0},{16,8},{24,16},{1,25},{9,1},{17,9},{25,17},{2,26},{10... | collective-permute-start | bytes 165896 | tf_op jit(solution)/shard_map/ppermute | solution.py:30
  97.4 10.3 %collective-permute-start.6 = (bf16[24,2304]{1,0:T(8,128)(2,1)S(1)}, bf16[24,2304]{1,0:T(8,128)(2,1)S(1)}, u32[]{:S(2)}, u32[]{:S(2)}) collective-permute-start(bf16[24,2304]{1,0:T(8,128)(2,1)S(1)} %get-tuple-element.32), channel_id=1, source_target_pairs={{0,8},{8,16},{16,24},{24,0},{1,9},{9,17},{17,25},{25,1},{2,10},{10... | collective-permute-start | bytes 331784 | tf_op jit(solution)/shard_map/ppermute | solution.py:30
  99.9 9.7 %collective-permute-start.7 = (bf16[24,2304]{1,0:T(8,128)(2,1)S(1)}, bf16[24,2304]{1,0:T(8,128)(2,1)S(1)}, u32[]{:S(2)}, u32[]{:S(2)}) collective-permute-start(bf16[24,2304]{1,0:T(8,128)(2,1)S(1)} %get-tuple-element.33), channel_id=1, source_target_pairs={{0,24},{8,0},{16,8},{24,16},{1,25},{9,1},{17,9},{25,17},{2,26},{10... | collective-permute-start | bytes 331784 | tf_op jit(solution)/shard_map/ppermute | solution.py:30
  171.4 33.3 %collective-permute-start.8 = (bf16[128,2304]{1,0:T(8,128)(2,1)S(1)}, bf16[128,2304]{1,0:T(8,128)(2,1)S(1)}, u32[]{:S(2)}, u32[]{:S(2)}) collective-permute-start(bf16[128,2304]{1,0:T(8,128)(2,1)S(1)} %get-tuple-element.38), channel_id=1, source_target_pairs={{0,2},{1,3},{2,4},{3,5},{4,6},{5,7},{6,8},{7,9},{8,10},{9,11},{10,... | collective-permute-start | bytes 1769480 | tf_op jit(solution)/shard_map/ppermute | solution.py:40
  175.7 29.0 %collective-permute-start.9 = (bf16[128,2304]{1,0:T(8,128)(2,1)S(1)}, bf16[128,2304]{1,0:T(8,128)(2,1)S(1)}, u32[]{:S(2)}, u32[]{:S(2)}) collective-permute-start(bf16[128,2304]{1,0:T(8,128)(2,1)S(1)} %get-tuple-element.39), channel_id=1, source_target_pairs={{0,30},{1,31},{2,0},{3,1},{4,2},{5,3},{6,4},{7,5},{8,6},{9,7},{10,... | collective-permute-start | bytes 1769480 | tf_op jit(solution)/shard_map/ppermute | solution.py:40
  183.2 27.5 %copy-start.1 = (bf16[1,128,768]{2,1,0:T(8,128)(2,1)S(1)}, bf16[1,128,768]{2,1,0:T(8,128)(2,1)}, u32[]{:S(2)}) copy-start(bf16[1,128,768]{2,1,0:T(8,128)(2,1)} %ng.1) | copy-start | bytes 589828
  183.2 27.5 %copy-start.2 = (bf16[1,128,768]{2,1,0:T(8,128)(2,1)S(1)}, bf16[1,128,768]{2,1,0:T(8,128)(2,1)}, u32[]{:S(2)}) copy-start(bf16[1,128,768]{2,1,0:T(8,128)(2,1)} %nu.1) | copy-start | bytes 589828
  183.2 27.5 %copy-start.3 = (bf16[1,768,128]{2,1,0:T(8,128)(2,1)S(1)}, bf16[1,768,128]{2,1,0:T(8,128)(2,1)}, u32[]{:S(2)}) copy-start(bf16[1,768,128]{2,1,0:T(8,128)(2,1)} %nd.1) | copy-start | bytes 589828
  183.2 27.4 %collective-permute-start.10 = (bf16[128,2304]{1,0:T(8,128)(2,1)S(1)}, bf16[128,2304]{1,0:T(8,128)(2,1)S(1)}, u32[]{:S(2)}, u32[]{:S(2)}) collective-permute-start(bf16[128,2304]{1,0:T(8,128)(2,1)S(1)} %get-tuple-element.34.rest_0_), channel_id=1, source_target_pairs={{0,4},{1,29},{2,6},{3,31},{4,8},{5,1},{6,10},{7,3},{8,12},{9,5},{1... | collective-permute-start | bytes 1769480 | tf_op jit(solution)/shard_map/ppermute | solution.py:40

commit v4 on v3

--- a/solution.py
+++ b/solution.py
@@ -1,3 +1,5 @@
+import itertools
+
 import jax
 import jax.numpy as jnp
 from jax import lax
@@ -10,6 +12,7 @@
 PLANE = ("y", "x")
 RING = ("za", "zb", "core")
 QUAD = 4
+NOTES = 16
 WINDOW = ((0, 1, -1, 2), (0, 1, -1, -2))
 
 
@@ -38,6 +41,27 @@
         for core in range(2)
     ]
     return lax.ppermute(value, RING, pairs)
+
+
+def to_window(value, cross, back=False):
+    sizes = [lax.axis_size(name) for name in PLANE + RING]
+    quads = sizes[3]
+
+    def index(place):
+        number = 0
+        for size, at in zip(sizes, place):
+            number = number * size + at
+        return number
+
+    pairs = []
+    for y, x, za, zb, core in itertools.product(*map(range, sizes)):
+        side = 1 - core if cross else core
+        for goal in range(QUAD):
+            for step in WINDOW[side]:
+                if (quads * goal + zb + step - quads * y - x) % (QUAD * quads) == 0:
+                    pair = (index((y, x, za, zb, core)), index((za, x, goal, zb, side)))
+                    pairs.append(pair[::-1] if back else pair)
+    return lax.ppermute(value, PLANE + RING, pairs)
 
 
 def kernel_call(kernel, outs, *operands, free=0, scalars=0, scratch=()):
@@ -60,7 +84,7 @@
 
 
 def sample_kernel(*refs):
-    sources, out, rows, columns, done = refs[:9], refs[9], refs[10], refs[11], refs[12]
+    sources, (out, rows, columns, done) = refs[:9], refs[-4:]
     places = [rows.at[i] for i in range(6)] + [columns.at[i] for i in range(3)]
     copies = [
         pltpu.make_async_copy(source.at[0], place, done.at[i])
@@ -81,49 +105,114 @@
     out[:, 2 * width :] = down.T.astype(BF)
 
 
-def pick_kernel(route, weight, tokens, cotangent, out):
-    experts, cap, feats = out.shape[0], out.shape[1], tokens.shape[1]
-    one, two = place_routes(route[...], experts, cap)
-    cot = cotangent[...].astype(F32)
-    x = contract(one + two, tokens[...], 0, 0).astype(BF)
-    d = (
-        contract(one, (weight[:, 0:1] * cot).astype(BF), 0, 0)
-        + contract(two, (weight[:, 1:2] * cot).astype(BF), 0, 0)
-    ).astype(BF)
-    for expert in range(experts):
-        rows = slice(expert * cap, (expert + 1) * cap)
-        out[expert, :, :feats] = x[rows]
-        out[expert, :, feats:] = d[rows]
-
-
-def spread_kernel(where, got, *rest):
-    out = rest[-1]
-    chips, half = got.shape[0], got.shape[2] // 4
-    for core in range(2):
-        for za in range(QUAD):
-            for at, step in enumerate(WINDOW[core]):
-                chip = lax.rem(where[0] + (4 * za + step + chips), chips)
+def pack_kernel(where, route, weight, tokens, cotangent, same, cross):
+    rows, half = tokens.shape[0], tokens.shape[1] // 2
+    experts = 2 * 2 * QUAD
+    columns = place_routes(route[...], experts)
+    for r in range(2):
+        rest = weight[:, r : r + 1]
+        for _ in range(3):
+            term = rest.astype(BF).astype(F32)
+            columns.append(term)
+            rest = rest - term
+    names = lax.broadcasted_iota(jnp.int32, (rows, rows), 1)
+    table = jnp.zeros((rows, rows), F32)
+    for at, column in enumerate(columns):
+        table = jnp.where(names == at, column, table)
+    table = table.T[:NOTES].astype(BF)
+    core = where[0]
+    for out, side in ((same, core), (cross, 1 - core)):
+        for kind, source in enumerate((tokens, cotangent)):
+            lanes = slice(kind * half, (kind + 1) * half)
+            out[:rows, lanes] = jnp.where(side == 0, source[:, :half], source[:, half:])
+            out[rows:, lanes] = table[:, :half]
+
+
+def selection(packed, slots):
+    rows = packed.shape[0] - NOTES
+    notes = packed[rows:, :rows].astype(F32)
+    names = lax.broadcasted_iota(jnp.int32, (slots, rows), 0)
+    chosen, weights = [], []
+    for r in range(2):
+        cap = slots // (4 * QUAD)
+        target = (notes[r : r + 1] * cap + notes[2 + r : 3 + r]).astype(jnp.int32)
+        chosen.append(ones_where(target == names))
+        at = 4 + 3 * r
+        weights.append((notes[at : at + 1] + notes[at + 1 : at + 2]) + notes[at + 2 : at + 3])
+    return chosen, weights
+
+
+def pick_kernel(where, same, cross, out):
+    experts, cap, half = out.shape[0], out.shape[2], out.shape[3] // 2
+    rows = same.shape[0] - NOTES
+    for packed, side in ((same, where[0]), (cross, 1 - where[0])):
+        chosen, weights = selection(packed, experts * cap)
+        both = (chosen[0] + chosen[1]).astype(BF)
+        weight = jnp.sum(
+            chosen[0] * weights[0] + chosen[1] * weights[1], axis=1, keepdims=True
+        )
+        x = contract(both, packed[:rows, :half], 1, 0)
+        d = weight * contract(both, packed[:rows, half:], 1, 0)
+        for expert in range(experts):
+            at = slice(expert * cap, (expert + 1) * cap)
+            out[expert, side, :, :half] = x[at].astype(BF)
+            out[expert, side, :, half:] = d[at].astype(BF)
+
+
+def spread_kernel(where, got, out):
+    half = got.shape[3] // 2
+    for za in range(QUAD):
+        for at, step in enumerate(WINDOW[0]):
+            chip = 4 * za + jnp.bitwise_and(where[0] + (step + 4), 3)
+            for core in range(2):
                 for kind in range(2):
                     lane = (4 * kind + at) * half
-                    here = (2 * kind + core) * half
                     out[core * QUAD + za, :, lane : lane + half] = got[
-                        chip, :, here : here + half
+                        chip, core, :, kind * half : (kind + 1) * half
                     ]
 
 
 def collect_kernel(where, got, *rest):
     out = rest[-1]
-    chips, half = out.shape[0], out.shape[2] // 4
-    for core in range(2):
-        for za in range(QUAD):
-            for at, step in enumerate(WINDOW[core]):
-                chip = lax.rem(where[0] + (4 * za + step + chips), chips)
+    half = out.shape[3] // 2
+    for za in range(QUAD):
+        for at, step in enumerate(WINDOW[0]):
+            chip = 4 * za + jnp.bitwise_and(where[0] + (step + 4), 3)
+            for core in range(2):
                 for kind in range(2):
                     lane = (4 * kind + at) * half
-                    here = (2 * kind + core) * half
-                    out[chip, :, here : here + half] = got[
+                    out[chip, core, :, kind * half : (kind + 1) * half] = got[
                         core * QUAD + za, :, lane : lane + half
                     ]
+
+
+def combine_kernel(where, same, cross, home, to_same, to_cross):
+    experts, cap, half = home.shape[0], home.shape[2], home.shape[3] // 2
+    for packed, side, out in (
+        (same, where[0], to_same),
+        (cross, 1 - where[0], to_cross),
+    ):
+        rows = out.shape[0]
+        chosen, weights = selection(packed, experts * cap)
+        columns = jnp.concatenate(weights * 4, axis=0).T
+        slots = jnp.concatenate(
+            [home[expert, side].astype(F32) for expert in range(experts)], axis=0
+        ).astype(BF)
+        one, two = chosen[0].astype(BF), chosen[1].astype(BF)
+        out[:, :half] = (
+            columns[:, 0:1] * contract(one, slots[:, :half], 0, 0)
+            + columns[:, 1:2] * contract(two, slots[:, :half], 0, 0)
+        ).astype(BF)
+        out[:, half:] = contract(one + two, slots[:, half:], 0, 0).astype(BF)
+
+
+def unpack_kernel(where, same, cross, mixed, grad):
+    half = same.shape[1] // 2
+    first = where[0] == 0
+    for kind, out in enumerate((mixed, grad)):
+        lanes = slice(kind * half, (kind + 1) * half)
+        out[:, :half] = jnp.where(first, same[:, lanes], cross[:, lanes])
+        out[:, half:] = jnp.where(first, cross[:, lanes], same[:, lanes])
 
 
 def partial_sum(slots, weights, side, rows, part):
@@ -210,8 +299,7 @@
         out[:, (4 + at) * half : (5 + at) * half] = value.astype(BF)
 
 
-def grads_kernel(slots, rows, after, g0, g1, g2, g3):
-    del after
+def grads_kernel(slots, rows, g0, g1, g2, g3):
     width, half = g0.shape[1] // 3, g0.shape[0]
     for at, g in enumerate((g0, g1, g2, g3)):
         left = slots[:, at * half : (at + 1) * half]
@@ -220,17 +308,6 @@
         left = slots[:, (4 + at) * half : (5 + at) * half]
         value = contract(left, rows[:, 2 * width :], 0, 0)
         g[:, 2 * width :] = value.astype(g.dtype)
-
-
-def combine_kernel(route, weight, home, mixed, grad):
-    experts, cap, feats = home.shape[0], home.shape[1], mixed.shape[1]
-    one, two = place_routes(route[...], experts, cap)
-    slots = jnp.concatenate([home[e].astype(F32) for e in range(experts)], axis=0).astype(BF)
-    mixed[...] = (
-        weight[:, 0:1] * contract(one, slots[:, :feats], 1, 0)
-        + weight[:, 1:2] * contract(two, slots[:, :feats], 1, 0)
-    ).astype(BF)
-    grad[...] = contract(one + two, slots[:, feats:], 1, 0).astype(BF)
 
 
 def finish_kernel(g0, g1, g2, g3, ng, nu, nd, mg, sg, mu, su, md, sd):
@@ -257,7 +334,7 @@
     return jnp.where(condition, 1.0, 0.0).astype(F32)
 
 
-def place_routes(route, experts, capacity):
+def place_routes(route, experts):
     rows = route.shape[0]
     names = lax.broadcasted_iota(jnp.int32, (rows, experts), 1)
     first = ones_where(route[:, 0:1] == names)
@@ -267,12 +344,12 @@
         > lax.broadcasted_iota(jnp.int32, (rows, rows), 1)
     ).astype(BF)
     earlier = contract(below, (first + second).astype(BF), 1, 0)
-    place_first = jnp.sum(earlier * first, axis=1, keepdims=True).astype(jnp.int32)
-    place_second = jnp.sum((earlier + first) * second, axis=1, keepdims=True).astype(jnp.int32)
-    slots = lax.broadcasted_iota(jnp.int32, (rows, experts * capacity), 1)
-    one = ones_where(route[:, 0:1] * capacity + place_first == slots).astype(BF)
-    two = ones_where(route[:, 1:2] * capacity + place_second == slots).astype(BF)
-    return one, two
+    return [
+        route[:, 0:1].astype(F32),
+        route[:, 1:2].astype(F32),
+        jnp.sum(earlier * first, axis=1, keepdims=True),
+        jnp.sum((earlier + first) * second, axis=1, keepdims=True),
+    ]
 
 
 def body(
@@ -301,10 +378,23 @@
     zb = lax.axis_index("zb").astype(jnp.int32).reshape(1)
     core = lax.axis_index("core").astype(jnp.int32).reshape(1)
 
+    packed = kernel_call(
+        pack_kernel,
+        [jax.ShapeDtypeStruct((group_rows + NOTES, 2 * half), BF)] * 2,
+        core,
+        route,
+        route_weight,
+        tokens,
+        cotangent,
+        scalars=1,
+    )
+    same = to_window(packed[0], False)
+    cross = to_window(packed[1], True)
     w_own = pl.pallas_call(
         sample_kernel,
         out_shape=jax.ShapeDtypeStruct((half, 3 * width), BF),
-        in_specs=[pl.BlockSpec(memory_space=pltpu.HBM)] * 9,
+        in_specs=[pl.BlockSpec(memory_space=pltpu.HBM)] * 9
+        + [pl.BlockSpec(memory_space=pl.ANY)] * 2,
         out_specs=pl.BlockSpec(memory_space=pltpu.VMEM),
         scratch_shapes=[
             pltpu.VMEM((6, half, width), BF),
@@ -322,6 +412,8 @@
         mean_down,
         spread_down,
         noise_down,
+        same,
+        cross,
     )
     weights = (
         w_own,
@@ -332,11 +424,11 @@
 
     (send,) = kernel_call(
         pick_kernel,
-        [jax.ShapeDtypeStruct((experts, cap, 2 * feats), BF)],
-        route,
-        route_weight,
-        tokens,
-        cotangent,
+        [jax.ShapeDtypeStruct((experts, 2, cap, 2 * half), BF)],
+        core,
+        same,
+        cross,
+        scalars=1,
     )
     got = lax.all_to_all(send, PLANE, split_axis=0, concat_axis=0, tiled=True)
     (got,) = kernel_call(
@@ -344,11 +436,8 @@
         [jax.ShapeDtypeStruct((2 * QUAD, cap, 8 * half), BF)],
         zb,
         got,
-        *weights[1:],
-        scalars=1,
-        free=3,
-    )
-    got = lax.all_to_all(got, ("core", "za"), split_axis=0, concat_axis=0, tiled=True)
+        scalars=1,
+    )
     slots = got.reshape(rows_all, 8 * half)
 
     (other,) = kernel_call(
@@ -387,16 +476,12 @@
         outs_kernel, [jax.ShapeDtypeStruct((rows_all, 8 * half), BF)], rows, *weights
     )
     outs = outs.reshape(2 * QUAD, cap, 8 * half)
-    home = lax.all_to_all(outs, ("core", "za"), split_axis=0, concat_axis=0, tiled=True)
-
     w_sent = kernel_call(
         grads_kernel,
         [jax.ShapeDtypeStruct((half, 3 * width), F32)]
         + [jax.ShapeDtypeStruct((half, 3 * width), BF)] * 3,
         slots,
         rows,
-        home,
-        free=1,
     )
     w_grads = (
         w_sent[0],
@@ -407,20 +492,30 @@
 
     (home,) = kernel_call(
         collect_kernel,
-        [jax.ShapeDtypeStruct((experts, cap, 2 * feats), BF)],
+        [jax.ShapeDtypeStruct((experts, 2, cap, 2 * half), BF)],
         zb,
+        outs,
+        w_sent[3],
+        scalars=1,
+        free=1,
+    )
+    home = lax.all_to_all(home, PLANE, split_axis=0, concat_axis=0, tiled=True)
+    ready = kernel_call(
+        combine_kernel,
+        [jax.ShapeDtypeStruct((group_rows, 2 * half), BF)] * 2,
+        core,
+        same,
+        cross,
         home,
-        w_sent[3],
-        scalars=1,
-        free=1,
-    )
-    home = lax.all_to_all(home, PLANE, split_axis=0, concat_axis=0, tiled=True)
+        scalars=1,
+    )
     mixed_out, token_grad = kernel_call(
-        combine_kernel,
+        unpack_kernel,
         [jax.ShapeDtypeStruct((group_rows, feats), BF)] * 2,
-        route,
-        route_weight,
-        home,
+        core,
+        to_window(ready[0], False, True),
+        to_window(ready[1], True, True),
+        scalars=1,
     )
     by_row = jax.ShapeDtypeStruct((1, half, width), F32)
     by_column = jax.ShapeDtypeStruct((1, width, half), F32)

time: 213 us -> 199 us (0.934)
  the two profiles are of different devices: /device:TPU:1 before, /device:TPU:48 now
where the time goes in v4:
time: 199 us; the launch traced here: 198 us
  starting transfers between devices  88 us (44%)
  waiting for transfers between devices  49.6 us (25%)
  blocking collectives  42.2 us (21%)
  Pallas kernels  11.6 us (6%)
  local copies, waits for them, and re-layouts  5.68 us (3%)
    ppermute x4, starting transfers between devices, to_window(): return lax.ppermute(value, PLANE + RING, pairs)  32.3 us
    ppermute x4, waiting for transfers between devices, to_window(): return lax.ppermute(value, PLANE + RING, pairs)  25.9 us
    ppermute x6, starting transfers between devices, along_ring(): return lax.ppermute(value, RING, pairs)  24.1 us
    all_gather x1, blocking collectives, body(): rows = lax.all_gather(rows, 'za', axis=0, tiled=True)  21.5 us
    ppermute x4, starting transfers between devices, shift(): lax.ppermute(value, 'za', [(i, (i + step) % QUAD) for i in range(QUAD)])  19.5 us
    all_to_all x1, blocking collectives, body(): home = lax.all_to_all(home, PLANE, split_axis=0, concat_axis=0, tiled=True)  18.3 us
    ppermute x4, waiting for transfers between devices, shift(): lax.ppermute(value, 'za', [(i, (i + step) % QUAD) for i in range(QUAD)])  11.7 us
    all_to_all x1, starting transfers between devices, body(): got = lax.all_to_all(send, PLANE, split_axis=0, concat_axis=0, tiled=True)  10.1 us
  transfers between devices with their start and end apart: 16, of which 11 were waited for; matrix products, arithmetic and copies ran while one was open for 0% of the time, Pallas kernels for 2%

profile of v4, /device:TPU:48, one launch (start us, length us, event | category | flops | bytes accessed | tf_op | source)
XLA Modules:
  0.0 198.0 jit_solution(10794444564837784999)
XLA Ops:
  4.3 14.6 %collective-permute-start = (bf16[144,256]{1,0:T(8,128)(2,1)S(1)}, bf16[144,256]{1,0:T(8,128)(2,1)S(1)}, u32[]{:S(2)}, u32[]{:S(2)}) collective-permute-start(bf16[144,256]{1,0:T(8,128)(2,1)S(1)} %get-tuple-element.31), channel_id=1, source_target_pairs={{0,0},{1,1},{2,2},{3,3},{4,28},{5,5},{6,30},{7,31},{8,128},{9,129}... | collective-permute-start | bytes 221192 | tf_op jit(solution)/shard_map/ppermute | solution.py:64
  18.9 1.9 collective-permute-start.1
  21.7 14.6 %collective-permute-done.1.cross.refs_10_ = bf16[144,256]{1,0:T(8,128)(2,1)S(1)} collective-permute-done((bf16[144,256]{1,0:T(8,128)(2,1)S(1)}, bf16[144,256]{1,0:T(8,128)(2,1)S(1)}, u32[]{:S(2)}, u32[]{:S(2)}) %collective-permute-start.1) | collective-permute-done | bytes 73760 | tf_op jit(solution)/shard_map/ppermute | solution.py:64
  36.9 2.5 %shard_map.191.w0 = bf16[128,2304]{1,0:T(8,128)(2,1)} custom-call(bf16[1,128,768]{2,1,0:T(8,128)(2,1)} %refs_0_.1, bf16[1,128,768]{2,1,0:T(8,128)(2,1)} %refs_1_.1, bf16[1,128,768]{2,1,0:T(8,128)(2,1)} %ng.1, bf16[1,128,768]{2,1,0:T(8,128)(2,1)} %refs_3_.1, bf16[1,128,768]{2,1,0:T(8,128)(2,1)} %refs_4_.1, bf16[1,128,768]{2,1,0:T(8,128)(2,1)} %nu.1, ...), custom_call_target="tpu_custom_call" | custom-call | tf_op jit(solution)/shard_map/pallas_call | solution.py:393
  39.5 2.1 %collective-permute-start.4 = (bf16[128,2304]{1,0:T(8,128)(2,1)}, bf16[128,2304]{1,0:T(8,128)(2,1)S(1)}, u32[]{:S(2)}, u32[]{:S(2)}) collective-permute-start(bf16[128,2304]{1,0:T(8,128)(2,1)} %shard_map.191.w0), channel_id=1, source_target_pairs={{0,28},{1,5},{2,30},{3,7},{4,0},{5,9},{6,2},{7,11},{8,4},{9,13},{1... | collective-permute-start | bytes 1769480 | tf_op jit(solution)/shard_map/ppermute | solution.py:43
  41.6 4.3 %collective-permute-start.3 = (bf16[128,2304]{1,0:T(8,128)(2,1)}, bf16[128,2304]{1,0:T(8,128)(2,1)S(1)}, u32[]{:S(2)}, u32[]{:S(2)}) collective-permute-start(bf16[128,2304]{1,0:T(8,128)(2,1)} %shard_map.191.w0), channel_id=1, source_target_pairs={{0,2},{1,3},{2,4},{3,5},{4,6},{5,7},{6,8},{7,9},{8,10},{9,11},{10,... | collective-permute-start | bytes 1769480 | tf_op jit(solution)/shard_map/ppermute | solution.py:43
  45.8 1.9 collective-permute-start.2
  50.5 10.1 %all-to-all-start = ((bf16[16,2,24,256]{3,2,1,0:T(8,128)(2,1)}), bf16[16,2,24,256]{3,2,1,0:T(8,128)(2,1)S(1)}, u32[]{:S(2)}, u32[]{:S(2)}) async-start(bf16[16,2,24,256]{3,2,1,0:T(8,128)(2,1)} %shard_map.189), calls=%async_computation | async-start | bytes 786432 | tf_op jit(solution)/shard_map/all_to_all | solution.py:433
  60.7 6.8 %all-to-all-done.got = bf16[16,2,24,256]{3,2,1,0:T(8,128)(2,1)S(1)} async-done(((bf16[16,2,24,256]{3,2,1,0:T(8,128)(2,1)}), bf16[16,2,24,256]{3,2,1,0:T(8,128)(2,1)S(1)}, u32[]{:S(2)}, u32[]{:S(2)}) %all-to-all-start) | async-done | bytes 393248 | tf_op jit(solution)/shard_map/all_to_all | solution.py:433
  67.6 3.3 %collective-permute-done.2.w1 = bf16[128,2304]{1,0:T(8,128)(2,1)S(1)} collective-permute-done((bf16[128,2304]{1,0:T(8,128)(2,1)}, bf16[128,2304]{1,0:T(8,128)(2,1)S(1)}, u32[]{:S(2)}, u32[]{:S(2)}) %collective-permute-start.2) | collective-permute-done | bytes 589856 | tf_op jit(solution)/shard_map/ppermute | solution.py:43
  70.9 1.4 shard_map.192
  72.3 1.9 collective-permute-start.5
  74.3 1.9 collective-permute-done.5.other
  77.5 1.9 collective-permute-start.6
  79.4 7.8 %collective-permute-start.7 = (bf16[24,1152]{1,0:T(8,128)(2,1)S(1)}, bf16[24,1152]{1,0:T(8,128)(2,1)S(1)}, u32[]{:S(2)}, u32[]{:S(2)}) collective-permute-start(bf16[24,1152]{1,0:T(8,128)(2,1)S(1)} %get-tuple-element.37), channel_id=1, source_target_pairs={{0,24},{8,0},{16,8},{24,16},{1,25},{9,1},{17,9},{25,17},{2,26},{10... | collective-permute-start | bytes 165896 | tf_op jit(solution)/shard_map/ppermute | solution.py:33
  87.2 1.7 collective-permute-done.6.from_left
  89.0 2.0 collective-permute-done.7.from_right
  91.0 2.9 %collective-permute-start.8 = (bf16[24,2304]{1,0:T(8,128)(2,1)S(1)}, bf16[24,2304]{1,0:T(8,128)(2,1)S(1)}, u32[]{:S(2)}, u32[]{:S(2)}) collective-permute-start(bf16[24,2304]{1,0:T(8,128)(2,1)S(1)} %get-tuple-element.38), channel_id=1, source_target_pairs={{0,8},{8,16},{16,24},{24,0},{1,9},{9,17},{17,25},{25,1},{2,10},{10... | collective-permute-start | bytes 331784 | tf_op jit(solution)/shard_map/ppermute | solution.py:33
  93.9 6.9 %collective-permute-start.9 = (bf16[24,2304]{1,0:T(8,128)(2,1)S(1)}, bf16[24,2304]{1,0:T(8,128)(2,1)S(1)}, u32[]{:S(2)}, u32[]{:S(2)}) collective-permute-start(bf16[24,2304]{1,0:T(8,128)(2,1)S(1)} %get-tuple-element.39), channel_id=1, source_target_pairs={{0,24},{8,0},{16,8},{24,16},{1,25},{9,1},{17,9},{25,17},{2,26},{10... | collective-permute-start | bytes 331784 | tf_op jit(solution)/shard_map/ppermute | solution.py:33
  100.7 3.4 %collective-permute-done.8.from_left = bf16[24,2304]{1,0:T(8,128)(2,1)S(1)} collective-permute-done((bf16[24,2304]{1,0:T(8,128)(2,1)S(1)}, bf16[24,2304]{1,0:T(8,128)(2,1)S(1)}, u32[]{:S(2)}, u32[]{:S(2)}) %collective-permute-start.8) | collective-permute-done | bytes 110624 | tf_op jit(solution)/shard_map/ppermute | solution.py:33
  104.2 4.5 %collective-permute-done.9.from_right = bf16[24,2304]{1,0:T(8,128)(2,1)S(1)} collective-permute-done((bf16[24,2304]{1,0:T(8,128)(2,1)S(1)}, bf16[24,2304]{1,0:T(8,128)(2,1)S(1)}, u32[]{:S(2)}, u32[]{:S(2)}) %collective-permute-start.9) | collective-permute-done | bytes 110624 | tf_op jit(solution)/shard_map/ppermute | solution.py:33
  108.8 21.5 %all_gather.6 = bf16[96,2304]{1,0:T(8,128)(2,1)S(1)} all-gather(bf16[24,2304]{1,0:T(8,128)(2,1)S(1)} %shard_map.195), channel_id=1, replica_groups=mesh['y'=4,'x'=4,'za'=4,'zb'=4,'core'=2] {'za'}, dimensions={0}, use_global_device_ids=true | all-gather | bytes 552960 | tf_op jit(solution)/shard_map/all_gather | solution.py:473
  130.3 2.4 %all_gather.7.rows = bf16[192,2304]{1,0:T(8,128)(2,1)S(1)} all-gather(bf16[96,2304]{1,0:T(8,128)(2,1)S(1)} %all_gather.6), channel_id=1, replica_groups=mesh['y'=4,'x'=4,'za'=4,'zb'=4,'core'=2] {'core'}, dimensions={0}, use_global_device_ids=true | all-gather | bytes 1327104 | tf_op jit(solution)/shard_map/all_gather | solution.py:474
  133.5 6.0 %collective-permute-start.12 = (bf16[128,2304]{1,0:T(8,128)(2,1)S(1)}, bf16[128,2304]{1,0:T(8,128)(2,1)S(1)}, u32[]{:S(2)}, u32[]{:S(2)}) collective-permute-start(bf16[128,2304]{1,0:T(8,128)(2,1)S(1)} %get-tuple-element.46), channel_id=1, source_target_pairs={{0,2},{1,3},{2,4},{3,5},{4,6},{5,7},{6,8},{7,9},{8,10},{9,11},{10,... | collective-permute-start | bytes 1769480 | tf_op jit(solution)/shard_map/ppermute | solution.py:43
  139.5 3.9 %collective-permute-start.13 = (bf16[128,2304]{1,0:T(8,128)(2,1)S(1)}, bf16[128,2304]{1,0:T(8,128)(2,1)S(1)}, u32[]{:S(2)}, u32[]{:S(2)}) collective-permute-start(bf16[128,2304]{1,0:T(8,128)(2,1)S(1)} %get-tuple-element.47), channel_id=1, source_target_pairs={{0,30},{1,31},{2,0},{3,1},{4,2},{5,3},{6,4},{7,5},{8,6},{9,7},{10,... | collective-permute-start | bytes 1769480 | tf_op jit(solution)/shard_map/ppermute | solution.py:43
  143.4 6.1 %collective-permute-start.14 = (bf16[128,2304]{1,0:T(8,128)(2,1)S(1)}, bf16[128,2304]{1,0:T(8,128)(2,1)S(1)}, u32[]{:S(2)}, u32[]{:S(2)}) collective-permute-start(bf16[128,2304]{1,0:T(8,128)(2,1)S(1)} %get-tuple-element.40.rest_0_), channel_id=1, source_target_pairs={{0,4},{1,29},{2,6},{3,31},{4,8},{5,1},{6,10},{7,3},{8,12},{9,5},{1... | collective-permute-start | bytes 1769480 | tf_op jit(solution)/shard_map/ppermute | solution.py:43
  150.7 18.3 %all_to_all.10.home = bf16[16,2,24,256]{3,2,1,0:T(8,128)(2,1)S(1)} all-to-all(bf16[16,2,24,256]{3,2,1,0:T(8,128)(2,1)S(1)} %shard_map.198), channel_id=1, replica_groups=mesh['y'=4,'x'=4,'za'=4,'zb'=4,'core'=2] {'y','x'}, dimensions={0} | all-to-all | bytes 786432 | tf_op jit(solution)/shard_map/all_to_all | solution.py:502
  169.4 9.4 %collective-permute-start.10 = (bf16[128,256]{1,0:T(8,128)(2,1)S(1)}, bf16[128,256]{1,0:T(8,128)(2,1)S(1)}, u32[]{:S(2)}, u32[]{:S(2)}) collective-permute-start(bf16[128,256]{1,0:T(8,128)(2,1)S(1)} %get-tuple-element.41), channel_id=1, source_target_pairs={{0,0},{1,1},{2,2},{3,3},{28,4},{5,5},{30,6},{31,7},{128,8},{129,9}... | collective-permute-start | bytes 196616 | tf_op jit(solution)/shard_map/ppermute | solution.py:64
  178.8 6.4 %collective-permute-start.11 = (bf16[128,256]{1,0:T(8,128)(2,1)S(1)}, bf16[128,256]{1,0:T(8,128)(2,1)S(1)}, u32[]{:S(2)}, u32[]{:S(2)}) collective-permute-start(bf16[128,256]{1,0:T(8,128)(2,1)S(1)} %get-tuple-element.42), channel_id=1, source_target_pairs={{1,0},{0,1},{3,2},{2,3},{5,4},{28,5},{31,6},{30,7},{129,8},{128,9}... | collective-permute-start | bytes 196616 | tf_op jit(solution)/shard_map/ppermute | solution.py:64
  185.2 2.4 %collective-permute-done.10.same = bf16[128,256]{1,0:T(8,128)(2,1)S(1)} collective-permute-done((bf16[128,256]{1,0:T(8,128)(2,1)S(1)}, bf16[128,256]{1,0:T(8,128)(2,1)S(1)}, u32[]{:S(2)}, u32[]{:S(2)}) %collective-permute-start.10) | collective-permute-done | bytes 65568 | tf_op jit(solution)/shard_map/ppermute | solution.py:64
  187.6 8.0 %collective-permute-done.11.cross = bf16[128,256]{1,0:T(8,128)(2,1)S(1)} collective-permute-done((bf16[128,256]{1,0:T(8,128)(2,1)S(1)}, bf16[128,256]{1,0:T(8,128)(2,1)S(1)}, u32[]{:S(2)}, u32[]{:S(2)}) %collective-permute-start.11) | collective-permute-done | bytes 65568 | tf_op jit(solution)/shard_map/ppermute | solution.py:64
  196.3 1.7 shard_map.201
  (44 shorter events, 12.6 us)
Async XLA Ops:
  2.2 0.8 copy-start.10
  3.0 0.8 copy-start.11
  4.3 17.4 %collective-permute-start = (bf16[144,256]{1,0:T(8,128)(2,1)S(1)}, bf16[144,256]{1,0:T(8,128)(2,1)S(1)}, u32[]{:S(2)}, u32[]{:S(2)}) collective-permute-start(bf16[144,256]{1,0:T(8,128)(2,1)S(1)} %get-tuple-element.31), channel_id=1, source_target_pairs={{0,0},{1,1},{2,2},{3,3},{4,28},{5,5},{6,30},{7,31},{8,128},{9,129}... | collective-permute-start | bytes 221192 | tf_op jit(solution)/shard_map/ppermute | solution.py:64
  18.9 17.4 %collective-permute-start.1 = (bf16[144,256]{1,0:T(8,128)(2,1)S(1)}, bf16[144,256]{1,0:T(8,128)(2,1)S(1)}, u32[]{:S(2)}, u32[]{:S(2)}) collective-permute-start(bf16[144,256]{1,0:T(8,128)(2,1)S(1)} %get-tuple-element.32), channel_id=1, source_target_pairs={{0,1},{1,0},{2,3},{3,2},{4,5},{5,28},{6,31},{7,30},{8,129},{9,128}... | collective-permute-start | bytes 221192 | tf_op jit(solution)/shard_map/ppermute | solution.py:64
  21.7 14.6 %copy-start.4 = (bf16[144,256]{1,0:T(8,128)(2,1)}, bf16[144,256]{1,0:T(8,128)(2,1)S(1)}, u32[]{:S(2)}) copy-start(bf16[144,256]{1,0:T(8,128)(2,1)S(1)} %collective-permute-done.same.refs_9_) | copy-start | bytes 221188
  36.3 0.6 copy-start.7
  39.5 31.4 %copy-start = (bf16[128,2304]{1,0:T(8,128)(2,1)S(1)}, bf16[128,2304]{1,0:T(8,128)(2,1)}, u32[]{:S(2)}) copy-start(bf16[128,2304]{1,0:T(8,128)(2,1)} %shard_map.191.w0) | copy-start | bytes 1769476
  39.5 28.1 %collective-permute-start.4 = (bf16[128,2304]{1,0:T(8,128)(2,1)}, bf16[128,2304]{1,0:T(8,128)(2,1)S(1)}, u32[]{:S(2)}, u32[]{:S(2)}) collective-permute-start(bf16[128,2304]{1,0:T(8,128)(2,1)} %shard_map.191.w0), channel_id=1, source_target_pairs={{0,28},{1,5},{2,30},{3,7},{4,0},{5,9},{6,2},{7,11},{8,4},{9,13},{1... | collective-permute-start | bytes 1769480 | tf_op jit(solution)/shard_map/ppermute | solution.py:43
  41.6 26.0 %collective-permute-start.3 = (bf16[128,2304]{1,0:T(8,128)(2,1)}, bf16[128,2304]{1,0:T(8,128)(2,1)S(1)}, u32[]{:S(2)}, u32[]{:S(2)}) collective-permute-start(bf16[128,2304]{1,0:T(8,128)(2,1)} %shard_map.191.w0), channel_id=1, source_target_pairs={{0,2},{1,3},{2,4},{3,5},{4,6},{5,7},{6,8},{7,9},{8,10},{9,11},{10,... | collective-permute-start | bytes 1769480 | tf_op jit(solution)/shard_map/ppermute | solution.py:43
  45.8 25.1 %collective-permute-start.2 = (bf16[128,2304]{1,0:T(8,128)(2,1)}, bf16[128,2304]{1,0:T(8,128)(2,1)S(1)}, u32[]{:S(2)}, u32[]{:S(2)}) collective-permute-start(bf16[128,2304]{1,0:T(8,128)(2,1)} %shard_map.191.w0), channel_id=1, source_target_pairs={{0,30},{1,31},{2,0},{3,1},{4,2},{5,3},{6,4},{7,5},{8,6},{9,7},{10,... | collective-permute-start | bytes 1769480 | tf_op jit(solution)/shard_map/ppermute | solution.py:43
  47.8 0.9 copy-start.5
  48.6 0.9 copy-start.8
  50.5 16.9 %all-to-all-start = ((bf16[16,2,24,256]{3,2,1,0:T(8,128)(2,1)}), bf16[16,2,24,256]{3,2,1,0:T(8,128)(2,1)S(1)}, u32[]{:S(2)}, u32[]{:S(2)}) async-start(bf16[16,2,24,256]{3,2,1,0:T(8,128)(2,1)} %shard_map.189), calls=%async_computation | async-start | bytes 786432 | tf_op jit(solution)/shard_map/all_to_all | solution.py:433
  72.3 3.9 %collective-permute-start.5 = (bf16[4,24,2304]{2,1,0:T(8,128)(2,1)}, bf16[4,24,2304]{2,1,0:T(8,128)(2,1)S(1)}, u32[]{:S(2)}, u32[]{:S(2)}) collective-permute-start(bf16[4,24,2304]{2,1,0:T(8,128)(2,1)} %shard_map.192), channel_id=1, source_target_pairs={{0,1},{1,0},{2,3},{3,2},{4,5},{5,4},{6,7},{7,6},{8,9},{9,8},{10,11... | collective-permute-start | bytes 1327112 | tf_op jit(solution)/shard_map/ppermute | solution.py:451
  77.5 11.5 %collective-permute-start.6 = (bf16[24,1152]{1,0:T(8,128)(2,1)S(1)}, bf16[24,1152]{1,0:T(8,128)(2,1)S(1)}, u32[]{:S(2)}, u32[]{:S(2)}) collective-permute-start(bf16[24,1152]{1,0:T(8,128)(2,1)S(1)} %get-tuple-element.36), channel_id=1, source_target_pairs={{0,8},{8,16},{16,24},{24,0},{1,9},{9,17},{17,25},{25,1},{2,10},{10... | collective-permute-start | bytes 165896 | tf_op jit(solution)/shard_map/ppermute | solution.py:33
  79.4 11.5 %collective-permute-start.7 = (bf16[24,1152]{1,0:T(8,128)(2,1)S(1)}, bf16[24,1152]{1,0:T(8,128)(2,1)S(1)}, u32[]{:S(2)}, u32[]{:S(2)}) collective-permute-start(bf16[24,1152]{1,0:T(8,128)(2,1)S(1)} %get-tuple-element.37), channel_id=1, source_target_pairs={{0,24},{8,0},{16,8},{24,16},{1,25},{9,1},{17,9},{25,17},{2,26},{10... | collective-permute-start | bytes 165896 | tf_op jit(solution)/shard_map/ppermute | solution.py:33
  91.0 13.2 %collective-permute-start.8 = (bf16[24,2304]{1,0:T(8,128)(2,1)S(1)}, bf16[24,2304]{1,0:T(8,128)(2,1)S(1)}, u32[]{:S(2)}, u32[]{:S(2)}) collective-permute-start(bf16[24,2304]{1,0:T(8,128)(2,1)S(1)} %get-tuple-element.38), channel_id=1, source_target_pairs={{0,8},{8,16},{16,24},{24,0},{1,9},{9,17},{17,25},{25,1},{2,10},{10... | collective-permute-start | bytes 331784 | tf_op jit(solution)/shard_map/ppermute | solution.py:33
  93.9 14.8 %collective-permute-start.9 = (bf16[24,2304]{1,0:T(8,128)(2,1)S(1)}, bf16[24,2304]{1,0:T(8,128)(2,1)S(1)}, u32[]{:S(2)}, u32[]{:S(2)}) collective-permute-start(bf16[24,2304]{1,0:T(8,128)(2,1)S(1)} %get-tuple-element.39), channel_id=1, source_target_pairs={{0,24},{8,0},{16,8},{24,16},{1,25},{9,1},{17,9},{25,17},{2,26},{10... | collective-permute-start | bytes 331784 | tf_op jit(solution)/shard_map/ppermute | solution.py:33
  133.5 62.8 %collective-permute-start.12 = (bf16[128,2304]{1,0:T(8,128)(2,1)S(1)}, bf16[128,2304]{1,0:T(8,128)(2,1)S(1)}, u32[]{:S(2)}, u32[]{:S(2)}) collective-permute-start(bf16[128,2304]{1,0:T(8,128)(2,1)S(1)} %get-tuple-element.46), channel_id=1, source_target_pairs={{0,2},{1,3},{2,4},{3,5},{4,6},{5,7},{6,8},{7,9},{8,10},{9,11},{10,... | collective-permute-start | bytes 1769480 | tf_op jit(solution)/shard_map/ppermute | solution.py:43
  139.5 56.8 %collective-permute-start.13 = (bf16[128,2304]{1,0:T(8,128)(2,1)S(1)}, bf16[128,2304]{1,0:T(8,128)(2,1)S(1)}, u32[]{:S(2)}, u32[]{:S(2)}) collective-permute-start(bf16[128,2304]{1,0:T(8,128)(2,1)S(1)} %get-tuple-element.47), channel_id=1, source_target_pairs={{0,30},{1,31},{2,0},{3,1},{4,2},{5,3},{6,4},{7,5},{8,6},{9,7},{10,... | collective-permute-start | bytes 1769480 | tf_op jit(solution)/shard_map/ppermute | solution.py:43
  143.4 52.9 %collective-permute-start.14 = (bf16[128,2304]{1,0:T(8,128)(2,1)S(1)}, bf16[128,2304]{1,0:T(8,128)(2,1)S(1)}, u32[]{:S(2)}, u32[]{:S(2)}) collective-permute-start(bf16[128,2304]{1,0:T(8,128)(2,1)S(1)} %get-tuple-element.40.rest_0_), channel_id=1, source_target_pairs={{0,4},{1,29},{2,6},{3,31},{4,8},{5,1},{6,10},{7,3},{8,12},{9,5},{1... | collective-permute-start | bytes 1769480 | tf_op jit(solution)/shard_map/ppermute | solution.py:43
  150.5 18.4 %copy-start.6 = (bf16[144,256]{1,0:T(8,128)(2,1)S(1)}, bf16[144,256]{1,0:T(8,128)(2,1)}, u32[]{:S(2)}) copy-start(bf16[144,256]{1,0:T(8,128)(2,1)} %copy-done.4) | copy-start | bytes 221188
  150.5 18.4 %copy-start.9 = (bf16[144,256]{1,0:T(8,128)(2,1)S(1)}, bf16[144,256]{1,0:T(8,128)(2,1)}, u32[]{:S(2)}) copy-start(bf16[144,256]{1,0:T(8,128)(2,1)} %copy-done.7) | copy-start | bytes 221188
  150.5 45.8 %copy-start.1 = (bf16[1,128,768]{2,1,0:T(8,128)(2,1)S(1)}, bf16[1,128,768]{2,1,0:T(8,128)(2,1)}, u32[]{:S(2)}) copy-start(bf16[1,128,768]{2,1,0:T(8,128)(2,1)} %ng.1) | copy-start | bytes 589828
  150.6 45.8 %copy-start.2 = (bf16[1,128,768]{2,1,0:T(8,128)(2,1)S(1)}, bf16[1,128,768]{2,1,0:T(8,128)(2,1)}, u32[]{:S(2)}) copy-start(bf16[1,128,768]{2,1,0:T(8,128)(2,1)} %nu.1) | copy-start | bytes 589828
  150.6 45.7 %copy-start.3 = (bf16[1,768,128]{2,1,0:T(8,128)(2,1)S(1)}, bf16[1,768,128]{2,1,0:T(8,128)(2,1)}, u32[]{:S(2)}) copy-start(bf16[1,768,128]{2,1,0:T(8,128)(2,1)} %nd.1) | copy-start | bytes 589828
  169.4 18.1 %collective-permute-start.10 = (bf16[128,256]{1,0:T(8,128)(2,1)S(1)}, bf16[128,256]{1,0:T(8,128)(2,1)S(1)}, u32[]{:S(2)}, u32[]{:S(2)}) collective-permute-start(bf16[128,256]{1,0:T(8,128)(2,1)S(1)} %get-tuple-element.41), channel_id=1, source_target_pairs={{0,0},{1,1},{2,2},{3,3},{28,4},{5,5},{30,6},{31,7},{128,8},{129,9}... | collective-permute-start | bytes 196616 | tf_op jit(solution)/shard_map/ppermute | solution.py:64
  178.8 16.8 %collective-permute-start.11 = (bf16[128,256]{1,0:T(8,128)(2,1)S(1)}, bf16[128,256]{1,0:T(8,128)(2,1)S(1)}, u32[]{:S(2)}, u32[]{:S(2)}) collective-permute-start(bf16[128,256]{1,0:T(8,128)(2,1)S(1)} %get-tuple-element.42), channel_id=1, source_target_pairs={{1,0},{0,1},{3,2},{2,3},{5,4},{28,5},{31,6},{30,7},{129,8},{128,9}... | collective-permute-start | bytes 196616 | tf_op jit(solution)/shard_map/ppermute | solution.py:64

commit v5 on v4

--- a/solution.py
+++ b/solution.py
@@ -59,7 +59,10 @@
         for goal in range(QUAD):
             for step in WINDOW[side]:
                 if (quads * goal + zb + step - quads * y - x) % (QUAD * quads) == 0:
-                    pair = (index((y, x, za, zb, core)), index((za, x, goal, zb, side)))
+                    pair = (
+                        index((y, x, za, zb, core)),
+                        index(((za + goal) % QUAD, x, goal, zb, side)),
+                    )
                     pairs.append(pair[::-1] if back else pair)
     return lax.ppermute(value, PLANE + RING, pairs)
 
@@ -105,21 +108,27 @@
     out[:, 2 * width :] = down.T.astype(BF)
 
 
-def pack_kernel(where, route, weight, tokens, cotangent, same, cross):
+def pack_kernel(where, *refs):
+    sources, (same, cross), places, done = refs[:4], refs[4:6], refs[6:10], refs[10]
+    copies = [
+        pltpu.make_async_copy(source, place, done.at[i])
+        for i, (source, place) in enumerate(zip(sources, places))
+    ]
+    for copy in copies:
+        copy.start()
+    for copy in copies:
+        copy.wait()
+    route, weight, tokens, cotangent = places
     rows, half = tokens.shape[0], tokens.shape[1] // 2
-    experts = 2 * 2 * QUAD
-    columns = place_routes(route[...], experts)
+    notes = place_routes(route[...], 4 * QUAD)
     for r in range(2):
-        rest = weight[:, r : r + 1]
+        rest = weight[r : r + 1]
         for _ in range(3):
             term = rest.astype(BF).astype(F32)
-            columns.append(term)
+            notes.append(term)
             rest = rest - term
-    names = lax.broadcasted_iota(jnp.int32, (rows, rows), 1)
-    table = jnp.zeros((rows, rows), F32)
-    for at, column in enumerate(columns):
-        table = jnp.where(names == at, column, table)
-    table = table.T[:NOTES].astype(BF)
+    notes.append(jnp.zeros((NOTES - len(notes), rows), F32))
+    table = jnp.concatenate(notes, axis=0).astype(BF)
     core = where[0]
     for out, side in ((same, core), (cross, 1 - core)):
         for kind, source in enumerate((tokens, cotangent)):
@@ -163,7 +172,7 @@
     half = got.shape[3] // 2
     for za in range(QUAD):
         for at, step in enumerate(WINDOW[0]):
-            chip = 4 * za + jnp.bitwise_and(where[0] + (step + 4), 3)
+            chip = 4 * jnp.bitwise_and(where[1] + za, 3) + jnp.bitwise_and(where[0] + (step + 4), 3)
             for core in range(2):
                 for kind in range(2):
                     lane = (4 * kind + at) * half
@@ -177,7 +186,7 @@
     half = out.shape[3] // 2
     for za in range(QUAD):
         for at, step in enumerate(WINDOW[0]):
-            chip = 4 * za + jnp.bitwise_and(where[0] + (step + 4), 3)
+            chip = 4 * jnp.bitwise_and(where[1] + za, 3) + jnp.bitwise_and(where[0] + (step + 4), 3)
             for core in range(2):
                 for kind in range(2):
                     lane = (4 * kind + at) * half
@@ -335,20 +344,20 @@
 
 
 def place_routes(route, experts):
-    rows = route.shape[0]
-    names = lax.broadcasted_iota(jnp.int32, (rows, experts), 1)
-    first = ones_where(route[:, 0:1] == names)
-    second = ones_where(route[:, 1:2] == names)
-    below = ones_where(
+    rows = route.shape[1]
+    names = lax.broadcasted_iota(jnp.int32, (experts, rows), 0)
+    first = ones_where(route[0:1] == names)
+    second = ones_where(route[1:2] == names)
+    before = ones_where(
         lax.broadcasted_iota(jnp.int32, (rows, rows), 0)
-        > lax.broadcasted_iota(jnp.int32, (rows, rows), 1)
+        < lax.broadcasted_iota(jnp.int32, (rows, rows), 1)
     ).astype(BF)
-    earlier = contract(below, (first + second).astype(BF), 1, 0)
+    earlier = contract((first + second).astype(BF), before, 1, 0)
     return [
-        route[:, 0:1].astype(F32),
-        route[:, 1:2].astype(F32),
-        jnp.sum(earlier * first, axis=1, keepdims=True),
-        jnp.sum((earlier + first) * second, axis=1, keepdims=True),
+        route[0:1].astype(F32),
+        route[1:2].astype(F32),
+        jnp.sum(earlier * first, axis=0, keepdims=True),
+        jnp.sum((earlier + first) * second, axis=0, keepdims=True),
     ]
 
 
@@ -378,23 +387,23 @@
     zb = lax.axis_index("zb").astype(jnp.int32).reshape(1)
     core = lax.axis_index("core").astype(jnp.int32).reshape(1)
 
-    packed = kernel_call(
+    routed = (route.T, route_weight.T, tokens, cotangent)
+    packed = pl.pallas_call(
         pack_kernel,
-        [jax.ShapeDtypeStruct((group_rows + NOTES, 2 * half), BF)] * 2,
-        core,
-        route,
-        route_weight,
-        tokens,
-        cotangent,
-        scalars=1,
-    )
+        out_shape=(jax.ShapeDtypeStruct((group_rows + NOTES, 2 * half), BF),) * 2,
+        in_specs=[pl.BlockSpec(memory_space=pltpu.SMEM)]
+        + [pl.BlockSpec(memory_space=pltpu.HBM)] * 4,
+        out_specs=(pl.BlockSpec(memory_space=pltpu.VMEM),) * 2,
+        scratch_shapes=[pltpu.VMEM(a.shape, a.dtype) for a in routed]
+        + [pltpu.SemaphoreType.DMA((4,))],
+        compiler_params=pltpu.CompilerParams(vmem_limit_bytes=60 * 1024 * 1024),
+    )(core, *routed)
     same = to_window(packed[0], False)
     cross = to_window(packed[1], True)
     w_own = pl.pallas_call(
         sample_kernel,
         out_shape=jax.ShapeDtypeStruct((half, 3 * width), BF),
-        in_specs=[pl.BlockSpec(memory_space=pltpu.HBM)] * 9
-        + [pl.BlockSpec(memory_space=pl.ANY)] * 2,
+        in_specs=[pl.BlockSpec(memory_space=pltpu.HBM)] * 9,
         out_specs=pl.BlockSpec(memory_space=pltpu.VMEM),
         scratch_shapes=[
             pltpu.VMEM((6, half, width), BF),
@@ -412,9 +421,8 @@
         mean_down,
         spread_down,
         noise_down,
-        same,
-        cross,
-    )
+    )
+    w_own, same, cross = lax.optimization_barrier((w_own, same, cross))
     weights = (
         w_own,
         along_ring(w_own, (-1, -1)),
@@ -434,7 +442,7 @@
     (got,) = kernel_call(
         spread_kernel,
         [jax.ShapeDtypeStruct((2 * QUAD, cap, 8 * half), BF)],
-        zb,
+        jnp.concatenate([zb, me]),
         got,
         scalars=1,
     )
@@ -493,7 +501,7 @@
     (home,) = kernel_call(
         collect_kernel,
         [jax.ShapeDtypeStruct((experts, 2, cap, 2 * half), BF)],
-        zb,
+        jnp.concatenate([zb, me]),
         outs,
         w_sent[3],
         scalars=1,

time: 199 us -> 189 us (0.950)
  the two profiles are of different devices: /device:TPU:48 before, /device:TPU:16 now
where the time goes in v5:
time: 189 us; the launch traced here: 188 us
  starting transfers between devices  77.6 us (41%)
  waiting for transfers between devices  53.3 us (28%)
  blocking collectives  42.6 us (23%)
  Pallas kernels  13.3 us (7%)
    ppermute x4, starting transfers between devices, to_window(): return lax.ppermute(value, PLANE + RING, pairs)  28.7 us
    ppermute x4, waiting for transfers between devices, to_window(): return lax.ppermute(value, PLANE + RING, pairs)  25.7 us
    all_gather x1, blocking collectives, body(): rows = lax.all_gather(rows, 'za', axis=0, tiled=True)  23.7 us
    ppermute x4, starting transfers between devices, shift(): lax.ppermute(value, 'za', [(i, (i + step) % QUAD) for i in range(QUAD)])  19.5 us
    ppermute x6, starting transfers between devices, along_ring(): return lax.ppermute(value, RING, pairs)  17.9 us
    all_to_all x1, blocking collectives, body(): home = lax.all_to_all(home, PLANE, split_axis=0, concat_axis=0, tiled=True)  16.4 us
    ppermute x4, waiting for transfers between devices, shift(): lax.ppermute(value, 'za', [(i, (i + step) % QUAD) for i in range(QUAD)])  15.4 us
    pallas_call x12, Pallas kernels, kernel_call(): pl.pallas_call(kernel, out_shape=tuple(outs), in_specs=[pl.BlockSpec(memo...  8.99 us
  transfers between devices with their start and end apart: 16, of which 11 were waited for; matrix products, arithmetic and copies ran while one was open for 0% of the time, Pallas kernels for 4%

profile of v5, /device:TPU:16, one launch (start us, length us, event | category | flops | bytes accessed | tf_op | source)
XLA Modules:
  0.0 187.9 jit_solution(18092096965343542737)
XLA Ops:
  0.6 1.7 shard_map.189
  2.4 15.7 %collective-permute-start = (bf16[144,256]{1,0:T(8,128)(2,1)}, bf16[144,256]{1,0:T(8,128)(2,1)S(1)}, u32[]{:S(2)}, u32[]{:S(2)}) collective-permute-start(bf16[144,256]{1,0:T(8,128)(2,1)} %get-tuple-element.34), channel_id=1, source_target_pairs={{0,0},{1,1},{2,2},{3,3},{4,412},{5,5},{6,414},{7,415},{8,128},{9,1... | collective-permute-start | bytes 221192 | tf_op jit(solution)/shard_map/ppermute | solution.py:67
  18.1 1.9 %collective-permute-start.1 = (bf16[144,256]{1,0:T(8,128)(2,1)}, bf16[144,256]{1,0:T(8,128)(2,1)S(1)}, u32[]{:S(2)}, u32[]{:S(2)}) collective-permute-start(bf16[144,256]{1,0:T(8,128)(2,1)} %get-tuple-element.35), channel_id=1, source_target_pairs={{0,1},{1,0},{2,3},{3,2},{4,5},{5,412},{6,415},{7,414},{8,129},{9,1... | collective-permute-start | bytes 221192 | tf_op jit(solution)/shard_map/ppermute | solution.py:67
  20.0 2.6 %shard_map.188.w0 = bf16[128,2304]{1,0:T(8,128)(2,1)} custom-call(bf16[1,128,768]{2,1,0:T(8,128)(2,1)} %refs_0_.1, bf16[1,128,768]{2,1,0:T(8,128)(2,1)} %refs_1_.1, bf16[1,128,768]{2,1,0:T(8,128)(2,1)} %ng.1, bf16[1,128,768]{2,1,0:T(8,128)(2,1)} %refs_3_.2, bf16[1,128,768]{2,1,0:T(8,128)(2,1)} %refs_4_.1, bf16[1,128,768]{2,1,0:T(8,128)(2,1)} %nu.1, ...), custom_call_target="tpu_custom_call" | custom-call | tf_op jit(solution)/shard_map/pallas_call | solution.py:403
  22.7 13.1 %collective-permute-done.1.cross = bf16[144,256]{1,0:T(8,128)(2,1)S(1)} collective-permute-done((bf16[144,256]{1,0:T(8,128)(2,1)}, bf16[144,256]{1,0:T(8,128)(2,1)S(1)}, u32[]{:S(2)}, u32[]{:S(2)}) %collective-permute-start.1) | collective-permute-done | bytes 73760 | tf_op jit(solution)/shard_map/ppermute | solution.py:67
  35.7 1.9 %collective-permute-start.4 = (bf16[128,2304]{1,0:T(8,128)(2,1)}, bf16[128,2304]{1,0:T(8,128)(2,1)S(1)}, u32[]{:S(2)}, u32[]{:S(2)}) collective-permute-start(bf16[128,2304]{1,0:T(8,128)(2,1)} %shard_map.188.w0), channel_id=1, source_target_pairs={{0,28},{1,5},{2,30},{3,7},{4,0},{5,9},{6,2},{7,11},{8,4},{9,13},{1... | collective-permute-start | bytes 1769480 | tf_op jit(solution)/shard_map/ppermute | solution.py:43
  37.7 3.0 %collective-permute-start.3 = (bf16[128,2304]{1,0:T(8,128)(2,1)}, bf16[128,2304]{1,0:T(8,128)(2,1)S(1)}, u32[]{:S(2)}, u32[]{:S(2)}) collective-permute-start(bf16[128,2304]{1,0:T(8,128)(2,1)} %shard_map.188.w0), channel_id=1, source_target_pairs={{0,2},{1,3},{2,4},{3,5},{4,6},{5,7},{6,8},{7,9},{8,10},{9,11},{10,... | collective-permute-start | bytes 1769480 | tf_op jit(solution)/shard_map/ppermute | solution.py:43
  40.7 4.0 %collective-permute-start.2 = (bf16[128,2304]{1,0:T(8,128)(2,1)}, bf16[128,2304]{1,0:T(8,128)(2,1)S(1)}, u32[]{:S(2)}, u32[]{:S(2)}) collective-permute-start(bf16[128,2304]{1,0:T(8,128)(2,1)} %shard_map.188.w0), channel_id=1, source_target_pairs={{0,30},{1,31},{2,0},{3,1},{4,2},{5,3},{6,4},{7,5},{8,6},{9,7},{10,... | collective-permute-start | bytes 1769480 | tf_op jit(solution)/shard_map/ppermute | solution.py:43
  45.7 8.4 %all-to-all-start = ((bf16[16,2,24,256]{3,2,1,0:T(8,128)(2,1)}), bf16[16,2,24,256]{3,2,1,0:T(8,128)(2,1)S(1)}, u32[]{:S(2)}, u32[]{:S(2)}) async-start(bf16[16,2,24,256]{3,2,1,0:T(8,128)(2,1)} %shard_map.190), calls=%async_computation | async-start | bytes 786432 | tf_op jit(solution)/shard_map/all_to_all | solution.py:441
  54.2 7.7 %all-to-all-done.got = bf16[16,2,24,256]{3,2,1,0:T(8,128)(2,1)S(1)} async-done(((bf16[16,2,24,256]{3,2,1,0:T(8,128)(2,1)}), bf16[16,2,24,256]{3,2,1,0:T(8,128)(2,1)S(1)}, u32[]{:S(2)}, u32[]{:S(2)}) %all-to-all-start) | async-done | bytes 393248 | tf_op jit(solution)/shard_map/all_to_all | solution.py:441
  63.3 2.6 %collective-permute-done.2.w1 = bf16[128,2304]{1,0:T(8,128)(2,1)S(1)} collective-permute-done((bf16[128,2304]{1,0:T(8,128)(2,1)}, bf16[128,2304]{1,0:T(8,128)(2,1)S(1)}, u32[]{:S(2)}, u32[]{:S(2)}) %collective-permute-start.2) | collective-permute-done | bytes 589856 | tf_op jit(solution)/shard_map/ppermute | solution.py:43
  66.5 3.0 %collective-permute-start.5 = (bf16[4,24,2304]{2,1,0:T(8,128)(2,1)S(1)}, bf16[4,24,2304]{2,1,0:T(8,128)(2,1)S(1)}, u32[]{:S(2)}, u32[]{:S(2)}) collective-permute-start(bf16[4,24,2304]{2,1,0:T(8,128)(2,1)S(1)} %shard_map.192), channel_id=1, source_target_pairs={{0,1},{1,0},{2,3},{3,2},{4,5},{5,4},{6,7},{7,6},{8,9},{9,8},{10,11... | collective-permute-start | bytes 1327112 | tf_op jit(solution)/shard_map/ppermute | solution.py:459
  69.6 1.3 collective-permute-done.5.other
  70.9 1.3 shard_map.193
  72.2 3.9 %collective-permute-start.6 = (bf16[24,1152]{1,0:T(8,128)(2,1)S(1)}, bf16[24,1152]{1,0:T(8,128)(2,1)S(1)}, u32[]{:S(2)}, u32[]{:S(2)}) collective-permute-start(bf16[24,1152]{1,0:T(8,128)(2,1)S(1)} %get-tuple-element.42), channel_id=1, source_target_pairs={{0,8},{8,16},{16,24},{24,0},{1,9},{9,17},{17,25},{25,1},{2,10},{10... | collective-permute-start | bytes 165896 | tf_op jit(solution)/shard_map/ppermute | solution.py:33
  76.0 5.9 %collective-permute-start.7 = (bf16[24,1152]{1,0:T(8,128)(2,1)S(1)}, bf16[24,1152]{1,0:T(8,128)(2,1)S(1)}, u32[]{:S(2)}, u32[]{:S(2)}) collective-permute-start(bf16[24,1152]{1,0:T(8,128)(2,1)S(1)} %get-tuple-element.43), channel_id=1, source_target_pairs={{0,24},{8,0},{16,8},{24,16},{1,25},{9,1},{17,9},{25,17},{2,26},{10... | collective-permute-start | bytes 165896 | tf_op jit(solution)/shard_map/ppermute | solution.py:33
  82.5 6.2 %collective-permute-done.7.from_right = bf16[24,1152]{1,0:T(8,128)(2,1)S(1)} collective-permute-done((bf16[24,1152]{1,0:T(8,128)(2,1)S(1)}, bf16[24,1152]{1,0:T(8,128)(2,1)S(1)}, u32[]{:S(2)}, u32[]{:S(2)}) %collective-permute-start.7) | collective-permute-done | bytes 55328 | tf_op jit(solution)/shard_map/ppermute | solution.py:33
  88.8 3.4 %collective-permute-start.8 = (bf16[24,2304]{1,0:T(8,128)(2,1)S(1)}, bf16[24,2304]{1,0:T(8,128)(2,1)S(1)}, u32[]{:S(2)}, u32[]{:S(2)}) collective-permute-start(bf16[24,2304]{1,0:T(8,128)(2,1)S(1)} %get-tuple-element.44), channel_id=1, source_target_pairs={{0,8},{8,16},{16,24},{24,0},{1,9},{9,17},{17,25},{25,1},{2,10},{10... | collective-permute-start | bytes 331784 | tf_op jit(solution)/shard_map/ppermute | solution.py:33
  92.2 6.3 %collective-permute-start.9 = (bf16[24,2304]{1,0:T(8,128)(2,1)S(1)}, bf16[24,2304]{1,0:T(8,128)(2,1)S(1)}, u32[]{:S(2)}, u32[]{:S(2)}) collective-permute-start(bf16[24,2304]{1,0:T(8,128)(2,1)S(1)} %get-tuple-element.45), channel_id=1, source_target_pairs={{0,24},{8,0},{16,8},{24,16},{1,25},{9,1},{17,9},{25,17},{2,26},{10... | collective-permute-start | bytes 331784 | tf_op jit(solution)/shard_map/ppermute | solution.py:33
  98.5 4.1 %collective-permute-done.8.from_left = bf16[24,2304]{1,0:T(8,128)(2,1)S(1)} collective-permute-done((bf16[24,2304]{1,0:T(8,128)(2,1)S(1)}, bf16[24,2304]{1,0:T(8,128)(2,1)S(1)}, u32[]{:S(2)}, u32[]{:S(2)}) %collective-permute-start.8) | collective-permute-done | bytes 110624 | tf_op jit(solution)/shard_map/ppermute | solution.py:33
  102.6 4.5 %collective-permute-done.9.from_right = bf16[24,2304]{1,0:T(8,128)(2,1)S(1)} collective-permute-done((bf16[24,2304]{1,0:T(8,128)(2,1)S(1)}, bf16[24,2304]{1,0:T(8,128)(2,1)S(1)}, u32[]{:S(2)}, u32[]{:S(2)}) %collective-permute-start.9) | collective-permute-done | bytes 110624 | tf_op jit(solution)/shard_map/ppermute | solution.py:33
  107.2 23.7 %all_gather.6 = bf16[96,2304]{1,0:T(8,128)(2,1)S(1)} all-gather(bf16[24,2304]{1,0:T(8,128)(2,1)S(1)} %shard_map.195), channel_id=1, replica_groups=mesh['y'=4,'x'=4,'za'=4,'zb'=4,'core'=2] {'za'}, dimensions={0}, use_global_device_ids=true | all-gather | bytes 552960 | tf_op jit(solution)/shard_map/all_gather | solution.py:481
  130.9 2.4 %all_gather.7.rows = bf16[192,2304]{1,0:T(8,128)(2,1)S(1)} all-gather(bf16[96,2304]{1,0:T(8,128)(2,1)S(1)} %all_gather.6), channel_id=1, replica_groups=mesh['y'=4,'x'=4,'za'=4,'zb'=4,'core'=2] {'core'}, dimensions={0}, use_global_device_ids=true | all-gather | bytes 1327104 | tf_op jit(solution)/shard_map/all_gather | solution.py:482
  134.2 1.9 %collective-permute-start.12 = (bf16[128,2304]{1,0:T(8,128)(2,1)S(1)}, bf16[128,2304]{1,0:T(8,128)(2,1)S(1)}, u32[]{:S(2)}, u32[]{:S(2)}) collective-permute-start(bf16[128,2304]{1,0:T(8,128)(2,1)S(1)} %get-tuple-element.52), channel_id=1, source_target_pairs={{0,2},{1,3},{2,4},{3,5},{4,6},{5,7},{6,8},{7,9},{8,10},{9,11},{10,... | collective-permute-start | bytes 1769480 | tf_op jit(solution)/shard_map/ppermute | solution.py:43
  136.1 5.1 %collective-permute-start.13 = (bf16[128,2304]{1,0:T(8,128)(2,1)S(1)}, bf16[128,2304]{1,0:T(8,128)(2,1)S(1)}, u32[]{:S(2)}, u32[]{:S(2)}) collective-permute-start(bf16[128,2304]{1,0:T(8,128)(2,1)S(1)} %get-tuple-element.53), channel_id=1, source_target_pairs={{0,30},{1,31},{2,0},{3,1},{4,2},{5,3},{6,4},{7,5},{8,6},{9,7},{10,... | collective-permute-start | bytes 1769480 | tf_op jit(solution)/shard_map/ppermute | solution.py:43
  141.2 1.9 %collective-permute-start.14 = (bf16[128,2304]{1,0:T(8,128)(2,1)S(1)}, bf16[128,2304]{1,0:T(8,128)(2,1)S(1)}, u32[]{:S(2)}, u32[]{:S(2)}) collective-permute-start(bf16[128,2304]{1,0:T(8,128)(2,1)S(1)} %get-tuple-element.46.rest_0_), channel_id=1, source_target_pairs={{0,4},{1,29},{2,6},{3,31},{4,8},{5,1},{6,10},{7,3},{8,12},{9,5},{1... | collective-permute-start | bytes 1769480 | tf_op jit(solution)/shard_map/ppermute | solution.py:43
  144.9 16.4 %all_to_all.10.home = bf16[16,2,24,256]{3,2,1,0:T(8,128)(2,1)S(1)} all-to-all(bf16[16,2,24,256]{3,2,1,0:T(8,128)(2,1)S(1)} %shard_map.198), channel_id=1, replica_groups=mesh['y'=4,'x'=4,'za'=4,'zb'=4,'core'=2] {'y','x'}, dimensions={0} | all-to-all | bytes 786432 | tf_op jit(solution)/shard_map/all_to_all | solution.py:510
  161.8 9.2 %collective-permute-start.10 = (bf16[128,256]{1,0:T(8,128)(2,1)S(1)}, bf16[128,256]{1,0:T(8,128)(2,1)S(1)}, u32[]{:S(2)}, u32[]{:S(2)}) collective-permute-start(bf16[128,256]{1,0:T(8,128)(2,1)S(1)} %get-tuple-element.47), channel_id=1, source_target_pairs={{0,0},{1,1},{2,2},{3,3},{412,4},{5,5},{414,6},{415,7},{128,8},{129... | collective-permute-start | bytes 196616 | tf_op jit(solution)/shard_map/ppermute | solution.py:67
  171.0 1.9 %collective-permute-start.11 = (bf16[128,256]{1,0:T(8,128)(2,1)S(1)}, bf16[128,256]{1,0:T(8,128)(2,1)S(1)}, u32[]{:S(2)}, u32[]{:S(2)}) collective-permute-start(bf16[128,256]{1,0:T(8,128)(2,1)S(1)} %get-tuple-element.48), channel_id=1, source_target_pairs={{1,0},{0,1},{3,2},{2,3},{5,4},{412,5},{415,6},{414,7},{129,8},{128... | collective-permute-start | bytes 196616 | tf_op jit(solution)/shard_map/ppermute | solution.py:67
  172.9 3.9 %collective-permute-done.10.same = bf16[128,256]{1,0:T(8,128)(2,1)S(1)} collective-permute-done((bf16[128,256]{1,0:T(8,128)(2,1)S(1)}, bf16[128,256]{1,0:T(8,128)(2,1)S(1)}, u32[]{:S(2)}, u32[]{:S(2)}) %collective-permute-start.10) | collective-permute-done | bytes 65568 | tf_op jit(solution)/shard_map/ppermute | solution.py:67
  176.8 8.7 %collective-permute-done.11.cross = bf16[128,256]{1,0:T(8,128)(2,1)S(1)} collective-permute-done((bf16[128,256]{1,0:T(8,128)(2,1)S(1)}, bf16[128,256]{1,0:T(8,128)(2,1)S(1)}, u32[]{:S(2)}, u32[]{:S(2)}) %collective-permute-start.11) | collective-permute-done | bytes 65568 | tf_op jit(solution)/shard_map/ppermute | solution.py:67
  186.2 1.7 shard_map.201
  (27 shorter events, 7.5 us)
Async XLA Ops:
  2.4 20.3 %collective-permute-start = (bf16[144,256]{1,0:T(8,128)(2,1)}, bf16[144,256]{1,0:T(8,128)(2,1)S(1)}, u32[]{:S(2)}, u32[]{:S(2)}) collective-permute-start(bf16[144,256]{1,0:T(8,128)(2,1)} %get-tuple-element.34), channel_id=1, source_target_pairs={{0,0},{1,1},{2,2},{3,3},{4,412},{5,5},{6,414},{7,415},{8,128},{9,1... | collective-permute-start | bytes 221192 | tf_op jit(solution)/shard_map/ppermute | solution.py:67
  18.1 17.6 %collective-permute-start.1 = (bf16[144,256]{1,0:T(8,128)(2,1)}, bf16[144,256]{1,0:T(8,128)(2,1)S(1)}, u32[]{:S(2)}, u32[]{:S(2)}) collective-permute-start(bf16[144,256]{1,0:T(8,128)(2,1)} %get-tuple-element.35), channel_id=1, source_target_pairs={{0,1},{1,0},{2,3},{3,2},{4,5},{5,412},{6,415},{7,414},{8,129},{9,1... | collective-permute-start | bytes 221192 | tf_op jit(solution)/shard_map/ppermute | solution.py:67
  22.6 43.2 %copy-start = (bf16[128,2304]{1,0:T(8,128)(2,1)S(1)}, bf16[128,2304]{1,0:T(8,128)(2,1)}, u32[]{:S(2)}) copy-start(bf16[128,2304]{1,0:T(8,128)(2,1)} %shard_map.188.w0) | copy-start | bytes 1769476
  35.7 26.8 %collective-permute-start.4 = (bf16[128,2304]{1,0:T(8,128)(2,1)}, bf16[128,2304]{1,0:T(8,128)(2,1)S(1)}, u32[]{:S(2)}, u32[]{:S(2)}) collective-permute-start(bf16[128,2304]{1,0:T(8,128)(2,1)} %shard_map.188.w0), channel_id=1, source_target_pairs={{0,28},{1,5},{2,30},{3,7},{4,0},{5,9},{6,2},{7,11},{8,4},{9,13},{1... | collective-permute-start | bytes 1769480 | tf_op jit(solution)/shard_map/ppermute | solution.py:43
  37.7 25.6 %collective-permute-start.3 = (bf16[128,2304]{1,0:T(8,128)(2,1)}, bf16[128,2304]{1,0:T(8,128)(2,1)S(1)}, u32[]{:S(2)}, u32[]{:S(2)}) collective-permute-start(bf16[128,2304]{1,0:T(8,128)(2,1)} %shard_map.188.w0), channel_id=1, source_target_pairs={{0,2},{1,3},{2,4},{3,5},{4,6},{5,7},{6,8},{7,9},{8,10},{9,11},{10,... | collective-permute-start | bytes 1769480 | tf_op jit(solution)/shard_map/ppermute | solution.py:43
  40.7 25.1 %collective-permute-start.2 = (bf16[128,2304]{1,0:T(8,128)(2,1)}, bf16[128,2304]{1,0:T(8,128)(2,1)S(1)}, u32[]{:S(2)}, u32[]{:S(2)}) collective-permute-start(bf16[128,2304]{1,0:T(8,128)(2,1)} %shard_map.188.w0), channel_id=1, source_target_pairs={{0,30},{1,31},{2,0},{3,1},{4,2},{5,3},{6,4},{7,5},{8,6},{9,7},{10,... | collective-permute-start | bytes 1769480 | tf_op jit(solution)/shard_map/ppermute | solution.py:43
  45.7 16.2 %all-to-all-start = ((bf16[16,2,24,256]{3,2,1,0:T(8,128)(2,1)}), bf16[16,2,24,256]{3,2,1,0:T(8,128)(2,1)S(1)}, u32[]{:S(2)}, u32[]{:S(2)}) async-start(bf16[16,2,24,256]{3,2,1,0:T(8,128)(2,1)} %shard_map.190), calls=%async_computation | async-start | bytes 786432 | tf_op jit(solution)/shard_map/all_to_all | solution.py:441
  66.5 4.4 %collective-permute-start.5 = (bf16[4,24,2304]{2,1,0:T(8,128)(2,1)S(1)}, bf16[4,24,2304]{2,1,0:T(8,128)(2,1)S(1)}, u32[]{:S(2)}, u32[]{:S(2)}) collective-permute-start(bf16[4,24,2304]{2,1,0:T(8,128)(2,1)S(1)} %shard_map.192), channel_id=1, source_target_pairs={{0,1},{1,0},{2,3},{3,2},{4,5},{5,4},{6,7},{7,6},{8,9},{9,8},{10,11... | collective-permute-start | bytes 1327112 | tf_op jit(solution)/shard_map/ppermute | solution.py:459
  72.2 10.4 %collective-permute-start.6 = (bf16[24,1152]{1,0:T(8,128)(2,1)S(1)}, bf16[24,1152]{1,0:T(8,128)(2,1)S(1)}, u32[]{:S(2)}, u32[]{:S(2)}) collective-permute-start(bf16[24,1152]{1,0:T(8,128)(2,1)S(1)} %get-tuple-element.42), channel_id=1, source_target_pairs={{0,8},{8,16},{16,24},{24,0},{1,9},{9,17},{17,25},{25,1},{2,10},{10... | collective-permute-start | bytes 165896 | tf_op jit(solution)/shard_map/ppermute | solution.py:33
  76.0 12.7 %collective-permute-start.7 = (bf16[24,1152]{1,0:T(8,128)(2,1)S(1)}, bf16[24,1152]{1,0:T(8,128)(2,1)S(1)}, u32[]{:S(2)}, u32[]{:S(2)}) collective-permute-start(bf16[24,1152]{1,0:T(8,128)(2,1)S(1)} %get-tuple-element.43), channel_id=1, source_target_pairs={{0,24},{8,0},{16,8},{24,16},{1,25},{9,1},{17,9},{25,17},{2,26},{10... | collective-permute-start | bytes 165896 | tf_op jit(solution)/shard_map/ppermute | solution.py:33
  88.8 13.9 %collective-permute-start.8 = (bf16[24,2304]{1,0:T(8,128)(2,1)S(1)}, bf16[24,2304]{1,0:T(8,128)(2,1)S(1)}, u32[]{:S(2)}, u32[]{:S(2)}) collective-permute-start(bf16[24,2304]{1,0:T(8,128)(2,1)S(1)} %get-tuple-element.44), channel_id=1, source_target_pairs={{0,8},{8,16},{16,24},{24,0},{1,9},{9,17},{17,25},{25,1},{2,10},{10... | collective-permute-start | bytes 331784 | tf_op jit(solution)/shard_map/ppermute | solution.py:33
  92.2 14.9 %collective-permute-start.9 = (bf16[24,2304]{1,0:T(8,128)(2,1)S(1)}, bf16[24,2304]{1,0:T(8,128)(2,1)S(1)}, u32[]{:S(2)}, u32[]{:S(2)}) collective-permute-start(bf16[24,2304]{1,0:T(8,128)(2,1)S(1)} %get-tuple-element.45), channel_id=1, source_target_pairs={{0,24},{8,0},{16,8},{24,16},{1,25},{9,1},{17,9},{25,17},{2,26},{10... | collective-permute-start | bytes 331784 | tf_op jit(solution)/shard_map/ppermute | solution.py:33
  134.2 52.0 %collective-permute-start.12 = (bf16[128,2304]{1,0:T(8,128)(2,1)S(1)}, bf16[128,2304]{1,0:T(8,128)(2,1)S(1)}, u32[]{:S(2)}, u32[]{:S(2)}) collective-permute-start(bf16[128,2304]{1,0:T(8,128)(2,1)S(1)} %get-tuple-element.52), channel_id=1, source_target_pairs={{0,2},{1,3},{2,4},{3,5},{4,6},{5,7},{6,8},{7,9},{8,10},{9,11},{10,... | collective-permute-start | bytes 1769480 | tf_op jit(solution)/shard_map/ppermute | solution.py:43
  136.1 50.1 %collective-permute-start.13 = (bf16[128,2304]{1,0:T(8,128)(2,1)S(1)}, bf16[128,2304]{1,0:T(8,128)(2,1)S(1)}, u32[]{:S(2)}, u32[]{:S(2)}) collective-permute-start(bf16[128,2304]{1,0:T(8,128)(2,1)S(1)} %get-tuple-element.53), channel_id=1, source_target_pairs={{0,30},{1,31},{2,0},{3,1},{4,2},{5,3},{6,4},{7,5},{8,6},{9,7},{10,... | collective-permute-start | bytes 1769480 | tf_op jit(solution)/shard_map/ppermute | solution.py:43
  141.2 44.9 %collective-permute-start.14 = (bf16[128,2304]{1,0:T(8,128)(2,1)S(1)}, bf16[128,2304]{1,0:T(8,128)(2,1)S(1)}, u32[]{:S(2)}, u32[]{:S(2)}) collective-permute-start(bf16[128,2304]{1,0:T(8,128)(2,1)S(1)} %get-tuple-element.46.rest_0_), channel_id=1, source_target_pairs={{0,4},{1,29},{2,6},{3,31},{4,8},{5,1},{6,10},{7,3},{8,12},{9,5},{1... | collective-permute-start | bytes 1769480 | tf_op jit(solution)/shard_map/ppermute | solution.py:43
  144.2 41.9 %copy-start.1 = (bf16[1,128,768]{2,1,0:T(8,128)(2,1)S(1)}, bf16[1,128,768]{2,1,0:T(8,128)(2,1)}, u32[]{:S(2)}) copy-start(bf16[1,128,768]{2,1,0:T(8,128)(2,1)} %ng.1) | copy-start | bytes 589828
  144.3 41.9 %copy-start.2 = (bf16[1,128,768]{2,1,0:T(8,128)(2,1)S(1)}, bf16[1,128,768]{2,1,0:T(8,128)(2,1)}, u32[]{:S(2)}) copy-start(bf16[1,128,768]{2,1,0:T(8,128)(2,1)} %nu.1) | copy-start | bytes 589828
  144.3 41.9 %copy-start.3 = (bf16[1,768,128]{2,1,0:T(8,128)(2,1)S(1)}, bf16[1,768,128]{2,1,0:T(8,128)(2,1)}, u32[]{:S(2)}) copy-start(bf16[1,768,128]{2,1,0:T(8,128)(2,1)} %nd.1) | copy-start | bytes 589828
  161.8 15.0 %collective-permute-start.10 = (bf16[128,256]{1,0:T(8,128)(2,1)S(1)}, bf16[128,256]{1,0:T(8,128)(2,1)S(1)}, u32[]{:S(2)}, u32[]{:S(2)}) collective-permute-start(bf16[128,256]{1,0:T(8,128)(2,1)S(1)} %get-tuple-element.47), channel_id=1, source_target_pairs={{0,0},{1,1},{2,2},{3,3},{412,4},{5,5},{414,6},{415,7},{128,8},{129... | collective-permute-start | bytes 196616 | tf_op jit(solution)/shard_map/ppermute | solution.py:67
  171.0 14.5 %collective-permute-start.11 = (bf16[128,256]{1,0:T(8,128)(2,1)S(1)}, bf16[128,256]{1,0:T(8,128)(2,1)S(1)}, u32[]{:S(2)}, u32[]{:S(2)}) collective-permute-start(bf16[128,256]{1,0:T(8,128)(2,1)S(1)} %get-tuple-element.48), channel_id=1, source_target_pairs={{1,0},{0,1},{3,2},{2,3},{5,4},{412,5},{415,6},{414,7},{129,8},{128... | collective-permute-start | bytes 196616 | tf_op jit(solution)/shard_map/ppermute | solution.py:67

commit v6 on v5

--- a/solution.py
+++ b/solution.py
@@ -56,12 +56,13 @@
     pairs = []
     for y, x, za, zb, core in itertools.product(*map(range, sizes)):
         side = 1 - core if cross else core
+        near = (zb + quads // 2) % quads
         for goal in range(QUAD):
             for step in WINDOW[side]:
-                if (quads * goal + zb + step - quads * y - x) % (QUAD * quads) == 0:
+                if (quads * goal + near + step - quads * y - x) % (QUAD * quads) == 0:
                     pair = (
                         index((y, x, za, zb, core)),
-                        index(((za + goal) % QUAD, x, goal, zb, side)),
+                        index(((za + goal) % QUAD, x, goal, near, side)),
                     )
                     pairs.append(pair[::-1] if back else pair)
     return lax.ppermute(value, PLANE + RING, pairs)
@@ -215,7 +216,8 @@
         out[:, half:] = contract(one + two, slots[:, half:], 0, 0).astype(BF)
 
 
-def unpack_kernel(where, same, cross, mixed, grad):
+def unpack_kernel(where, same, cross, after, mixed, grad):
+    del after
     half = same.shape[1] // 2
     first = where[0] == 0
     for kind, out in enumerate((mixed, grad)):
@@ -319,7 +321,7 @@
         g[:, 2 * width :] = value.astype(g.dtype)
 
 
-def finish_kernel(g0, g1, g2, g3, ng, nu, nd, mg, sg, mu, su, md, sd):
+def finish_kernel(g0, g1, g2, g3, ng, nu, nd, mg, sg, mu, su, md, sd, done):
     width = ng.shape[2]
 
     def total(start):
@@ -337,6 +339,7 @@
     down = total(2 * width).T
     md[0] = down
     sd[0] = down * nd[0].astype(F32)
+    done[...] = jnp.zeros_like(done)
 
 
 def ones_where(condition):
@@ -517,25 +520,27 @@
         home,
         scalars=1,
     )
+    by_row = jax.ShapeDtypeStruct((1, half, width), F32)
+    by_column = jax.ShapeDtypeStruct((1, width, half), F32)
+    ends = kernel_call(
+        finish_kernel,
+        [by_row] * 4 + [by_column] * 2 + [jax.ShapeDtypeStruct((8, 128), F32)],
+        *w_grads,
+        noise_gate,
+        noise_up,
+        noise_down,
+    )
     mixed_out, token_grad = kernel_call(
         unpack_kernel,
         [jax.ShapeDtypeStruct((group_rows, feats), BF)] * 2,
         core,
         to_window(ready[0], False, True),
         to_window(ready[1], True, True),
-        scalars=1,
-    )
-    by_row = jax.ShapeDtypeStruct((1, half, width), F32)
-    by_column = jax.ShapeDtypeStruct((1, width, half), F32)
-    ends = kernel_call(
-        finish_kernel,
-        [by_row] * 4 + [by_column] * 2,
-        *w_grads,
-        noise_gate,
-        noise_up,
-        noise_down,
-    )
-    return (mixed_out, token_grad) + tuple(ends)
+        ends[6],
+        scalars=1,
+        free=1,
+    )
+    return (mixed_out, token_grad) + tuple(ends[:6])
 
 
 def solution(mesh):

time: 189 us -> 183 us (0.968)
  waiting for transfers between devices: 53.3 us -> 45.2 us
  starting transfers between devices: 77.6 us -> 84.1 us
  blocking collectives: 42.6 us -> 38.5 us
    ppermute x4, waiting for transfers between devices: 25.7 us -> 16.1 us  [to_window(): return lax.ppermute(value, PLANE + RING, pairs)]
    ppermute x6, starting transfers between devices: 17.9 us -> 26.3 us  [along_ring(): return lax.ppermute(value, RING, pairs)]
    all_to_all x1, blocking collectives: 16.4 us -> 14.1 us  [body(): home = lax.all_to_all(home, PLANE, split_axis=0, concat_axis=0, tiled=True)]
  transfers between devices with their start and end apart: 16 -> 16, of which waited for: 11 -> 9; matrix products, arithmetic and copies ran while one was open for 0% -> 0% of each run, Pallas kernels for 4% -> 4%
where the time goes in v6:
time: 183 us; the launch traced here: 182 us
  starting transfers between devices  84.1 us (46%)
  waiting for transfers between devices  45.2 us (25%)
  blocking collectives  38.5 us (21%)
  Pallas kernels  13.3 us (7%)
    ppermute x4, starting transfers between devices, to_window(): return lax.ppermute(value, PLANE + RING, pairs)  28.6 us
    ppermute x6, starting transfers between devices, along_ring(): return lax.ppermute(value, RING, pairs)  26.3 us
    all_gather x1, blocking collectives, body(): rows = lax.all_gather(rows, 'za', axis=0, tiled=True)  22 us
    ppermute x4, starting transfers between devices, shift(): lax.ppermute(value, 'za', [(i, (i + step) % QUAD) for i in range(QUAD)])  19.5 us
    ppermute x4, waiting for transfers between devices, shift(): lax.ppermute(value, 'za', [(i, (i + step) % QUAD) for i in range(QUAD)])  16.2 us
    ppermute x4, waiting for transfers between devices, to_window(): return lax.ppermute(value, PLANE + RING, pairs)  16.1 us
    all_to_all x1, blocking collectives, body(): home = lax.all_to_all(home, PLANE, split_axis=0, concat_axis=0, tiled=True)  14.1 us
    pallas_call x12, Pallas kernels, kernel_call(): pl.pallas_call(kernel, out_shape=tuple(outs), in_specs=[pl.BlockSpec(memo...  8.98 us
  transfers between devices with their start and end apart: 16, of which 9 were waited for; matrix products, arithmetic and copies ran while one was open for 0% of the time, Pallas kernels for 4%

profile of v6, /device:TPU:16, one launch (start us, length us, event | category | flops | bytes accessed | tf_op | source)
XLA Modules:
  0.0 182.3 jit_solution(15299596204523775662)
XLA Ops:
  0.6 1.7 shard_map.189
  2.4 11.7 %collective-permute-start = (bf16[144,256]{1,0:T(8,128)(2,1)}, bf16[144,256]{1,0:T(8,128)(2,1)S(1)}, u32[]{:S(2)}, u32[]{:S(2)}) collective-permute-start(bf16[144,256]{1,0:T(8,128)(2,1)} %get-tuple-element.35), channel_id=1, source_target_pairs={{0,412},{1,5},{2,414},{3,415},{4,0},{5,1},{6,2},{7,3},{8,28},{9,13... | collective-permute-start | bytes 221192 | tf_op jit(solution)/shard_map/ppermute | solution.py:68
  14.1 5.4 %collective-permute-start.1 = (bf16[144,256]{1,0:T(8,128)(2,1)}, bf16[144,256]{1,0:T(8,128)(2,1)S(1)}, u32[]{:S(2)}, u32[]{:S(2)}) collective-permute-start(bf16[144,256]{1,0:T(8,128)(2,1)} %get-tuple-element.36), channel_id=1, source_target_pairs={{0,5},{1,412},{2,415},{3,414},{4,1},{5,0},{6,3},{7,2},{8,133},{9,2... | collective-permute-start | bytes 221192 | tf_op jit(solution)/shard_map/ppermute | solution.py:68
  19.5 2.6 %shard_map.188.w0 = bf16[128,2304]{1,0:T(8,128)(2,1)} custom-call(bf16[1,128,768]{2,1,0:T(8,128)(2,1)} %refs_0_.1, bf16[1,128,768]{2,1,0:T(8,128)(2,1)} %refs_1_.1, bf16[1,128,768]{2,1,0:T(8,128)(2,1)} %ng.1, bf16[1,128,768]{2,1,0:T(8,128)(2,1)} %refs_3_.2, bf16[1,128,768]{2,1,0:T(8,128)(2,1)} %refs_4_.1, bf16[1,128,768]{2,1,0:T(8,128)(2,1)} %nu.1, ...), custom_call_target="tpu_custom_call" | custom-call | tf_op jit(solution)/shard_map/pallas_call | solution.py:406
  22.1 7.3 %collective-permute-done.1.cross = bf16[144,256]{1,0:T(8,128)(2,1)S(1)} collective-permute-done((bf16[144,256]{1,0:T(8,128)(2,1)}, bf16[144,256]{1,0:T(8,128)(2,1)S(1)}, u32[]{:S(2)}, u32[]{:S(2)}) %collective-permute-start.1) | collective-permute-done | bytes 73760 | tf_op jit(solution)/shard_map/ppermute | solution.py:68
  29.5 6.1 %collective-permute-start.4 = (bf16[128,2304]{1,0:T(8,128)(2,1)}, bf16[128,2304]{1,0:T(8,128)(2,1)S(1)}, u32[]{:S(2)}, u32[]{:S(2)}) collective-permute-start(bf16[128,2304]{1,0:T(8,128)(2,1)} %shard_map.188.w0), channel_id=1, source_target_pairs={{0,28},{1,5},{2,30},{3,7},{4,0},{5,9},{6,2},{7,11},{8,4},{9,13},{1... | collective-permute-start | bytes 1769480 | tf_op jit(solution)/shard_map/ppermute | solution.py:43
  35.6 4.7 %collective-permute-start.3 = (bf16[128,2304]{1,0:T(8,128)(2,1)}, bf16[128,2304]{1,0:T(8,128)(2,1)S(1)}, u32[]{:S(2)}, u32[]{:S(2)}) collective-permute-start(bf16[128,2304]{1,0:T(8,128)(2,1)} %shard_map.188.w0), channel_id=1, source_target_pairs={{0,2},{1,3},{2,4},{3,5},{4,6},{5,7},{6,8},{7,9},{8,10},{9,11},{10,... | collective-permute-start | bytes 1769480 | tf_op jit(solution)/shard_map/ppermute | solution.py:43
  40.2 4.4 %collective-permute-start.2 = (bf16[128,2304]{1,0:T(8,128)(2,1)}, bf16[128,2304]{1,0:T(8,128)(2,1)S(1)}, u32[]{:S(2)}, u32[]{:S(2)}) collective-permute-start(bf16[128,2304]{1,0:T(8,128)(2,1)} %shard_map.188.w0), channel_id=1, source_target_pairs={{0,30},{1,31},{2,0},{3,1},{4,2},{5,3},{6,4},{7,5},{8,6},{9,7},{10,... | collective-permute-start | bytes 1769480 | tf_op jit(solution)/shard_map/ppermute | solution.py:43
  45.7 7.8 %all-to-all-start = ((bf16[16,2,24,256]{3,2,1,0:T(8,128)(2,1)}), bf16[16,2,24,256]{3,2,1,0:T(8,128)(2,1)S(1)}, u32[]{:S(2)}, u32[]{:S(2)}) async-start(bf16[16,2,24,256]{3,2,1,0:T(8,128)(2,1)} %shard_map.190), calls=%async_computation | async-start | bytes 786432 | tf_op jit(solution)/shard_map/all_to_all | solution.py:444
  53.5 8.0 %all-to-all-done.got = bf16[16,2,24,256]{3,2,1,0:T(8,128)(2,1)S(1)} async-done(((bf16[16,2,24,256]{3,2,1,0:T(8,128)(2,1)}), bf16[16,2,24,256]{3,2,1,0:T(8,128)(2,1)S(1)}, u32[]{:S(2)}, u32[]{:S(2)}) %all-to-all-start) | async-done | bytes 393248 | tf_op jit(solution)/shard_map/all_to_all | solution.py:444
  62.1 3.2 %collective-permute-done.2.w1 = bf16[128,2304]{1,0:T(8,128)(2,1)S(1)} collective-permute-done((bf16[128,2304]{1,0:T(8,128)(2,1)}, bf16[128,2304]{1,0:T(8,128)(2,1)S(1)}, u32[]{:S(2)}, u32[]{:S(2)}) %collective-permute-start.2) | collective-permute-done | bytes 589856 | tf_op jit(solution)/shard_map/ppermute | solution.py:43
  66.0 1.9 %collective-permute-start.5 = (bf16[4,24,2304]{2,1,0:T(8,128)(2,1)S(1)}, bf16[4,24,2304]{2,1,0:T(8,128)(2,1)S(1)}, u32[]{:S(2)}, u32[]{:S(2)}) collective-permute-start(bf16[4,24,2304]{2,1,0:T(8,128)(2,1)S(1)} %shard_map.192), channel_id=1, source_target_pairs={{0,1},{1,0},{2,3},{3,2},{4,5},{5,4},{6,7},{7,6},{8,9},{9,8},{10,11... | collective-permute-start | bytes 1327112 | tf_op jit(solution)/shard_map/ppermute | solution.py:462
  68.0 1.7 collective-permute-done.5.other
  69.7 1.3 shard_map.193
  70.9 5.8 %collective-permute-start.6 = (bf16[24,1152]{1,0:T(8,128)(2,1)S(1)}, bf16[24,1152]{1,0:T(8,128)(2,1)S(1)}, u32[]{:S(2)}, u32[]{:S(2)}) collective-permute-start(bf16[24,1152]{1,0:T(8,128)(2,1)S(1)} %get-tuple-element.43), channel_id=1, source_target_pairs={{0,8},{8,16},{16,24},{24,0},{1,9},{9,17},{17,25},{25,1},{2,10},{10... | collective-permute-start | bytes 165896 | tf_op jit(solution)/shard_map/ppermute | solution.py:33
  76.7 4.0 %collective-permute-start.7 = (bf16[24,1152]{1,0:T(8,128)(2,1)S(1)}, bf16[24,1152]{1,0:T(8,128)(2,1)S(1)}, u32[]{:S(2)}, u32[]{:S(2)}) collective-permute-start(bf16[24,1152]{1,0:T(8,128)(2,1)S(1)} %get-tuple-element.44), channel_id=1, source_target_pairs={{0,24},{8,0},{16,8},{24,16},{1,25},{9,1},{17,9},{25,17},{2,26},{10... | collective-permute-start | bytes 165896 | tf_op jit(solution)/shard_map/ppermute | solution.py:33
  80.7 2.7 %collective-permute-done.6.from_left = bf16[24,1152]{1,0:T(8,128)(2,1)S(1)} collective-permute-done((bf16[24,1152]{1,0:T(8,128)(2,1)S(1)}, bf16[24,1152]{1,0:T(8,128)(2,1)S(1)}, u32[]{:S(2)}, u32[]{:S(2)}) %collective-permute-start.6) | collective-permute-done | bytes 55328 | tf_op jit(solution)/shard_map/ppermute | solution.py:33
  83.4 4.3 %collective-permute-done.7.from_right = bf16[24,1152]{1,0:T(8,128)(2,1)S(1)} collective-permute-done((bf16[24,1152]{1,0:T(8,128)(2,1)S(1)}, bf16[24,1152]{1,0:T(8,128)(2,1)S(1)}, u32[]{:S(2)}, u32[]{:S(2)}) %collective-permute-start.7) | collective-permute-done | bytes 55328 | tf_op jit(solution)/shard_map/ppermute | solution.py:33
  87.7 5.1 %collective-permute-start.8 = (bf16[24,2304]{1,0:T(8,128)(2,1)S(1)}, bf16[24,2304]{1,0:T(8,128)(2,1)S(1)}, u32[]{:S(2)}, u32[]{:S(2)}) collective-permute-start(bf16[24,2304]{1,0:T(8,128)(2,1)S(1)} %get-tuple-element.45), channel_id=1, source_target_pairs={{0,8},{8,16},{16,24},{24,0},{1,9},{9,17},{17,25},{25,1},{2,10},{10... | collective-permute-start | bytes 331784 | tf_op jit(solution)/shard_map/ppermute | solution.py:33
  92.9 4.6 %collective-permute-start.9 = (bf16[24,2304]{1,0:T(8,128)(2,1)S(1)}, bf16[24,2304]{1,0:T(8,128)(2,1)S(1)}, u32[]{:S(2)}, u32[]{:S(2)}) collective-permute-start(bf16[24,2304]{1,0:T(8,128)(2,1)S(1)} %get-tuple-element.46), channel_id=1, source_target_pairs={{0,24},{8,0},{16,8},{24,16},{1,25},{9,1},{17,9},{25,17},{2,26},{10... | collective-permute-start | bytes 331784 | tf_op jit(solution)/shard_map/ppermute | solution.py:33
  97.5 6.5 %collective-permute-done.8.from_left = bf16[24,2304]{1,0:T(8,128)(2,1)S(1)} collective-permute-done((bf16[24,2304]{1,0:T(8,128)(2,1)S(1)}, bf16[24,2304]{1,0:T(8,128)(2,1)S(1)}, u32[]{:S(2)}, u32[]{:S(2)}) %collective-permute-start.8) | collective-permute-done | bytes 110624 | tf_op jit(solution)/shard_map/ppermute | solution.py:33
  104.1 2.7 %collective-permute-done.9.from_right = bf16[24,2304]{1,0:T(8,128)(2,1)S(1)} collective-permute-done((bf16[24,2304]{1,0:T(8,128)(2,1)S(1)}, bf16[24,2304]{1,0:T(8,128)(2,1)S(1)}, u32[]{:S(2)}, u32[]{:S(2)}) %collective-permute-start.9) | collective-permute-done | bytes 110624 | tf_op jit(solution)/shard_map/ppermute | solution.py:33
  106.8 22.0 %all_gather.6 = bf16[96,2304]{1,0:T(8,128)(2,1)S(1)} all-gather(bf16[24,2304]{1,0:T(8,128)(2,1)S(1)} %shard_map.195), channel_id=1, replica_groups=mesh['y'=4,'x'=4,'za'=4,'zb'=4,'core'=2] {'za'}, dimensions={0}, use_global_device_ids=true | all-gather | bytes 552960 | tf_op jit(solution)/shard_map/all_gather | solution.py:484
  128.8 2.4 %all_gather.7.rows = bf16[192,2304]{1,0:T(8,128)(2,1)S(1)} all-gather(bf16[96,2304]{1,0:T(8,128)(2,1)S(1)} %all_gather.6), channel_id=1, replica_groups=mesh['y'=4,'x'=4,'za'=4,'zb'=4,'core'=2] {'core'}, dimensions={0}, use_global_device_ids=true | all-gather | bytes 1327104 | tf_op jit(solution)/shard_map/all_gather | solution.py:485
  132.1 1.9 %collective-permute-start.12 = (bf16[128,2304]{1,0:T(8,128)(2,1)S(1)}, bf16[128,2304]{1,0:T(8,128)(2,1)S(1)}, u32[]{:S(2)}, u32[]{:S(2)}) collective-permute-start(bf16[128,2304]{1,0:T(8,128)(2,1)S(1)} %get-tuple-element.51), channel_id=1, source_target_pairs={{0,2},{1,3},{2,4},{3,5},{4,6},{5,7},{6,8},{7,9},{8,10},{9,11},{10,... | collective-permute-start | bytes 1769480 | tf_op jit(solution)/shard_map/ppermute | solution.py:43
  134.0 5.7 %collective-permute-start.13 = (bf16[128,2304]{1,0:T(8,128)(2,1)S(1)}, bf16[128,2304]{1,0:T(8,128)(2,1)S(1)}, u32[]{:S(2)}, u32[]{:S(2)}) collective-permute-start(bf16[128,2304]{1,0:T(8,128)(2,1)S(1)} %get-tuple-element.52), channel_id=1, source_target_pairs={{0,30},{1,31},{2,0},{3,1},{4,2},{5,3},{6,4},{7,5},{8,6},{9,7},{10,... | collective-permute-start | bytes 1769480 | tf_op jit(solution)/shard_map/ppermute | solution.py:43
  139.7 3.5 %collective-permute-start.14 = (bf16[128,2304]{1,0:T(8,128)(2,1)S(1)}, bf16[128,2304]{1,0:T(8,128)(2,1)S(1)}, u32[]{:S(2)}, u32[]{:S(2)}) collective-permute-start(bf16[128,2304]{1,0:T(8,128)(2,1)S(1)} %get-tuple-element.47.rest_0_), channel_id=1, source_target_pairs={{0,4},{1,29},{2,6},{3,31},{4,8},{5,1},{6,10},{7,3},{8,12},{9,5},{1... | collective-permute-start | bytes 1769480 | tf_op jit(solution)/shard_map/ppermute | solution.py:43
  145.0 14.1 %all_to_all.10.home = bf16[16,2,24,256]{3,2,1,0:T(8,128)(2,1)S(1)} all-to-all(bf16[16,2,24,256]{3,2,1,0:T(8,128)(2,1)S(1)} %shard_map.198), channel_id=1, replica_groups=mesh['y'=4,'x'=4,'za'=4,'zb'=4,'core'=2] {'y','x'}, dimensions={0} | all-to-all | bytes 786432 | tf_op jit(solution)/shard_map/all_to_all | solution.py:513
  159.6 9.6 %collective-permute-start.10 = (bf16[128,256]{1,0:T(8,128)(2,1)S(1)}, bf16[128,256]{1,0:T(8,128)(2,1)S(1)}, u32[]{:S(2)}, u32[]{:S(2)}) collective-permute-start(bf16[128,256]{1,0:T(8,128)(2,1)S(1)} %get-tuple-element.48), channel_id=1, source_target_pairs={{412,0},{5,1},{414,2},{415,3},{0,4},{1,5},{2,6},{3,7},{28,8},{133,... | collective-permute-start | bytes 196616 | tf_op jit(solution)/shard_map/ppermute | solution.py:68
  169.1 1.9 %collective-permute-start.11 = (bf16[128,256]{1,0:T(8,128)(2,1)S(1)}, bf16[128,256]{1,0:T(8,128)(2,1)S(1)}, u32[]{:S(2)}, u32[]{:S(2)}) collective-permute-start(bf16[128,256]{1,0:T(8,128)(2,1)S(1)} %get-tuple-element.49), channel_id=1, source_target_pairs={{5,0},{412,1},{415,2},{414,3},{1,4},{0,5},{3,6},{2,7},{133,8},{28,... | collective-permute-start | bytes 196616 | tf_op jit(solution)/shard_map/ppermute | solution.py:68
  171.1 1.7 shard_map.200
  172.8 8.8 %collective-permute-done.11.cross = bf16[128,256]{1,0:T(8,128)(2,1)S(1)} collective-permute-done((bf16[128,256]{1,0:T(8,128)(2,1)S(1)}, bf16[128,256]{1,0:T(8,128)(2,1)S(1)}, u32[]{:S(2)}, u32[]{:S(2)}) %collective-permute-start.11) | collective-permute-done | bytes 65568 | tf_op jit(solution)/shard_map/ppermute | solution.py:68
  (27 shorter events, 6.2 us)
Async XLA Ops:
  2.4 19.8 %collective-permute-start = (bf16[144,256]{1,0:T(8,128)(2,1)}, bf16[144,256]{1,0:T(8,128)(2,1)S(1)}, u32[]{:S(2)}, u32[]{:S(2)}) collective-permute-start(bf16[144,256]{1,0:T(8,128)(2,1)} %get-tuple-element.35), channel_id=1, source_target_pairs={{0,412},{1,5},{2,414},{3,415},{4,0},{5,1},{6,2},{7,3},{8,28},{9,13... | collective-permute-start | bytes 221192 | tf_op jit(solution)/shard_map/ppermute | solution.py:68
  14.1 15.4 %collective-permute-start.1 = (bf16[144,256]{1,0:T(8,128)(2,1)}, bf16[144,256]{1,0:T(8,128)(2,1)S(1)}, u32[]{:S(2)}, u32[]{:S(2)}) collective-permute-start(bf16[144,256]{1,0:T(8,128)(2,1)} %get-tuple-element.36), channel_id=1, source_target_pairs={{0,5},{1,412},{2,415},{3,414},{4,1},{5,0},{6,3},{7,2},{8,133},{9,2... | collective-permute-start | bytes 221192 | tf_op jit(solution)/shard_map/ppermute | solution.py:68
  22.1 43.2 %copy-start = (bf16[128,2304]{1,0:T(8,128)(2,1)S(1)}, bf16[128,2304]{1,0:T(8,128)(2,1)}, u32[]{:S(2)}) copy-start(bf16[128,2304]{1,0:T(8,128)(2,1)} %shard_map.188.w0) | copy-start | bytes 1769476
  29.5 32.7 %collective-permute-start.4 = (bf16[128,2304]{1,0:T(8,128)(2,1)}, bf16[128,2304]{1,0:T(8,128)(2,1)S(1)}, u32[]{:S(2)}, u32[]{:S(2)}) collective-permute-start(bf16[128,2304]{1,0:T(8,128)(2,1)} %shard_map.188.w0), channel_id=1, source_target_pairs={{0,28},{1,5},{2,30},{3,7},{4,0},{5,9},{6,2},{7,11},{8,4},{9,13},{1... | collective-permute-start | bytes 1769480 | tf_op jit(solution)/shard_map/ppermute | solution.py:43
  35.6 26.6 %collective-permute-start.3 = (bf16[128,2304]{1,0:T(8,128)(2,1)}, bf16[128,2304]{1,0:T(8,128)(2,1)S(1)}, u32[]{:S(2)}, u32[]{:S(2)}) collective-permute-start(bf16[128,2304]{1,0:T(8,128)(2,1)} %shard_map.188.w0), channel_id=1, source_target_pairs={{0,2},{1,3},{2,4},{3,5},{4,6},{5,7},{6,8},{7,9},{8,10},{9,11},{10,... | collective-permute-start | bytes 1769480 | tf_op jit(solution)/shard_map/ppermute | solution.py:43
  40.2 25.1 %collective-permute-start.2 = (bf16[128,2304]{1,0:T(8,128)(2,1)}, bf16[128,2304]{1,0:T(8,128)(2,1)S(1)}, u32[]{:S(2)}, u32[]{:S(2)}) collective-permute-start(bf16[128,2304]{1,0:T(8,128)(2,1)} %shard_map.188.w0), channel_id=1, source_target_pairs={{0,30},{1,31},{2,0},{3,1},{4,2},{5,3},{6,4},{7,5},{8,6},{9,7},{10,... | collective-permute-start | bytes 1769480 | tf_op jit(solution)/shard_map/ppermute | solution.py:43
  45.7 15.8 %all-to-all-start = ((bf16[16,2,24,256]{3,2,1,0:T(8,128)(2,1)}), bf16[16,2,24,256]{3,2,1,0:T(8,128)(2,1)S(1)}, u32[]{:S(2)}, u32[]{:S(2)}) async-start(bf16[16,2,24,256]{3,2,1,0:T(8,128)(2,1)} %shard_map.190), calls=%async_computation | async-start | bytes 786432 | tf_op jit(solution)/shard_map/all_to_all | solution.py:444
  66.0 3.7 %collective-permute-start.5 = (bf16[4,24,2304]{2,1,0:T(8,128)(2,1)S(1)}, bf16[4,24,2304]{2,1,0:T(8,128)(2,1)S(1)}, u32[]{:S(2)}, u32[]{:S(2)}) collective-permute-start(bf16[4,24,2304]{2,1,0:T(8,128)(2,1)S(1)} %shard_map.192), channel_id=1, source_target_pairs={{0,1},{1,0},{2,3},{3,2},{4,5},{5,4},{6,7},{7,6},{8,9},{9,8},{10,11... | collective-permute-start | bytes 1327112 | tf_op jit(solution)/shard_map/ppermute | solution.py:462
  70.9 12.4 %collective-permute-start.6 = (bf16[24,1152]{1,0:T(8,128)(2,1)S(1)}, bf16[24,1152]{1,0:T(8,128)(2,1)S(1)}, u32[]{:S(2)}, u32[]{:S(2)}) collective-permute-start(bf16[24,1152]{1,0:T(8,128)(2,1)S(1)} %get-tuple-element.43), channel_id=1, source_target_pairs={{0,8},{8,16},{16,24},{24,0},{1,9},{9,17},{17,25},{25,1},{2,10},{10... | collective-permute-start | bytes 165896 | tf_op jit(solution)/shard_map/ppermute | solution.py:33
  76.7 11.0 %collective-permute-start.7 = (bf16[24,1152]{1,0:T(8,128)(2,1)S(1)}, bf16[24,1152]{1,0:T(8,128)(2,1)S(1)}, u32[]{:S(2)}, u32[]{:S(2)}) collective-permute-start(bf16[24,1152]{1,0:T(8,128)(2,1)S(1)} %get-tuple-element.44), channel_id=1, source_target_pairs={{0,24},{8,0},{16,8},{24,16},{1,25},{9,1},{17,9},{25,17},{2,26},{10... | collective-permute-start | bytes 165896 | tf_op jit(solution)/shard_map/ppermute | solution.py:33
  87.7 16.3 %collective-permute-start.8 = (bf16[24,2304]{1,0:T(8,128)(2,1)S(1)}, bf16[24,2304]{1,0:T(8,128)(2,1)S(1)}, u32[]{:S(2)}, u32[]{:S(2)}) collective-permute-start(bf16[24,2304]{1,0:T(8,128)(2,1)S(1)} %get-tuple-element.45), channel_id=1, source_target_pairs={{0,8},{8,16},{16,24},{24,0},{1,9},{9,17},{17,25},{25,1},{2,10},{10... | collective-permute-start | bytes 331784 | tf_op jit(solution)/shard_map/ppermute | solution.py:33
  92.9 13.9 %collective-permute-start.9 = (bf16[24,2304]{1,0:T(8,128)(2,1)S(1)}, bf16[24,2304]{1,0:T(8,128)(2,1)S(1)}, u32[]{:S(2)}, u32[]{:S(2)}) collective-permute-start(bf16[24,2304]{1,0:T(8,128)(2,1)S(1)} %get-tuple-element.46), channel_id=1, source_target_pairs={{0,24},{8,0},{16,8},{24,16},{1,25},{9,1},{17,9},{25,17},{2,26},{10... | collective-permute-start | bytes 331784 | tf_op jit(solution)/shard_map/ppermute | solution.py:33
  132.1 39.0 %collective-permute-start.12 = (bf16[128,2304]{1,0:T(8,128)(2,1)S(1)}, bf16[128,2304]{1,0:T(8,128)(2,1)S(1)}, u32[]{:S(2)}, u32[]{:S(2)}) collective-permute-start(bf16[128,2304]{1,0:T(8,128)(2,1)S(1)} %get-tuple-element.51), channel_id=1, source_target_pairs={{0,2},{1,3},{2,4},{3,5},{4,6},{5,7},{6,8},{7,9},{8,10},{9,11},{10,... | collective-permute-start | bytes 1769480 | tf_op jit(solution)/shard_map/ppermute | solution.py:43
  134.0 37.1 %collective-permute-start.13 = (bf16[128,2304]{1,0:T(8,128)(2,1)S(1)}, bf16[128,2304]{1,0:T(8,128)(2,1)S(1)}, u32[]{:S(2)}, u32[]{:S(2)}) collective-permute-start(bf16[128,2304]{1,0:T(8,128)(2,1)S(1)} %get-tuple-element.52), channel_id=1, source_target_pairs={{0,30},{1,31},{2,0},{3,1},{4,2},{5,3},{6,4},{7,5},{8,6},{9,7},{10,... | collective-permute-start | bytes 1769480 | tf_op jit(solution)/shard_map/ppermute | solution.py:43
  139.7 31.4 %collective-permute-start.14 = (bf16[128,2304]{1,0:T(8,128)(2,1)S(1)}, bf16[128,2304]{1,0:T(8,128)(2,1)S(1)}, u32[]{:S(2)}, u32[]{:S(2)}) collective-permute-start(bf16[128,2304]{1,0:T(8,128)(2,1)S(1)} %get-tuple-element.47.rest_0_), channel_id=1, source_target_pairs={{0,4},{1,29},{2,6},{3,31},{4,8},{5,1},{6,10},{7,3},{8,12},{9,5},{1... | collective-permute-start | bytes 1769480 | tf_op jit(solution)/shard_map/ppermute | solution.py:43
  144.3 26.8 %copy-start.1 = (bf16[1,128,768]{2,1,0:T(8,128)(2,1)S(1)}, bf16[1,128,768]{2,1,0:T(8,128)(2,1)}, u32[]{:S(2)}) copy-start(bf16[1,128,768]{2,1,0:T(8,128)(2,1)} %ng.1) | copy-start | bytes 589828
  144.3 26.8 %copy-start.2 = (bf16[1,128,768]{2,1,0:T(8,128)(2,1)S(1)}, bf16[1,128,768]{2,1,0:T(8,128)(2,1)}, u32[]{:S(2)}) copy-start(bf16[1,128,768]{2,1,0:T(8,128)(2,1)} %nu.1) | copy-start | bytes 589828
  144.3 26.8 %copy-start.3 = (bf16[1,768,128]{2,1,0:T(8,128)(2,1)S(1)}, bf16[1,768,128]{2,1,0:T(8,128)(2,1)}, u32[]{:S(2)}) copy-start(bf16[1,768,128]{2,1,0:T(8,128)(2,1)} %nd.1) | copy-start | bytes 589828
  159.6 13.3 %collective-permute-start.10 = (bf16[128,256]{1,0:T(8,128)(2,1)S(1)}, bf16[128,256]{1,0:T(8,128)(2,1)S(1)}, u32[]{:S(2)}, u32[]{:S(2)}) collective-permute-start(bf16[128,256]{1,0:T(8,128)(2,1)S(1)} %get-tuple-element.48), channel_id=1, source_target_pairs={{412,0},{5,1},{414,2},{415,3},{0,4},{1,5},{2,6},{3,7},{28,8},{133,... | collective-permute-start | bytes 196616 | tf_op jit(solution)/shard_map/ppermute | solution.py:68
  169.1 12.5 %collective-permute-start.11 = (bf16[128,256]{1,0:T(8,128)(2,1)S(1)}, bf16[128,256]{1,0:T(8,128)(2,1)S(1)}, u32[]{:S(2)}, u32[]{:S(2)}) collective-permute-start(bf16[128,256]{1,0:T(8,128)(2,1)S(1)} %get-tuple-element.49), channel_id=1, source_target_pairs={{5,0},{412,1},{415,2},{414,3},{1,4},{0,5},{3,6},{2,7},{133,8},{28,... | collective-permute-start | bytes 196616 | tf_op jit(solution)/shard_map/ppermute | solution.py:68

commit v7 on v6

--- a/solution.py
+++ b/solution.py
@@ -253,10 +253,10 @@
 
 
 def split_kernel(
-    where, slots, w0, w1, w2, w3, other, far_right, far_left, own, ahead, behind, mine
+    where, slots, w0, w1, w2, w3, other, far, behind, own, ahead, mine
 ):
     quads, cap, width = other.shape[0], other.shape[1], w0.shape[1] // 3
-    core, me, cut = where[0], where[1], far_right.shape[1]
+    core, me = where[0], where[1]
     for part in range(3):
         lanes = slice(part * width, (part + 1) * width)
         total = partial_sum(slots, (w0, w1, w2, w3), core, quads * cap, part)
@@ -265,23 +265,17 @@
                 quad, :, lanes
             ].astype(F32)
 
-    def piece(step, lanes):
-        return mine[jnp.bitwise_and(me + step, QUAD - 1), :, lanes]
-
-    whole = slice(0, 2 * cut)
-    far_right[...] = piece(2, slice(0, cut)).astype(BF)
-    far_left[...] = piece(2, slice(cut, 2 * cut)).astype(BF)
-    own[...] = piece(0, whole)
-    ahead[...] = piece(1, whole)
-    behind[...] = piece(3, whole)
-
-
-def relay_kernel(ahead, behind, from_left, from_right, to_right, to_left):
-    cut = from_left.shape[1]
-    to_right[:, :cut] = (ahead[:, :cut] + from_left[...].astype(F32)).astype(BF)
-    to_right[:, cut:] = ahead[:, cut:].astype(BF)
-    to_left[:, :cut] = behind[:, :cut].astype(BF)
-    to_left[:, cut:] = (behind[:, cut:] + from_right[...].astype(F32)).astype(BF)
+    def piece(step):
+        return mine[jnp.bitwise_and(me + step, QUAD - 1)]
+
+    far[...] = piece(2).astype(BF)
+    behind[...] = piece(3).astype(BF)
+    own[...] = piece(0)
+    ahead[...] = piece(1)
+
+
+def relay_kernel(ahead, from_left, to_right):
+    to_right[...] = (ahead[...] + from_left[...].astype(F32)).astype(BF)
 
 
 def activate_kernel(own, from_left, from_right, out):
@@ -460,13 +454,11 @@
         scalars=1,
     )
     other = lax.ppermute(other, "core", [(0, 1), (1, 0)])
-    cut = 3 * width // 2
     total = jax.ShapeDtypeStruct((cap, 3 * width), F32)
     wire = jax.ShapeDtypeStruct((cap, 3 * width), BF)
-    half_wire = jax.ShapeDtypeStruct((cap, cut), BF)
-    far_right, far_left, own, ahead, behind = kernel_call(
+    far, behind, own, ahead = kernel_call(
         split_kernel,
-        [half_wire] * 2 + [total] * 3,
+        [wire] * 2 + [total] * 2,
         jnp.concatenate([core, me]),
         slots,
         *weights,
@@ -474,12 +466,9 @@
         scalars=1,
         scratch=[pltpu.VMEM((QUAD, cap, 3 * width), F32)],
     )
-    to_right, to_left = kernel_call(
-        relay_kernel, [wire] * 2, ahead, behind, shift(far_right, 1), shift(far_left, -1)
-    )
-    (rows,) = kernel_call(
-        activate_kernel, [wire], own, shift(to_right, 1), shift(to_left, -1)
-    )
+    from_right = shift(behind, -1)
+    (to_right,) = kernel_call(relay_kernel, [wire], ahead, shift(far, 1))
+    (rows,) = kernel_call(activate_kernel, [wire], own, shift(to_right, 1), from_right)
 
     rows = lax.all_gather(rows, "za", axis=0, tiled=True)
     rows = lax.all_gather(rows, "core", axis=0, tiled=True)
@@ -494,13 +483,6 @@
         slots,
         rows,
     )
-    w_grads = (
-        w_sent[0],
-        along_ring(w_sent[1], (1, 1)),
-        along_ring(w_sent[2], (-1, -1)),
-        along_ring(w_sent[3], (2, -2)),
-    )
-
     (home,) = kernel_call(
         collect_kernel,
         [jax.ShapeDtypeStruct((experts, 2, cap, 2 * half), BF)],
@@ -510,6 +492,14 @@
         scalars=1,
         free=1,
     )
+    last_sent, home = lax.optimization_barrier((w_sent[3], home))
+    w_grads = (
+        w_sent[0],
+        along_ring(w_sent[1], (1, 1)),
+        along_ring(w_sent[2], (-1, -1)),
+        along_ring(last_sent, (2, -2)),
+    )
+
     home = lax.all_to_all(home, PLANE, split_axis=0, concat_axis=0, tiled=True)
     ready = kernel_call(
         combine_kernel,

time: 183 us -> 178 us (0.973)
  the two profiles are of different devices: /device:TPU:16 before, /device:TPU:11 now
where the time goes in v7:
time: 178 us
  starting transfers between devices  77 us (43%)
  blocking collectives  44.8 us (25%)
  waiting for transfers between devices  41.4 us (23%)
  Pallas kernels  13.3 us (7%)
    ppermute x4, starting transfers between devices, to_window(): return lax.ppermute(value, PLANE + RING, pairs)  30 us
    all_gather x1, blocking collectives, body(): rows = lax.all_gather(rows, 'za', axis=0, tiled=True)  28.4 us
    ppermute x6, starting transfers between devices, along_ring(): return lax.ppermute(value, RING, pairs)  24.5 us
    ppermute x3, waiting for transfers between devices, shift(): lax.ppermute(value, 'za', [(i, (i + step) % QUAD) for i in range(QUAD)])  15.4 us
    ppermute x4, waiting for transfers between devices, to_window(): return lax.ppermute(value, PLANE + RING, pairs)  14.3 us
    all_to_all x1, blocking collectives, body(): home = lax.all_to_all(home, PLANE, split_axis=0, concat_axis=0, tiled=True)  13.7 us
    ppermute x3, starting transfers between devices, shift(): lax.ppermute(value, 'za', [(i, (i + step) % QUAD) for i in range(QUAD)])  11.5 us
    all_to_all x1, starting transfers between devices, body(): got = lax.all_to_all(send, PLANE, split_axis=0, concat_axis=0, tiled=True)  9.15 us
  transfers between devices with their start and end apart: 15, of which 9 were waited for; matrix products, arithmetic and copies ran while one was open for 0% of the time, Pallas kernels for 4%

profile of v7, /device:TPU:11, one launch (start us, length us, event | category | flops | bytes accessed | tf_op | source)
XLA Modules:
  0.0 177.6 jit_solution(3433723604399000691)
XLA Ops:
  0.6 1.7 shard_map.189
  2.4 11.5 %collective-permute-start = (bf16[144,256]{1,0:T(8,128)(2,1)}, bf16[144,256]{1,0:T(8,128)(2,1)S(1)}, u32[]{:S(2)}, u32[]{:S(2)}) collective-permute-start(bf16[144,256]{1,0:T(8,128)(2,1)} %get-tuple-element.34), channel_id=1, source_target_pairs={{0,412},{1,5},{2,414},{3,415},{4,0},{5,1},{6,2},{7,3},{8,28},{9,13... | collective-permute-start | bytes 221192 | tf_op jit(solution)/shard_map/ppermute | solution.py:68
  13.9 3.1 %collective-permute-start.1 = (bf16[144,256]{1,0:T(8,128)(2,1)}, bf16[144,256]{1,0:T(8,128)(2,1)S(1)}, u32[]{:S(2)}, u32[]{:S(2)}) collective-permute-start(bf16[144,256]{1,0:T(8,128)(2,1)} %get-tuple-element.35), channel_id=1, source_target_pairs={{0,5},{1,412},{2,415},{3,414},{4,1},{5,0},{6,3},{7,2},{8,133},{9,2... | collective-permute-start | bytes 221192 | tf_op jit(solution)/shard_map/ppermute | solution.py:68
  17.1 2.6 %shard_map.188.w0 = bf16[128,2304]{1,0:T(8,128)(2,1)} custom-call(bf16[1,128,768]{2,1,0:T(8,128)(2,1)} %refs_0_.1, bf16[1,128,768]{2,1,0:T(8,128)(2,1)} %refs_1_.1, bf16[1,128,768]{2,1,0:T(8,128)(2,1)} %ng.1, bf16[1,128,768]{2,1,0:T(8,128)(2,1)} %refs_3_.2, bf16[1,128,768]{2,1,0:T(8,128)(2,1)} %refs_4_.1, bf16[1,128,768]{2,1,0:T(8,128)(2,1)} %nu.1, ...), custom_call_target="tpu_custom_call" | custom-call | tf_op jit(solution)/shard_map/pallas_call | solution.py:400
  19.7 2.8 %collective-permute-done.same = bf16[144,256]{1,0:T(8,128)(2,1)S(1)} collective-permute-done((bf16[144,256]{1,0:T(8,128)(2,1)}, bf16[144,256]{1,0:T(8,128)(2,1)S(1)}, u32[]{:S(2)}, u32[]{:S(2)}) %collective-permute-start) | collective-permute-done | bytes 73760 | tf_op jit(solution)/shard_map/ppermute | solution.py:68
  22.5 4.8 %collective-permute-done.1.cross = bf16[144,256]{1,0:T(8,128)(2,1)S(1)} collective-permute-done((bf16[144,256]{1,0:T(8,128)(2,1)}, bf16[144,256]{1,0:T(8,128)(2,1)S(1)}, u32[]{:S(2)}, u32[]{:S(2)}) %collective-permute-start.1) | collective-permute-done | bytes 73760 | tf_op jit(solution)/shard_map/ppermute | solution.py:68
  27.2 6.5 %collective-permute-start.4 = (bf16[128,2304]{1,0:T(8,128)(2,1)}, bf16[128,2304]{1,0:T(8,128)(2,1)S(1)}, u32[]{:S(2)}, u32[]{:S(2)}) collective-permute-start(bf16[128,2304]{1,0:T(8,128)(2,1)} %shard_map.188.w0), channel_id=1, source_target_pairs={{0,28},{1,5},{2,30},{3,7},{4,0},{5,9},{6,2},{7,11},{8,4},{9,13},{1... | collective-permute-start | bytes 1769480 | tf_op jit(solution)/shard_map/ppermute | solution.py:43
  33.8 1.9 %collective-permute-start.3 = (bf16[128,2304]{1,0:T(8,128)(2,1)}, bf16[128,2304]{1,0:T(8,128)(2,1)S(1)}, u32[]{:S(2)}, u32[]{:S(2)}) collective-permute-start(bf16[128,2304]{1,0:T(8,128)(2,1)} %shard_map.188.w0), channel_id=1, source_target_pairs={{0,2},{1,3},{2,4},{3,5},{4,6},{5,7},{6,8},{7,9},{8,10},{9,11},{10,... | collective-permute-start | bytes 1769480 | tf_op jit(solution)/shard_map/ppermute | solution.py:43
  35.7 7.6 %collective-permute-start.2 = (bf16[128,2304]{1,0:T(8,128)(2,1)}, bf16[128,2304]{1,0:T(8,128)(2,1)S(1)}, u32[]{:S(2)}, u32[]{:S(2)}) collective-permute-start(bf16[128,2304]{1,0:T(8,128)(2,1)} %shard_map.188.w0), channel_id=1, source_target_pairs={{0,30},{1,31},{2,0},{3,1},{4,2},{5,3},{6,4},{7,5},{8,6},{9,7},{10,... | collective-permute-start | bytes 1769480 | tf_op jit(solution)/shard_map/ppermute | solution.py:43
  44.4 9.2 %all-to-all-start = ((bf16[16,2,24,256]{3,2,1,0:T(8,128)(2,1)}), bf16[16,2,24,256]{3,2,1,0:T(8,128)(2,1)S(1)}, u32[]{:S(2)}, u32[]{:S(2)}) async-start(bf16[16,2,24,256]{3,2,1,0:T(8,128)(2,1)} %shard_map.190), calls=%async_computation | async-start | bytes 786432 | tf_op jit(solution)/shard_map/all_to_all | solution.py:438
  53.6 6.2 %all-to-all-done.got = bf16[16,2,24,256]{3,2,1,0:T(8,128)(2,1)S(1)} async-done(((bf16[16,2,24,256]{3,2,1,0:T(8,128)(2,1)}), bf16[16,2,24,256]{3,2,1,0:T(8,128)(2,1)S(1)}, u32[]{:S(2)}, u32[]{:S(2)}) %all-to-all-start) | async-done | bytes 393248 | tf_op jit(solution)/shard_map/all_to_all | solution.py:438
  60.4 3.8 %collective-permute-done.3.w2 = bf16[128,2304]{1,0:T(8,128)(2,1)S(1)} collective-permute-done((bf16[128,2304]{1,0:T(8,128)(2,1)}, bf16[128,2304]{1,0:T(8,128)(2,1)S(1)}, u32[]{:S(2)}, u32[]{:S(2)}) %collective-permute-start.3) | collective-permute-done | bytes 589856 | tf_op jit(solution)/shard_map/ppermute | solution.py:43
  64.9 1.9 %collective-permute-start.5 = (bf16[4,24,2304]{2,1,0:T(8,128)(2,1)S(1)}, bf16[4,24,2304]{2,1,0:T(8,128)(2,1)S(1)}, u32[]{:S(2)}, u32[]{:S(2)}) collective-permute-start(bf16[4,24,2304]{2,1,0:T(8,128)(2,1)S(1)} %shard_map.192), channel_id=1, source_target_pairs={{0,1},{1,0},{2,3},{3,2},{4,5},{5,4},{6,7},{7,6},{8,9},{9,8},{10,11... | collective-permute-start | bytes 1327112 | tf_op jit(solution)/shard_map/ppermute | solution.py:456
  66.9 1.7 collective-permute-done.5.other
  68.6 1.3 shard_map.193
  69.9 2.8 %collective-permute-start.6 = (bf16[24,2304]{1,0:T(8,128)(2,1)S(1)}, bf16[24,2304]{1,0:T(8,128)(2,1)S(1)}, u32[]{:S(2)}, u32[]{:S(2)}) collective-permute-start(bf16[24,2304]{1,0:T(8,128)(2,1)S(1)} %get-tuple-element.41), channel_id=1, source_target_pairs={{0,8},{8,16},{16,24},{24,0},{1,9},{9,17},{17,25},{25,1},{2,10},{10... | collective-permute-start | bytes 331784 | tf_op jit(solution)/shard_map/ppermute | solution.py:33
  72.6 6.4 %collective-permute-start.8 = (bf16[24,2304]{1,0:T(8,128)(2,1)S(1)}, bf16[24,2304]{1,0:T(8,128)(2,1)S(1)}, u32[]{:S(2)}, u32[]{:S(2)}) collective-permute-start(bf16[24,2304]{1,0:T(8,128)(2,1)S(1)} %get-tuple-element.42), channel_id=1, source_target_pairs={{0,24},{8,0},{16,8},{24,16},{1,25},{9,1},{17,9},{25,17},{2,26},{10... | collective-permute-start | bytes 331784 | tf_op jit(solution)/shard_map/ppermute | solution.py:33
  79.1 5.5 %collective-permute-done.6.from_left = bf16[24,2304]{1,0:T(8,128)(2,1)S(1)} collective-permute-done((bf16[24,2304]{1,0:T(8,128)(2,1)S(1)}, bf16[24,2304]{1,0:T(8,128)(2,1)S(1)}, u32[]{:S(2)}, u32[]{:S(2)}) %collective-permute-start.6) | collective-permute-done | bytes 110624 | tf_op jit(solution)/shard_map/ppermute | solution.py:33
  84.6 2.3 %collective-permute-start.7 = (bf16[24,2304]{1,0:T(8,128)(2,1)S(1)}, bf16[24,2304]{1,0:T(8,128)(2,1)S(1)}, u32[]{:S(2)}, u32[]{:S(2)}) collective-permute-start(bf16[24,2304]{1,0:T(8,128)(2,1)S(1)} %shard_map.194), channel_id=1, source_target_pairs={{0,8},{8,16},{16,24},{24,0},{1,9},{9,17},{17,25},{25,1},{2,10},{10... | collective-permute-start | bytes 331784 | tf_op jit(solution)/shard_map/ppermute | solution.py:33
  86.9 3.5 %collective-permute-done.8.from_right = bf16[24,2304]{1,0:T(8,128)(2,1)S(1)} collective-permute-done((bf16[24,2304]{1,0:T(8,128)(2,1)S(1)}, bf16[24,2304]{1,0:T(8,128)(2,1)S(1)}, u32[]{:S(2)}, u32[]{:S(2)}) %collective-permute-start.8) | collective-permute-done | bytes 110624 | tf_op jit(solution)/shard_map/ppermute | solution.py:33
  90.4 6.3 %collective-permute-done.7.from_left = bf16[24,2304]{1,0:T(8,128)(2,1)S(1)} collective-permute-done((bf16[24,2304]{1,0:T(8,128)(2,1)S(1)}, bf16[24,2304]{1,0:T(8,128)(2,1)S(1)}, u32[]{:S(2)}, u32[]{:S(2)}) %collective-permute-start.7) | collective-permute-done | bytes 110624 | tf_op jit(solution)/shard_map/ppermute | solution.py:33
  96.8 28.4 %all_gather.6 = bf16[96,2304]{1,0:T(8,128)(2,1)S(1)} all-gather(bf16[24,2304]{1,0:T(8,128)(2,1)S(1)} %shard_map.195), channel_id=1, replica_groups=mesh['y'=4,'x'=4,'za'=4,'zb'=4,'core'=2] {'za'}, dimensions={0}, use_global_device_ids=true | all-gather | bytes 552960 | tf_op jit(solution)/shard_map/all_gather | solution.py:473
  125.2 2.8 %all_gather.7.rows = bf16[192,2304]{1,0:T(8,128)(2,1)S(1)} all-gather(bf16[96,2304]{1,0:T(8,128)(2,1)S(1)} %all_gather.6), channel_id=1, replica_groups=mesh['y'=4,'x'=4,'za'=4,'zb'=4,'core'=2] {'core'}, dimensions={0}, use_global_device_ids=true | all-gather | bytes 1327104 | tf_op jit(solution)/shard_map/all_gather | solution.py:474
  128.8 1.1 shard_map.197
  130.5 1.9 %collective-permute-start.13 = (bf16[128,2304]{1,0:T(8,128)(2,1)S(1)}, bf16[128,2304]{1,0:T(8,128)(2,1)S(1)}, u32[]{:S(2)}, u32[]{:S(2)}) collective-permute-start(bf16[128,2304]{1,0:T(8,128)(2,1)S(1)} %get-tuple-element.50.rest_0_), channel_id=1, source_target_pairs={{0,4},{1,29},{2,6},{3,31},{4,8},{5,1},{6,10},{7,3},{8,12},{9,5},{1... | collective-permute-start | bytes 1769480 | tf_op jit(solution)/shard_map/ppermute | solution.py:43
  132.4 2.6 %collective-permute-start.11 = (bf16[128,2304]{1,0:T(8,128)(2,1)S(1)}, bf16[128,2304]{1,0:T(8,128)(2,1)S(1)}, u32[]{:S(2)}, u32[]{:S(2)}) collective-permute-start(bf16[128,2304]{1,0:T(8,128)(2,1)S(1)} %get-tuple-element.48), channel_id=1, source_target_pairs={{0,2},{1,3},{2,4},{3,5},{4,6},{5,7},{6,8},{7,9},{8,10},{9,11},{10,... | collective-permute-start | bytes 1769480 | tf_op jit(solution)/shard_map/ppermute | solution.py:43
  135.0 3.9 %collective-permute-start.12 = (bf16[128,2304]{1,0:T(8,128)(2,1)S(1)}, bf16[128,2304]{1,0:T(8,128)(2,1)S(1)}, u32[]{:S(2)}, u32[]{:S(2)}) collective-permute-start(bf16[128,2304]{1,0:T(8,128)(2,1)S(1)} %get-tuple-element.49), channel_id=1, source_target_pairs={{0,30},{1,31},{2,0},{3,1},{4,2},{5,3},{6,4},{7,5},{8,6},{9,7},{10,... | collective-permute-start | bytes 1769480 | tf_op jit(solution)/shard_map/ppermute | solution.py:43
  138.9 13.7 %all_to_all.10.home = bf16[16,2,24,256]{3,2,1,0:T(8,128)(2,1)S(1)} all-to-all(bf16[16,2,24,256]{3,2,1,0:T(8,128)(2,1)S(1)} %shard_map.198), channel_id=1, replica_groups=mesh['y'=4,'x'=4,'za'=4,'zb'=4,'core'=2] {'y','x'}, dimensions={0} | all-to-all | bytes 786432 | tf_op jit(solution)/shard_map/all_to_all | solution.py:503
  153.1 10.7 %collective-permute-start.9 = (bf16[128,256]{1,0:T(8,128)(2,1)S(1)}, bf16[128,256]{1,0:T(8,128)(2,1)S(1)}, u32[]{:S(2)}, u32[]{:S(2)}) collective-permute-start(bf16[128,256]{1,0:T(8,128)(2,1)S(1)} %get-tuple-element.45), channel_id=1, source_target_pairs={{412,0},{5,1},{414,2},{415,3},{0,4},{1,5},{2,6},{3,7},{28,8},{133,... | collective-permute-start | bytes 196616 | tf_op jit(solution)/shard_map/ppermute | solution.py:68
  163.8 4.6 %collective-permute-start.10 = (bf16[128,256]{1,0:T(8,128)(2,1)S(1)}, bf16[128,256]{1,0:T(8,128)(2,1)S(1)}, u32[]{:S(2)}, u32[]{:S(2)}) collective-permute-start(bf16[128,256]{1,0:T(8,128)(2,1)S(1)} %get-tuple-element.46), channel_id=1, source_target_pairs={{5,0},{412,1},{415,2},{414,3},{1,4},{0,5},{3,6},{2,7},{133,8},{28,... | collective-permute-start | bytes 196616 | tf_op jit(solution)/shard_map/ppermute | solution.py:68
  168.5 1.7 shard_map.200
  170.2 6.8 %collective-permute-done.10.cross = bf16[128,256]{1,0:T(8,128)(2,1)S(1)} collective-permute-done((bf16[128,256]{1,0:T(8,128)(2,1)S(1)}, bf16[128,256]{1,0:T(8,128)(2,1)S(1)}, u32[]{:S(2)}, u32[]{:S(2)}) %collective-permute-start.10) | collective-permute-done | bytes 65568 | tf_op jit(solution)/shard_map/ppermute | solution.py:68
  (25 shorter events, 5.1 us)
Async XLA Ops:
  2.4 20.1 %collective-permute-start = (bf16[144,256]{1,0:T(8,128)(2,1)}, bf16[144,256]{1,0:T(8,128)(2,1)S(1)}, u32[]{:S(2)}, u32[]{:S(2)}) collective-permute-start(bf16[144,256]{1,0:T(8,128)(2,1)} %get-tuple-element.34), channel_id=1, source_target_pairs={{0,412},{1,5},{2,414},{3,415},{4,0},{5,1},{6,2},{7,3},{8,28},{9,13... | collective-permute-start | bytes 221192 | tf_op jit(solution)/shard_map/ppermute | solution.py:68
  13.9 13.3 %collective-permute-start.1 = (bf16[144,256]{1,0:T(8,128)(2,1)}, bf16[144,256]{1,0:T(8,128)(2,1)S(1)}, u32[]{:S(2)}, u32[]{:S(2)}) collective-permute-start(bf16[144,256]{1,0:T(8,128)(2,1)} %get-tuple-element.35), channel_id=1, source_target_pairs={{0,5},{1,412},{2,415},{3,414},{4,1},{5,0},{6,3},{7,2},{8,133},{9,2... | collective-permute-start | bytes 221192 | tf_op jit(solution)/shard_map/ppermute | solution.py:68
  19.7 44.6 %copy-start = (bf16[128,2304]{1,0:T(8,128)(2,1)S(1)}, bf16[128,2304]{1,0:T(8,128)(2,1)}, u32[]{:S(2)}) copy-start(bf16[128,2304]{1,0:T(8,128)(2,1)} %shard_map.188.w0) | copy-start | bytes 1769476
  27.2 33.2 %collective-permute-start.4 = (bf16[128,2304]{1,0:T(8,128)(2,1)}, bf16[128,2304]{1,0:T(8,128)(2,1)S(1)}, u32[]{:S(2)}, u32[]{:S(2)}) collective-permute-start(bf16[128,2304]{1,0:T(8,128)(2,1)} %shard_map.188.w0), channel_id=1, source_target_pairs={{0,28},{1,5},{2,30},{3,7},{4,0},{5,9},{6,2},{7,11},{8,4},{9,13},{1... | collective-permute-start | bytes 1769480 | tf_op jit(solution)/shard_map/ppermute | solution.py:43
  33.8 30.5 %collective-permute-start.3 = (bf16[128,2304]{1,0:T(8,128)(2,1)}, bf16[128,2304]{1,0:T(8,128)(2,1)S(1)}, u32[]{:S(2)}, u32[]{:S(2)}) collective-permute-start(bf16[128,2304]{1,0:T(8,128)(2,1)} %shard_map.188.w0), channel_id=1, source_target_pairs={{0,2},{1,3},{2,4},{3,5},{4,6},{5,7},{6,8},{7,9},{8,10},{9,11},{10,... | collective-permute-start | bytes 1769480 | tf_op jit(solution)/shard_map/ppermute | solution.py:43
  35.7 28.6 %collective-permute-start.2 = (bf16[128,2304]{1,0:T(8,128)(2,1)}, bf16[128,2304]{1,0:T(8,128)(2,1)S(1)}, u32[]{:S(2)}, u32[]{:S(2)}) collective-permute-start(bf16[128,2304]{1,0:T(8,128)(2,1)} %shard_map.188.w0), channel_id=1, source_target_pairs={{0,30},{1,31},{2,0},{3,1},{4,2},{5,3},{6,4},{7,5},{8,6},{9,7},{10,... | collective-permute-start | bytes 1769480 | tf_op jit(solution)/shard_map/ppermute | solution.py:43
  44.4 15.4 %all-to-all-start = ((bf16[16,2,24,256]{3,2,1,0:T(8,128)(2,1)}), bf16[16,2,24,256]{3,2,1,0:T(8,128)(2,1)S(1)}, u32[]{:S(2)}, u32[]{:S(2)}) async-start(bf16[16,2,24,256]{3,2,1,0:T(8,128)(2,1)} %shard_map.190), calls=%async_computation | async-start | bytes 786432 | tf_op jit(solution)/shard_map/all_to_all | solution.py:438
  64.9 3.7 %collective-permute-start.5 = (bf16[4,24,2304]{2,1,0:T(8,128)(2,1)S(1)}, bf16[4,24,2304]{2,1,0:T(8,128)(2,1)S(1)}, u32[]{:S(2)}, u32[]{:S(2)}) collective-permute-start(bf16[4,24,2304]{2,1,0:T(8,128)(2,1)S(1)} %shard_map.192), channel_id=1, source_target_pairs={{0,1},{1,0},{2,3},{3,2},{4,5},{5,4},{6,7},{7,6},{8,9},{9,8},{10,11... | collective-permute-start | bytes 1327112 | tf_op jit(solution)/shard_map/ppermute | solution.py:456
  69.9 14.7 %collective-permute-start.6 = (bf16[24,2304]{1,0:T(8,128)(2,1)S(1)}, bf16[24,2304]{1,0:T(8,128)(2,1)S(1)}, u32[]{:S(2)}, u32[]{:S(2)}) collective-permute-start(bf16[24,2304]{1,0:T(8,128)(2,1)S(1)} %get-tuple-element.41), channel_id=1, source_target_pairs={{0,8},{8,16},{16,24},{24,0},{1,9},{9,17},{17,25},{25,1},{2,10},{10... | collective-permute-start | bytes 331784 | tf_op jit(solution)/shard_map/ppermute | solution.py:33
  72.6 17.8 %collective-permute-start.8 = (bf16[24,2304]{1,0:T(8,128)(2,1)S(1)}, bf16[24,2304]{1,0:T(8,128)(2,1)S(1)}, u32[]{:S(2)}, u32[]{:S(2)}) collective-permute-start(bf16[24,2304]{1,0:T(8,128)(2,1)S(1)} %get-tuple-element.42), channel_id=1, source_target_pairs={{0,24},{8,0},{16,8},{24,16},{1,25},{9,1},{17,9},{25,17},{2,26},{10... | collective-permute-start | bytes 331784 | tf_op jit(solution)/shard_map/ppermute | solution.py:33
  84.6 12.2 %collective-permute-start.7 = (bf16[24,2304]{1,0:T(8,128)(2,1)S(1)}, bf16[24,2304]{1,0:T(8,128)(2,1)S(1)}, u32[]{:S(2)}, u32[]{:S(2)}) collective-permute-start(bf16[24,2304]{1,0:T(8,128)(2,1)S(1)} %shard_map.194), channel_id=1, source_target_pairs={{0,8},{8,16},{16,24},{24,0},{1,9},{9,17},{17,25},{25,1},{2,10},{10... | collective-permute-start | bytes 331784 | tf_op jit(solution)/shard_map/ppermute | solution.py:33
  129.9 38.6 %copy-start.1 = (bf16[1,128,768]{2,1,0:T(8,128)(2,1)S(1)}, bf16[1,128,768]{2,1,0:T(8,128)(2,1)}, u32[]{:S(2)}) copy-start(bf16[1,128,768]{2,1,0:T(8,128)(2,1)} %ng.1) | copy-start | bytes 589828
  129.9 38.6 %copy-start.2 = (bf16[1,128,768]{2,1,0:T(8,128)(2,1)S(1)}, bf16[1,128,768]{2,1,0:T(8,128)(2,1)}, u32[]{:S(2)}) copy-start(bf16[1,128,768]{2,1,0:T(8,128)(2,1)} %nu.1) | copy-start | bytes 589828
  129.9 38.6 %copy-start.3 = (bf16[1,768,128]{2,1,0:T(8,128)(2,1)S(1)}, bf16[1,768,128]{2,1,0:T(8,128)(2,1)}, u32[]{:S(2)}) copy-start(bf16[1,768,128]{2,1,0:T(8,128)(2,1)} %nd.1) | copy-start | bytes 589828
  130.5 37.9 %collective-permute-start.13 = (bf16[128,2304]{1,0:T(8,128)(2,1)S(1)}, bf16[128,2304]{1,0:T(8,128)(2,1)S(1)}, u32[]{:S(2)}, u32[]{:S(2)}) collective-permute-start(bf16[128,2304]{1,0:T(8,128)(2,1)S(1)} %get-tuple-element.50.rest_0_), channel_id=1, source_target_pairs={{0,4},{1,29},{2,6},{3,31},{4,8},{5,1},{6,10},{7,3},{8,12},{9,5},{1... | collective-permute-start | bytes 1769480 | tf_op jit(solution)/shard_map/ppermute | solution.py:43
  132.4 36.0 %collective-permute-start.11 = (bf16[128,2304]{1,0:T(8,128)(2,1)S(1)}, bf16[128,2304]{1,0:T(8,128)(2,1)S(1)}, u32[]{:S(2)}, u32[]{:S(2)}) collective-permute-start(bf16[128,2304]{1,0:T(8,128)(2,1)S(1)} %get-tuple-element.48), channel_id=1, source_target_pairs={{0,2},{1,3},{2,4},{3,5},{4,6},{5,7},{6,8},{7,9},{8,10},{9,11},{10,... | collective-permute-start | bytes 1769480 | tf_op jit(solution)/shard_map/ppermute | solution.py:43
  135.0 33.4 %collective-permute-start.12 = (bf16[128,2304]{1,0:T(8,128)(2,1)S(1)}, bf16[128,2304]{1,0:T(8,128)(2,1)S(1)}, u32[]{:S(2)}, u32[]{:S(2)}) collective-permute-start(bf16[128,2304]{1,0:T(8,128)(2,1)S(1)} %get-tuple-element.49), channel_id=1, source_target_pairs={{0,30},{1,31},{2,0},{3,1},{4,2},{5,3},{6,4},{7,5},{8,6},{9,7},{10,... | collective-permute-start | bytes 1769480 | tf_op jit(solution)/shard_map/ppermute | solution.py:43
  153.1 17.1 %collective-permute-start.9 = (bf16[128,256]{1,0:T(8,128)(2,1)S(1)}, bf16[128,256]{1,0:T(8,128)(2,1)S(1)}, u32[]{:S(2)}, u32[]{:S(2)}) collective-permute-start(bf16[128,256]{1,0:T(8,128)(2,1)S(1)} %get-tuple-element.45), channel_id=1, source_target_pairs={{412,0},{5,1},{414,2},{415,3},{0,4},{1,5},{2,6},{3,7},{28,8},{133,... | collective-permute-start | bytes 196616 | tf_op jit(solution)/shard_map/ppermute | solution.py:68
  163.8 13.2 %collective-permute-start.10 = (bf16[128,256]{1,0:T(8,128)(2,1)S(1)}, bf16[128,256]{1,0:T(8,128)(2,1)S(1)}, u32[]{:S(2)}, u32[]{:S(2)}) collective-permute-start(bf16[128,256]{1,0:T(8,128)(2,1)S(1)} %get-tuple-element.46), channel_id=1, source_target_pairs={{5,0},{412,1},{415,2},{414,3},{1,4},{0,5},{3,6},{2,7},{133,8},{28,... | collective-permute-start | bytes 196616 | tf_op jit(solution)/shard_map/ppermute | solution.py:68
